TPU v7x, 256 devices: a whole 4x4x8 slice. The times are simulated.
256 devices in a mesh: dp: 8 (over y_lo, x), space: 32 (over y_hi, z, core).
Axes of the slice: x: 4, y: 4 (y_hi: 2, y_lo: 2; y = y_hi * 2 + y_lo), z: 8, core: 2. Of those that a mesh axis runs over, the one named last changes fastest.
Arguments:
- cells: bfloat16 [8, 32768, 256], P('dp', 'space'), may hold values from -6 to 6
- cotangent: bfloat16 [8, 32768, 256], P('dp', 'space'), may hold values from -6 to 6
- cell_count: int32 [8, 32], P('dp', 'space'), may hold values from 1 to 1024, 24576 in all within a row
- first_norm_gain: float32 [256], replicated, may hold values from 0.5 to 1.5
- first_norm_bias: float32 [256], replicated, may hold values from -1.2 to 1.2
- w_fx: bfloat16 [256, 256], replicated, may hold values from -0.375 to 0.375
- w_x: bfloat16 [256, 256], replicated, may hold values from -0.375 to 0.375
- w_slice: bfloat16 [32, 64], replicated, may hold values from -1 to 1
- temper: float32 [8], replicated, may hold values from 0.25 to 1
- query_weight: float32 [32, 32], replicated, may hold values from -1 to 1
- key_weight: float32 [32, 32], replicated, may hold values from -1 to 1
- value_weight: float32 [32, 32], replicated, may hold values from -1 to 1
- w_out: bfloat16 [256, 256], replicated, may hold values from -0.375 to 0.375
- second_norm_gain: float32 [256], replicated, may hold values from 0.5 to 1.5
- second_norm_bias: float32 [256], replicated, may hold values from -1.2 to 1.2
- w_up: bfloat16 [256, 256], replicated, may hold values from -0.375 to 0.375
- w_down: bfloat16 [256, 256], replicated, may hold values from -0.375 to 0.375
Outputs:
- layer_out: bfloat16 [8, 32768, 256], P('dp', 'space')
- grad_cells: bfloat16 [8, 32768, 256], P('dp', 'space')
- grad_ln1_gain: float32 [256], replicated
- grad_ln1_bias: float32 [256], replicated
- grad_fx: float32 [256, 256], replicated
- grad_x: float32 [256, 256], replicated
- grad_slice: float32 [32, 64], replicated
- grad_temper: float32 [8], replicated
- grad_q: float32 [32, 32], replicated
- grad_k: float32 [32, 32], replicated
- grad_v: float32 [32, 32], replicated
- grad_out: float32 [256, 256], replicated
- grad_ln2_gain: float32 [256], replicated
- grad_ln2_bias: float32 [256], replicated
- grad_up: float32 [256, 256], replicated
- grad_down: float32 [256, 256], replicated
Inputs may be any that keep to these rules, and one draw needn't show every extreme that they name: The first cell_count[s, j] of shard j's 1024 slots are live cells, the rest are padding; every scenario has a full shard.
All inputs are finite; a program needn't handle non-finite values.
Results may differ from a plain program's by a relative error of at most 0.034.
The roundings to bfloat16 on the way count: a program that leaves them out, or rounds other values in their place, can miss the bound.
Values sent between devices are 32-bit elements; how exact they have to be, the bound alone decides.
No kernel may reach another device: no remote copies, remote signals or barrier semaphores. Data moves between devices by JAX's collectives and lax.ppermute only.
A program may use at most 64 MiB of HBM per device.

v0:
```python
import math

import jax
import jax.numpy as jnp
from jax import lax
from jax.sharding import PartitionSpec as P

CELL_WIDTH = 256
ATTENTION_HEADS = 8
SLICES = 64
HEAD_SIZE = 32


EPS = 1e-05


def norm_forward_pass(input_rows, norm_gain, norm_shift):
    input_rows = input_rows.astype(jnp.float32)
    centered_input = input_rows - jnp.mean(input_rows, axis=-1, keepdims=True)
    inverse_deviation = lax.rsqrt(
        jnp.mean(centered_input * centered_input, axis=-1, keepdims=True) + EPS
    )
    normalized_input = centered_input * inverse_deviation
    return (
        normalized_input,
        inverse_deviation,
        (normalized_input * norm_gain + norm_shift).astype(jnp.bfloat16),
    )


def norm_backward_pass(norm_input_gradient, normalized_input, inverse_deviation, norm_gain):
    normalized_gradient = norm_input_gradient * norm_gain
    return inverse_deviation * (
        normalized_gradient
        - jnp.mean(normalized_gradient, axis=-1, keepdims=True)
        - normalized_input
        * jnp.mean(normalized_gradient * normalized_input, axis=-1, keepdims=True)
    )


def front(input_rows, count, first_norm_gain, first_norm_bias, w_fx, w_x, w_slice, temper):
    token_count = input_rows.shape[0]
    first_normalized_input, first_inverse_deviation, first_normed_rows = norm_forward_pass(
        input_rows, first_norm_gain, first_norm_bias
    )
    cell_features = jnp.dot(first_normed_rows, w_fx, preferred_element_type=jnp.float32).astype(
        jnp.bfloat16
    )
    hidden_activations = jnp.dot(first_normed_rows, w_x, preferred_element_type=jnp.float32).astype(
        jnp.bfloat16
    )
    slice_logits = jnp.dot(
        hidden_activations.reshape(token_count * ATTENTION_HEADS, HEAD_SIZE),
        w_slice,
        preferred_element_type=jnp.float32,
    )
    slice_logits = (
        slice_logits.reshape(token_count, ATTENTION_HEADS, SLICES) / temper[None, :, None]
    )
    live = (jnp.arange(token_count, dtype=jnp.int32) < count).astype(jnp.float32)
    attention_probabilities = jax.nn.softmax(slice_logits, axis=-1) * live[:, None, None]
    return (
        first_normalized_input,
        first_inverse_deviation,
        first_normed_rows,
        cell_features,
        hidden_activations,
        slice_logits,
        attention_probabilities,
    )


def mix_tokens(slice_tokens, query_weight, key_weight, value_weight):
    maximum_logit = lax.Precision.HIGHEST
    query_rows = jnp.einsum("zcr,rt->zct", slice_tokens, query_weight, precision=maximum_logit)
    key_rows = jnp.einsum("zcr,rt->zct", slice_tokens, key_weight, precision=maximum_logit)
    value_rows = jnp.einsum("zcr,rt->zct", slice_tokens, value_weight, precision=maximum_logit)
    attention_scores = jnp.einsum(
        "pfq,plq->pfl", query_rows, key_rows, precision=maximum_logit
    ) * HEAD_SIZE ** (-0.5)
    return jnp.einsum(
        "paz,pzy->pay",
        jax.nn.softmax(attention_scores, axis=-1),
        value_rows,
        precision=maximum_logit,
    )


def middle(
    input_rows,
    slice_weights,
    mixed_token_batch,
    incoming_gradients,
    w_out,
    second_norm_gain,
    second_norm_bias,
    w_up,
    w_down,
):
    token_count = input_rows.shape[0]
    spread_tokens = (
        jnp.einsum(
            "wqj,qja->wqa", slice_weights, mixed_token_batch, preferred_element_type=jnp.float32
        )
        .reshape(token_count, CELL_WIDTH)
        .astype(jnp.bfloat16)
    )
    residual_rows = (
        input_rows.astype(jnp.float32)
        + jnp.dot(spread_tokens, w_out, preferred_element_type=jnp.float32)
    ).astype(jnp.bfloat16)
    second_normalized_input, second_inverse_deviation, second_normed_rows = norm_forward_pass(
        residual_rows, second_norm_gain, second_norm_bias
    )
    up = jnp.dot(second_normed_rows, w_up, preferred_element_type=jnp.float32)
    act, gelu_back = jax.vjp(jax.nn.gelu, up)
    act_b = act.astype(jnp.bfloat16)
    layer = (
        residual_rows.astype(jnp.float32)
        + jnp.dot(act_b, w_down, preferred_element_type=jnp.float32)
    ).astype(jnp.bfloat16)
    grad_down = jnp.dot(act_b.T, incoming_gradients, preferred_element_type=jnp.float32)
    g_act = jnp.dot(incoming_gradients, w_down.T, preferred_element_type=jnp.float32)
    g_up = gelu_back(g_act)[0].astype(jnp.bfloat16)
    grad_up = jnp.dot(second_normed_rows.T, g_up, preferred_element_type=jnp.float32)
    second_norm_gradient = jnp.dot(g_up, w_up.T, preferred_element_type=jnp.float32)
    second_gain_gradient = jnp.sum(second_norm_gradient * second_normalized_input, axis=0)
    grad_bias2 = jnp.sum(second_norm_gradient, axis=0)
    residual_gradient = incoming_gradients.astype(jnp.float32) + norm_backward_pass(
        second_norm_gradient, second_normalized_input, second_inverse_deviation, second_norm_gain
    )
    g_resid_b = residual_gradient.astype(jnp.bfloat16)
    grad_out = jnp.dot(spread_tokens.T, g_resid_b, preferred_element_type=jnp.float32)
    spread_gradient = jnp.dot(g_resid_b, w_out.T, preferred_element_type=jnp.float32).astype(
        jnp.bfloat16
    )
    token_partial = jnp.einsum(
        "fup,fuk->upk",
        slice_weights,
        spread_gradient.reshape(token_count, ATTENTION_HEADS, HEAD_SIZE),
        preferred_element_type=jnp.float32,
    )
    return (
        layer,
        residual_gradient,
        spread_gradient,
        token_partial,
        (grad_out, second_gain_gradient, grad_bias2, grad_up, grad_down),
    )


def rear(
    next_value,
    slice_weights,
    residual_gradient,
    spread_gradient,
    mixed_token_batch,
    numerator_gradient,
    g_denom,
    w_fx,
    w_x,
    w_slice,
    temper,
    first_norm_gain,
):
    (
        first_normalized_input,
        first_inverse_deviation,
        first_normed_rows,
        cell_features,
        hidden_activations,
        slice_logits,
        attention_probabilities,
    ) = next_value
    token_count = attention_probabilities.shape[0]
    slice_weight_gradient = jnp.einsum(
        "zbe,ble->zbl",
        spread_gradient.reshape(token_count, ATTENTION_HEADS, HEAD_SIZE),
        mixed_token_batch,
        preferred_element_type=jnp.float32,
    )
    slice_weight_gradient = slice_weight_gradient + jnp.einsum(
        "zbe,ble->zbl",
        cell_features.reshape(token_count, ATTENTION_HEADS, HEAD_SIZE),
        numerator_gradient,
        preferred_element_type=jnp.float32,
    )
    slice_weight_gradient = slice_weight_gradient + g_denom[None]
    g_logits = attention_probabilities * (
        slice_weight_gradient
        - jnp.sum(slice_weight_gradient * attention_probabilities, axis=-1, keepdims=True)
    )
    grad_temper = -jnp.sum(g_logits * slice_logits, axis=(0, 2)) / temper
    g_scaled = (
        (g_logits / temper[None, :, None])
        .astype(jnp.bfloat16)
        .reshape(token_count * ATTENTION_HEADS, SLICES)
    )
    g_mids = (
        jnp.dot(g_scaled, w_slice.T, preferred_element_type=jnp.float32)
        .reshape(token_count, CELL_WIDTH)
        .astype(jnp.bfloat16)
    )
    grad_slice = jnp.dot(
        hidden_activations.reshape(token_count * ATTENTION_HEADS, HEAD_SIZE).T,
        g_scaled,
        preferred_element_type=jnp.float32,
    )
    features_gradient = (
        jnp.einsum(
            "wqj,qja->wqa", slice_weights, numerator_gradient, preferred_element_type=jnp.float32
        )
        .reshape(token_count, CELL_WIDTH)
        .astype(jnp.bfloat16)
    )
    grad_fx = jnp.dot(first_normed_rows.T, features_gradient, preferred_element_type=jnp.float32)
    grad_x = jnp.dot(first_normed_rows.T, g_mids, preferred_element_type=jnp.float32)
    first_norm_gradient = jnp.dot(
        features_gradient, w_fx.T, preferred_element_type=jnp.float32
    ) + jnp.dot(g_mids, w_x.T, preferred_element_type=jnp.float32)
    first_gain_gradient = jnp.sum(first_norm_gradient * first_normalized_input, axis=0)
    grad_bias1 = jnp.sum(first_norm_gradient, axis=0)
    row_gradient = (
        residual_gradient
        + norm_backward_pass(
            first_norm_gradient, first_normalized_input, first_inverse_deviation, first_norm_gain
        )
    ).astype(jnp.bfloat16)
    return (
        row_gradient,
        (first_gain_gradient, grad_bias1, grad_fx, grad_x, grad_slice, grad_temper),
    )


def body(
    cells,
    cotangent,
    cell_count,
    first_norm_gain,
    first_norm_bias,
    w_fx,
    w_x,
    w_slice,
    temper,
    query_weight,
    key_weight,
    value_weight,
    w_out,
    second_norm_gain,
    second_norm_bias,
    w_up,
    w_down,
):
    input_rows = cells[0]
    incoming_gradients = cotangent[0]
    count = cell_count[0, 0]
    shards = lax.axis_size("space")
    scale = 1.0 / math.sqrt(input_rows.shape[0] * shards * lax.axis_size("dp"))
    next_value = front(
        input_rows, count, first_norm_gain, first_norm_bias, w_fx, w_x, w_slice, temper
    )
    attention_probabilities = next_value[6]
    slice_weights = attention_probabilities.astype(jnp.bfloat16)
    slice_numerator = jnp.einsum(
        "fup,fuk->upk",
        slice_weights,
        next_value[3].reshape(input_rows.shape[0], ATTENTION_HEADS, HEAD_SIZE),
        preferred_element_type=jnp.float32,
    )
    denom = jnp.sum(attention_probabilities, axis=0)
    slice_numerator, denom = lax.psum((slice_numerator, denom), "space")
    lifted = denom[:, :, None] + EPS
    slice_tokens = slice_numerator / lifted
    mixed, mix_back = jax.vjp(mix_tokens, slice_tokens, query_weight, key_weight, value_weight)
    mixed_token_batch = mixed.astype(jnp.bfloat16)
    layer, residual_gradient, spread_gradient, token_partial, late = middle(
        input_rows,
        slice_weights,
        mixed_token_batch,
        incoming_gradients,
        w_out,
        second_norm_gain,
        second_norm_bias,
        w_up,
        w_down,
    )
    late_scaled = [piece * scale for piece in late]
    tok_grad = lax.psum(token_partial, "space")
    g_tokens, grad_q, grad_k, grad_v = mix_back(tok_grad)
    numerator_gradient = (g_tokens / lifted).astype(jnp.bfloat16)
    g_denom = -jnp.sum(g_tokens * slice_tokens, axis=-1) / lifted[:, :, 0]
    row_gradient, early = rear(
        next_value,
        slice_weights,
        residual_gradient,
        spread_gradient,
        mixed_token_batch,
        numerator_gradient,
        g_denom,
        w_fx,
        w_x,
        w_slice,
        temper,
        first_norm_gain,
    )
    first = (lax.axis_index("space") == 0).astype(jnp.float32)
    first_gain_gradient, grad_bias1, grad_fx, grad_x, grad_slice, grad_temper = early
    early_pieces = [
        first_gain_gradient,
        grad_bias1,
        grad_fx,
        grad_x,
        grad_slice,
        grad_temper,
        grad_q * first,
        grad_k * first,
        grad_v * first,
    ]
    early_pieces = [piece * scale for piece in early_pieces]
    pieces = early_pieces + late_scaled
    summed = list(
        lax.psum(
            (
                pieces[0],
                pieces[1],
                pieces[2],
                pieces[3],
                pieces[4],
                pieces[5],
                pieces[6],
                pieces[7],
                pieces[8],
                pieces[9],
                pieces[10],
                pieces[11],
                pieces[12],
                pieces[13],
            ),
            ("dp", "space"),
        )
    )
    return (
        layer[None],
        row_gradient[None],
        summed[0],
        summed[1],
        summed[2],
        summed[3],
        summed[4],
        summed[5],
        summed[6],
        summed[7],
        summed[8],
        summed[9],
        summed[10],
        summed[11],
        summed[12],
        summed[13],
    )


def solution(mesh):
    placed = (
        P("dp", "space", None),
        P("dp", "space", None),
        P("dp", "space"),
        P(),
        P(),
        P(),
        P(),
        P(),
        P(),
        P(),
        P(),
        P(),
        P(),
        P(),
        P(),
        P(),
        P(),
    )
    return jax.shard_map(
        body,
        mesh=mesh,
        in_specs=placed,
        out_specs=(
            P("dp", "space", None),
            P("dp", "space", None),
            P(),
            P(),
            P(),
            P(),
            P(),
            P(),
            P(),
            P(),
            P(),
            P(),
            P(),
            P(),
            P(),
            P(),
        ),
        check_vma=False,
    )
```

profile of v0, /device:TPU:1, one launch (start us, length us, event | category | flops | bytes accessed | tf_op | source)
XLA Modules:
  0.0 831.4 jit_solution(154137940925124775)
XLA Ops:
  7.3 1.3 copy.49
  9.9 3.0 fusion.98
  15.0 1.1 fusion.101
  16.1 69.2 %psum.120 = f32[8,64]{1,0:T(8,128)S(1)} all-reduce(f32[8,64]{1,0:T(8,128)S(1)} %get-tuple-element.69), channel_id=1, replica_groups=mesh['dp'=8,'space'=32] {'space'}, use_global_device_ids=true, to_apply=%region_6.0 | all-reduce | flops 512 | bytes 4096 | tf_op jit(solution)/shard_map/psum | solution.py:271
  85.5 1.0 copy.55
  86.5 1.9 reshape.185
  88.4 174.3 %all-reduce.6.cloned.1.call-done = f32[8,64,32]{1,2,0:T(8,128)} async-done(((f32[8,64,32]{1,2,0:T(8,128)}), f32[8,64,32]{1,2,0:T(8,128)}) %all-reduce.6.cloned.1.call-update) | async-done | bytes 65552 | tf_op jit(solution)/shard_map/psum | solution.py:271
  262.7 1.2 fusion.79
  263.9 1.3 fusion.82
  265.9 1.2 fusion.76
  269.3 0.9 fusion.54
  270.4 1.1 convolution_multiply_fusion.2
  271.4 1.9 fusion.100
  273.9 1.6 copy.56
  275.5 0.9 fusion.37
  276.4 1.6 fusion.36
  278.3 1.1 fusion.102
  279.4 2.8 fusion.103
  282.2 1.0 convolution_multiply_fusion.3
  283.3 1.2 convolution_multiply_fusion.1
  285.3 1.3 broadcast_multiply_fusion.6
  286.6 1.0 copy.66
  287.6 238.3 %all-reduce.8.cloned.1.call-done = f32[8,64,32]{1,2,0:T(8,128)} async-done(((f32[8,64,32]{1,2,0:T(8,128)}), f32[8,64,32]{1,2,0:T(8,128)}) %all-reduce.8.cloned.1.call-update) | async-done | bytes 65552 | tf_op jit(solution)/shard_map/psum | solution.py:288
  525.9 1.6 multiply_reduce_fusion.3
  527.6 1.4 fusion.87
  529.0 1.5 fusion.88
  532.6 1.2 convolution_convert_fusion.2
  534.4 1.0 copy-done.6
  536.1 2.3 multiply_reduce_fusion
  538.3 2.6 copy.60
  541.0 1.6 convolution_convert_fusion
  542.6 2.7 copy.61
  545.3 3.9 convert_element_type.130
  549.2 2.4 convolution_multiply_fusion.4
  551.6 1.3 fusion.104
  552.9 1.1 convolution_multiply_fusion.5
  554.0 2.2 fusion.46
  557.5 1.9 fusion.61
  559.4 1.2 fusion.30
  560.9 1.0 copy.67
  562.2 2.3 fusion.22
  564.6 79.0 %all-reduce = (f32[256]{0:T(256)}, f32[256]{0:T(256)}, f32[32,64]{1,0:T(8,128)}, f32[8]{0:T(128)}, f32[32,32]{1,0:T(8,128)}, /*index=5*/f32[32,32]{1,0:T(8,128)}, f32[32,32]{1,0:T(8,128)}, f32[256]{0:T(256)}, f32[256]{0:T(256)}) all-reduce(f32[256]{0:T(256)S(1)} %copy-done.62, ...), channel_id=1, replica_groups=mesh['dp'=8,'space'=32] {'dp','space'}, use_global_device_ids=true, to_apply=%region_20.0 | all-reduce | flops 6152 | bytes 49216 | tf_op jit(solution)/shard_map/psum | solution.py:322
  643.6 173.8 %all-reduce.10.cloned.1.call-done = (f32[256,256]{1,0:T(8,128)}, f32[256,256]{1,0:T(8,128)}, f32[256,256]{1,0:T(8,128)}, f32[256,256]{1,0:T(8,128)}, f32[256,256]{1,0:T(8,128)}) async-done(((f32[256,256]{1,0:T(8,128)}, f32[256,256]{1,0:T(8,128)}, f32[256,256]{1,0:T(8,128)}, f32[256,256]{1,0:T(8,128)}, f32[256,256]{1,0:T(8,128)}), (f32[256,256]{1,0:T(8,128)}, f32[256,256]{1,0:T(8,128)}, ...) | async-done | bytes 1310736 | tf_op jit(solution)/shard_map/psum | solution.py:322
  817.4 1.7 copy.89
  819.1 1.7 copy.90
  820.8 1.7 copy.91
  822.5 1.7 copy.92
  824.1 0.7 copy.93
  (199 shorter events, 12.4 us)
Async XLA Ops:
  7.2 6.5 copy-start
  7.3 255.4 %all-reduce.6.cloned.1.call-start = ((), (), s32[]{:S(2)}) async-start(), calls=%async_computation | async-start | bytes 262144 | tf_op jit(solution)/shard_map/psum | solution.py:271
  8.6 259.6 %copy-start.1 = (bf16[1,1024,256]{1,2,0:T(8,128)(2,1)}, bf16[1,1024,256]{1,2,0:T(8,128)(2,1)S(1)}, u32[]{:S(2)}) copy-start(bf16[1,1024,256]{1,2,0:T(8,128)(2,1)S(1)} %copy.49) | copy-start | bytes 1572868
  8.9 4.8 copy-start.44
  9.9 3.0 copy-start.14
  14.5 71.0 %copy-start.17 = (bf16[1,1024,256]{2,1,0:T(8,128)(2,1)S(1)}, bf16[1,1024,256]{2,1,0:T(8,128)(2,1)}, u32[]{:S(2)}) copy-start(bf16[1,1024,256]{2,1,0:T(8,128)(2,1)} %param.18) | copy-start | bytes 1572868
  16.1 509.9 %all-reduce.8.cloned.1.call-start = ((), (), s32[]{:S(2)}) async-start(), calls=%async_computation.1 | async-start | bytes 262144 | tf_op jit(solution)/shard_map/psum | solution.py:288
  85.3 3.1 copy-start.42
  85.5 177.1 %copy-start.53 = (f32[32,32]{1,0:T(8,128)S(1)}, f32[32,32]{1,0:T(8,128)}, u32[]{:S(2)}) copy-start(f32[32,32]{1,0:T(8,128)} %param.27) | copy-start | bytes 12292
  85.5 178.4 %copy-start.55 = (f32[32,32]{1,0:T(8,128)S(1)}, f32[32,32]{1,0:T(8,128)}, u32[]{:S(2)}) copy-start(f32[32,32]{1,0:T(8,128)} %param.26) | copy-start | bytes 12292
  86.5 179.4 %copy-start.51 = (f32[32,32]{1,0:T(8,128)S(1)}, f32[32,32]{1,0:T(8,128)}, u32[]{:S(2)}) copy-start(f32[32,32]{1,0:T(8,128)} %param.28) | copy-start | bytes 12292
  263.9 3.3 copy-start.36
  263.9 4.3 copy-start.20
  265.9 7.4 copy-start.48
  268.6 6.9 copy-start.7
  271.4 4.0 copy-start.41
  271.4 4.1 copy-start.60
  275.5 2.5 copy-start.21
  278.3 3.9 copy-start.10
  279.4 3.9 copy-start.18
  279.4 3.9 copy-start.77
  284.5 243.1 %copy-start.49 = (f32[8,64]{1,0:T(8,128)S(1)}, f32[8,64]{1,0:T(8,128)}, u32[]{:S(2)}) copy-start(f32[8,64]{1,0:T(8,128)} %copy-done.48) | copy-start | bytes 6148
  285.1 532.3 %all-reduce.10.cloned.1.call-start = ((), (), s32[]{:S(2)}) async-start(), calls=%async_computation.2 | async-start | bytes 2621440 | tf_op jit(solution)/shard_map/psum | solution.py:322
  287.6 242.9 %copy-start.50 = (f32[8,64]{1,0:T(8,128)S(1)}, f32[8,64]{1,0:T(8,128)}, u32[]{:S(2)}) copy-start(f32[8,64]{1,0:T(8,128)} %copy-done.48) | copy-start | bytes 6148
  287.6 244.2 %copy-start.52 = (f32[32,32]{1,0:T(8,128)S(1)}, f32[32,32]{1,0:T(8,128)}, u32[]{:S(2)}) copy-start(f32[32,32]{1,0:T(8,128)} %param.28) | copy-start | bytes 12292
  525.9 4.6 copy-start.30
  527.6 4.5 copy-start.54
  527.6 4.7 copy-start.33
  527.6 4.7 copy-start.56
  529.0 4.8 copy-start.37
  530.5 3.3 copy-start.27
  530.6 3.2 copy-start.43
  530.6 3.2 copy-start.4
  530.6 3.2 copy-start.12
  538.3 2.7 copy-start.58
  542.6 6.5 copy-start.45
  542.6 6.5 copy-start.66
  542.6 6.5 copy-start.71
  545.3 6.3 copy-start.39
  549.2 2.4 copy-start.13
  549.2 3.8 copy-start.2
  549.2 3.7 copy-start.19
  554.0 3.4 copy-start.3
  557.4 3.2 copy-start.28
  559.3 2.6 copy-start.32
  562.2 2.4 copy-start.61
  562.2 2.4 copy-start.62
  817.4 6.7 copy-start.22
  (33 other events, 50.5 us)
Sparse Core Ops, SparseCore 0:
  16.2 246.4 all-reduce.5
  285.2 240.6 all-reduce.7
  559.5 257.8 all-reduce.9
where the time goes:
time: 832 us; the launch traced here: 831 us
  waiting for transfers between devices  586 us (70%)
  blocking collectives  148 us (18%)
  matrix products  39.3 us (5%)
  local copies, waits for them, and re-layouts  28.1 us (3%)
  between operations  15.5 us (2%)
  other arithmetic  13.5 us (2%)
    psum x1, waiting for transfers between devices, body(): tok_grad = lax.psum(token_partial, 'space')  238 us
    psum x1, waiting for transfers between devices, body(): slice_numerator, denom = lax.psum((slice_numerator, denom), 'space')  174 us
    psum x1, waiting for transfers between devices, body(): lax.psum((pieces[0], pieces[1], pieces[2], pieces[3], pieces[4], pieces[5...  174 us
    psum x1, blocking collectives, body(): lax.psum((pieces[0], pieces[1], pieces[2], pieces[3], pieces[4], pieces[5...  79 us
    psum x1, blocking collectives, body(): slice_numerator, denom = lax.psum((slice_numerator, denom), 'space')  69.2 us
  transfers between devices with their start and end apart: 3, of which 3 were waited for; matrix products, arithmetic and copies ran while one was open for 1% of the time, Pallas kernels for 0%

commit v1 on v0

v1 whole, which is shorter than its diff:
```python
import math

import jax
import jax.numpy as jnp
from jax import lax
from jax.experimental import pallas as pl
from jax.experimental.pallas import tpu as pltpu
from jax.sharding import Mesh, PartitionSpec as P

WIDTH = 256
HEADS = 8
SLICES = 64
HEAD = 32
CELLS = 1024
PAIRS = HEADS // 2
EPS = 1e-05
CHUNK = 256
STEPS = CELLS // CHUNK
F32 = jnp.float32
BF16 = jnp.bfloat16
AXES = ("yl", "x", "yh", "z", "c")
PLANE = ("yl", "x", "yh")
SPACE = 32
Z_SCALE = 1.0 / math.sqrt(8 * 32768)
LATE, EARLY = 1536, 1280
LATE_HALF, EARLY_HALF = LATE // 2, EARLY // 2
LATE_PART, EARLY_PART = LATE_HALF // 16, EARLY_HALF // 16


def nn(a, b, precision=None):
    return lax.dot_general(
        a, b, (((1,), (0,)), ((), ())), precision=precision, preferred_element_type=F32
    )


def nt(a, b, precision=None):
    return lax.dot_general(
        a, b, (((1,), (1,)), ((), ())), precision=precision, preferred_element_type=F32
    )


def exact(f, a, b):
    return f(a, b, precision=lax.Precision.HIGHEST)


def turned(w):
    return w.astype(F32).T.astype(BF16)


def lane_half(rows):
    return lax.broadcasted_iota(jnp.int32, (rows, 128), 1) < SLICES


def diagonal_128():
    row = lax.broadcasted_iota(jnp.int32, (128, 128), 0) < SLICES
    lane = lax.broadcasted_iota(jnp.int32, (128, 128), 1) < SLICES
    return row == lane


def spread_pair(t):
    first = lane_half(HEAD)
    return jnp.concatenate([jnp.where(first, t, 0.0), jnp.where(first, 0.0, t)], axis=0)


def fold_pair(d):
    return jnp.where(lane_half(HEAD), d[:HEAD], d[HEAD:])


def slice_pair(w_slice):
    w = w_slice.astype(F32)
    return spread_pair(jnp.concatenate([w, w], axis=1))


def norm_stats(xt):
    mean = jnp.sum(xt, axis=0, keepdims=True) * (1.0 / WIDTH)
    centred = xt - mean
    inv = lax.rsqrt(jnp.sum(centred * centred, axis=0, keepdims=True) * (1.0 / WIDTH) + EPS)
    return mean, inv, centred * inv


def norm_back(g, xhat, inv, gain):
    ng = g * gain
    m1 = jnp.sum(ng, axis=0, keepdims=True) * (1.0 / WIDTH)
    m2 = jnp.sum(ng * xhat, axis=0, keepdims=True) * (1.0 / WIDTH)
    return inv * (ng - m1 - xhat * m2)


def lanes128(v):
    return v[:, :128] + v[:, 128:]


def live_row(count, step):
    lane = lax.broadcasted_iota(jnp.int32, (1, CHUNK), 1) + step * CHUNK
    return (lane < count).astype(F32)


def as_row(column128):
    return jnp.sum(column128.T, axis=0, keepdims=True)


def front_kernel(
    count_ref, temper_ref, cells_ref, gain_ref, bias_ref, wfx_ref, wx_ref, wsl_ref,
    pay_ref, xt_ref, feats_ref, mids_ref, weights_ref, stats_ref,
):
    count = count_ref[0]
    wfx_t = turned(wfx_ref[...])
    wx_t = turned(wx_ref[...])
    pair_t = slice_pair(wsl_ref[...]).T.astype(BF16)
    gain = gain_ref[...]
    bias = bias_ref[...]
    inv_t = [1.0 / jnp.full((1, CHUNK), temper_ref[h], F32) for h in range(HEADS)]
    ones = jnp.ones((16, CHUNK), BF16)
    pay_ref[...] = jnp.zeros_like(pay_ref)

    def step(i, carry):
        at = pl.ds(pl.multiple_of(i * CHUNK, CHUNK), CHUNK)
        xt = cells_ref[at, :].astype(F32).T
        xt_ref[:, at] = xt.astype(BF16)
        mean, inv, xhat = norm_stats(xt)
        n1 = (xhat * gain + bias).astype(BF16)
        feats = nn(wfx_t, n1).astype(BF16)
        mids = nn(wx_t, n1).astype(BF16)
        feats_ref[:, at] = feats
        mids_ref[:, at] = mids
        live = live_row(count, i)
        lses = []
        for p in range(PAIRS):
            rows = slice(64 * p, 64 * p + 64)
            logits = nn(pair_t, mids[rows])
            halves = []
            for k in range(2):
                l = logits[64 * k : 64 * k + 64] * inv_t[2 * p + k]
                m = jnp.max(l, axis=0, keepdims=True)
                e = jnp.exp(l - m)
                s = jnp.sum(e, axis=0, keepdims=True)
                halves.append((e * (live / s)).astype(BF16))
                lses.append(m + jnp.log(s))
            w = jnp.concatenate(halves, axis=0)
            weights_ref[128 * p : 128 * p + 128, at] = w
            d = nt(jnp.concatenate([feats[rows], ones], axis=0), w)
            part = jnp.concatenate([fold_pair(d[:64]), d[64:72]], axis=0)
            pay_ref[:, 128 * p : 128 * p + 128] += part
        stats_ref[:, at] = jnp.concatenate(
            [mean, inv] + lses + [jnp.zeros((6, CHUNK), F32)], axis=0
        )
        return carry

    lax.fori_loop(0, STEPS, step, 0)


def middle_kernel(
    core_ref, pay_ref, wq_ref, wk_ref, wv_ref, xt_ref, weights_ref, cot_ref, wout_ref, wup_ref,
    wdown_ref, gain_ref, bias_ref,
    layer_ref, gres_ref, gs_ref, tok_ref, keep_ref, send_ref, ln2_ref, mix_ref,
    late_ref, sums_ref,
):
    core = core_ref[0]
    lifted = pay_ref[HEAD : HEAD + 1, :] + EPS
    tok = pay_ref[:HEAD, :] / lifted
    qt = exact(nn, wq_ref[...].T, tok)
    kt = exact(nn, wk_ref[...].T, tok)
    vt = exact(nn, wv_ref[...].T, tok)
    mix_ref[0:32, :] = tok
    mix_ref[32:64, :] = qt
    mix_ref[64:96, :] = kt
    mix_ref[96:128, :] = vt
    diagonal = diagonal_128()
    blocks = []
    for p in range(PAIRS):
        lanes = slice(128 * p, 128 * p + 128)
        scores = exact(nn, kt[:, lanes].T, qt[:, lanes]) * (HEAD**-0.5)
        scores = jnp.where(diagonal, scores, -1e30)
        e = jnp.exp(scores - jnp.max(scores, axis=0, keepdims=True))
        e = jnp.where(diagonal, e, 0.0)
        attn = e / jnp.sum(e, axis=0, keepdims=True)
        mixed = exact(nn, vt[:, lanes], attn)
        mix_ref[128:256, lanes] = attn
        mixed_b = mixed.astype(BF16).astype(F32)
        mix_ref[256:288, lanes] = mixed_b
        blocks.append(spread_pair(mixed_b).astype(BF16))

    wout = wout_ref[...]
    wup = wup_ref[...]
    wdown = wdown_ref[...]
    wout_t, wup_t, wdown_t = turned(wout), turned(wup), turned(wdown)
    gain = gain_ref[...]
    bias = bias_ref[...]
    late_ref[...] = jnp.zeros_like(late_ref)
    sums_ref[...] = jnp.zeros_like(sums_ref)
    tok_ref[...] = jnp.zeros_like(tok_ref)
    c0 = math.sqrt(2.0 / math.pi)

    def step(i, carry):
        at = pl.ds(pl.multiple_of(i * CHUNK, CHUNK), CHUNK)
        spread = jnp.concatenate(
            [nn(blocks[p], weights_ref[128 * p : 128 * p + 128, at]) for p in range(PAIRS)], axis=0
        ).astype(BF16)
        resid = (xt_ref[:, at].astype(F32) + nn(wout_t, spread)).astype(BF16)
        resid_f = resid.astype(F32)
        _, inv, xhat = norm_stats(resid_f)
        n2 = (xhat * gain + bias).astype(BF16)
        up = nn(wup_t, n2)
        sq = up * up
        t = jnp.tanh(c0 * up * (1.0 + 0.044715 * sq))
        half = 0.5 * (1.0 + t)
        act = (up * half).astype(BF16)
        slope = half + 0.5 * up * (1.0 - t * t) * (c0 * (1.0 + 3.0 * 0.044715 * sq))
        layer = (resid_f + nn(wdown_t, act)).astype(BF16)
        layer_ref[at, :] = layer.astype(F32).T.astype(BF16)
        gt_f = cot_ref[at, :].astype(F32).T
        gt = gt_f.astype(BF16)
        late_ref[512:768, :] += nt(act, gt)
        g_up = (slope * nn(wdown, gt)).astype(BF16)
        late_ref[256:512, :] += nt(n2, g_up)
        g_n2 = nn(wup, g_up)
        sums_ref[0:256, :] += lanes128(g_n2 * xhat)
        sums_ref[256:512, :] += lanes128(g_n2)
        gres = gt_f + norm_back(g_n2, xhat, inv, gain)
        gres_ref[:, at] = gres
        gres_b = gres.astype(BF16)
        late_ref[0:256, :] += nt(spread, gres_b)
        gs = nn(wout, gres_b).astype(BF16)
        gs_ref[:, at] = gs
        for p in range(PAIRS):
            d = nt(gs[64 * p : 64 * p + 64], weights_ref[128 * p : 128 * p + 128, at])
            tok_ref[:, 128 * p : 128 * p + 128] += fold_pair(d)
        return carry

    lax.fori_loop(0, STEPS, step, 0)
    left = late_ref[:, :128] * Z_SCALE
    right = late_ref[:, 128:] * Z_SCALE
    keep_ref[...] = jnp.where(core == 0, left, right)
    send_ref[...] = jnp.where(core == 0, right, left)
    ln2_ref[...] = jnp.concatenate(
        [as_row(sums_ref[0:256, :]), as_row(sums_ref[256:512, :]), jnp.zeros((6, WIDTH), F32)],
        axis=0,
    )


def rear_kernel(
    core_ref, count_ref, temper_ref, pay_ref, grad_ref, mix_ref, wq_ref, wk_ref, wv_ref, xt_ref,
    feats_ref, mids_ref, stats_ref, gs_ref, gres_ref, gain_ref, bias_ref, wfx_ref, wx_ref,
    wsl_ref, ln2_ref,
    cells_out_ref, keep_ref, send_ref,
    early_ref, sums_ref, small_ref, temp_ref,
):
    core = core_ref[0]
    count = count_ref[0]
    lifted = pay_ref[HEAD : HEAD + 1, :] + EPS
    tok = mix_ref[0:32, :]
    qt = mix_ref[32:64, :]
    kt = mix_ref[64:96, :]
    vt = mix_ref[96:128, :]
    dqs, dks, dvs = [], [], []
    for p in range(PAIRS):
        lanes = slice(128 * p, 128 * p + 128)
        gm = grad_ref[:, lanes]
        attn = mix_ref[128:256, lanes]
        da = exact(nn, vt[:, lanes].T, gm)
        dvs.append(exact(nt, gm, attn))
        pulled = attn * da
        ds = (pulled - attn * jnp.sum(pulled, axis=0, keepdims=True)) * (HEAD**-0.5)
        dqs.append(exact(nn, kt[:, lanes], ds))
        dks.append(exact(nt, qt[:, lanes], ds))
    dq = jnp.concatenate(dqs, axis=1)
    dk = jnp.concatenate(dks, axis=1)
    dv = jnp.concatenate(dvs, axis=1)
    dtok = exact(nn, wq_ref[...], dq) + exact(nn, wk_ref[...], dk) + exact(nn, wv_ref[...], dv)
    qkv = exact(nt, tok, jnp.concatenate([dq, dk, dv, jnp.zeros_like(dq)], axis=0))
    gnum = (dtok / lifted).astype(BF16).astype(F32)
    gden = -jnp.sum(dtok * tok, axis=0, keepdims=True) / lifted
    back_blocks, num_blocks, den_columns = [], [], []
    for p in range(PAIRS):
        lanes = slice(128 * p, 128 * p + 128)
        num = spread_pair(gnum[:, lanes])
        num_blocks.append(num.astype(BF16))
        both = jnp.concatenate([spread_pair(mix_ref[256:288, lanes]), num], axis=0)
        back_blocks.append(both.T.astype(BF16))
        den_columns.append(jnp.broadcast_to(gden[:, lanes], (128, 128)).T[:, 0:1])

    pair = slice_pair(wsl_ref[...])
    pair_b = pair.astype(BF16)
    pair_t = pair.T.astype(BF16)
    wfx = wfx_ref[...]
    wx = wx_ref[...]
    gain = gain_ref[...]
    bias = bias_ref[...]
    inv_t = [1.0 / jnp.full((1, CHUNK), temper_ref[h], F32) for h in range(HEADS)]
    early_ref[...] = jnp.zeros_like(early_ref)
    sums_ref[...] = jnp.zeros_like(sums_ref)
    small_ref[...] = jnp.zeros_like(small_ref)
    temp_ref[...] = jnp.zeros_like(temp_ref)

    def step(i, carry):
        at = pl.ds(pl.multiple_of(i * CHUNK, CHUNK), CHUNK)
        live = live_row(count, i)
        stats = stats_ref[:, at]
        mean, inv = stats[0:1], stats[1:2]
        g_mids, g_feats, temps = [], [], []
        for p in range(PAIRS):
            rows = slice(64 * p, 64 * p + 64)
            mids = mids_ref[rows, at]
            logits = nn(pair_t, mids)
            gw = nn(
                back_blocks[p], jnp.concatenate([gs_ref[rows, at], feats_ref[rows, at]], axis=0)
            )
            gw = gw + den_columns[p]
            scaled, weights = [], []
            for k in range(2):
                h = 2 * p + k
                part = slice(64 * k, 64 * k + 64)
                l = logits[part] * inv_t[h]
                pr = jnp.exp(l - stats[2 + h : 3 + h]) * live
                weights.append(pr.astype(BF16))
                g = gw[part]
                pulled = g * pr
                gl = pulled - pr * jnp.sum(pulled, axis=0, keepdims=True)
                temps.append(jnp.sum(gl * l, axis=0, keepdims=True))
                scaled.append((gl * inv_t[h]).astype(BF16))
            scaled = jnp.concatenate(scaled, axis=0)
            g_mids.append(nn(pair_b, scaled))
            small_ref[:, 0:128] += fold_pair(nt(mids, scaled))
            g_feats.append(nn(num_blocks[p], jnp.concatenate(weights, axis=0)))
        temp_ref[...] += lanes128(jnp.concatenate(temps, axis=0))
        g_mids = jnp.concatenate(g_mids, axis=0).astype(BF16)
        g_feats = jnp.concatenate(g_feats, axis=0).astype(BF16)
        xhat = (xt_ref[:, at].astype(F32) - mean) * inv
        n1 = (xhat * gain + bias).astype(BF16)
        early_ref[0:256, :] += nt(n1, g_feats)
        early_ref[256:512, :] += nt(n1, g_mids)
        g_n1 = nn(wfx, g_feats) + nn(wx, g_mids)
        sums_ref[0:256, :] += lanes128(g_n1 * xhat)
        sums_ref[256:512, :] += lanes128(g_n1)
        out = gres_ref[:, at] + norm_back(g_n1, xhat, inv, gain)
        cells_out_ref[at, :] = out.T.astype(BF16)
        return carry

    lax.fori_loop(0, STEPS, step, 0)
    slices = small_ref[:, 0:128]
    slices = slices + pltpu.roll(slices, 64, 1)
    inv_col = jnp.concatenate([t[:, :128] for t in inv_t], axis=0)
    temper = -jnp.broadcast_to(jnp.sum(temp_ref[...], axis=1, keepdims=True), (8, 128)) * inv_col
    rows = jnp.concatenate(
        [as_row(sums_ref[0:256, :]), as_row(sums_ref[256:512, :]), ln2_ref[0:2, :],
         jnp.zeros((4, WIDTH), F32)],
        axis=0,
    )
    zeros = jnp.zeros((EARLY_HALF - 560, 128), F32)
    left = jnp.concatenate([early_ref[:, :128], slices, temper, rows[:, :128], zeros], axis=0)
    right = jnp.concatenate(
        [early_ref[:, 128:], qkv * (1.0 / SPACE), jnp.zeros((8, 128), F32), rows[:, 128:], zeros],
        axis=0,
    )
    left = left * Z_SCALE
    right = right * Z_SCALE
    keep_ref[...] = jnp.where(core == 0, left, right)
    send_ref[...] = jnp.where(core == 0, right, left)


def last_kernel(
    core_ref, mine_ref, theirs_ref,
    fx_ref, x_ref, out_ref, up_ref, down_ref, slice_ref, q_ref, k_ref, v_ref, temper_ref, rows_ref,
    whole_ref,
):
    core = core_ref[0]
    for part in range(16):
        mine = mine_ref[part]
        theirs = theirs_ref[part]
        left = jnp.where(core == 0, mine, theirs)
        right = jnp.where(core == 0, theirs, mine)
        both = jnp.concatenate([left, right], axis=1)
        whole_ref[part * LATE_PART : (part + 1) * LATE_PART, :] = both[:LATE_PART]
        at = LATE_HALF + part * EARLY_PART
        whole_ref[at : at + EARLY_PART, :] = both[LATE_PART:]
    out_ref[...] = whole_ref[0:256, :]
    up_ref[...] = whole_ref[256:512, :]
    down_ref[...] = whole_ref[512:768, :]
    fx_ref[...] = whole_ref[768:1024, :]
    x_ref[...] = whole_ref[1024:1280, :]
    slice_ref[...] = whole_ref[1280:1312, 0:64]
    qkv = whole_ref[1280:1312, 128:256]
    q_ref[...] = qkv[:, 0:32]
    k_ref[...] = qkv[:, 32:64]
    v_ref[...] = qkv[:, 64:96]
    temper_ref[...] = whole_ref[1312:1320, 0:128]
    rows_ref[...] = whole_ref[1320:1328, :]


def permutation(move):
    pairs = []
    for yl in range(2):
        for x in range(4):
            for yh in range(2):
                for z in range(8):
                    for c in range(2):
                        place = lambda a, b, e, f, g: (((a * 4 + b) * 2 + e) * 8 + f) * 2 + g
                        pairs.append((place(yl, x, yh, z, c), place(*move(yl, x, yh, z, c))))
    return pairs


OTHER_CORE = permutation(lambda yl, x, yh, z, c: (yl, x, yh, z, 1 - c))
Z_ONE = permutation(lambda yl, x, yh, z, c: (yl, x, yh, z ^ 1, c))
Z_TWO = permutation(lambda yl, x, yh, z, c: (yl, x, yh, z ^ 2, c))
Z_FAR = permutation(lambda yl, x, yh, z, c: (yl, x, yh, 7 - z, c))
Y_FAR = permutation(lambda yl, x, yh, z, c: (yl, x, 1 - yh, z, c))


def swap(v, pairs):
    return lax.ppermute(v, AXES, pairs)


def space_sum(v):
    for pairs in (OTHER_CORE, Z_ONE, Z_TWO, Z_FAR, Y_FAR):
        v = v + swap(v, pairs)
    return v


VMEM = pl.BlockSpec(memory_space=pltpu.VMEM)
SMEM = pl.BlockSpec(memory_space=pltpu.SMEM)
PARAMS = pltpu.CompilerParams(vmem_limit_bytes=40 * 1024 * 1024)


def call(kernel, name, outs, scalars, arrays, scratch=()):
    return pl.pallas_call(
        kernel,
        name=name,
        out_shape=[jax.ShapeDtypeStruct(shape, dtype) for shape, dtype in outs],
        in_specs=[SMEM] * len(scalars) + [VMEM] * len(arrays),
        out_specs=[VMEM] * len(outs),
        scratch_shapes=[pltpu.VMEM(shape, F32) for shape in scratch],
        compiler_params=PARAMS,
    )(*scalars, *arrays)


def body(
    cells, cotangent, cell_count, first_norm_gain, first_norm_bias, w_fx, w_x, w_slice, temper,
    query_weight, key_weight, value_weight, w_out, second_norm_gain, second_norm_bias, w_up, w_down,
):
    rows, cot = cells[0], cotangent[0]
    count = cell_count.reshape(1)
    core = lax.axis_index("c").astype(jnp.int32).reshape(1)
    gain1, bias1 = first_norm_gain.reshape(WIDTH, 1), first_norm_bias.reshape(WIDTH, 1)
    gain2, bias2 = second_norm_gain.reshape(WIDTH, 1), second_norm_bias.reshape(WIDTH, 1)
    pay, xt, feats, mids, weights, stats = call(
        front_kernel, "front",
        [((40, 512), F32), ((WIDTH, CELLS), BF16), ((WIDTH, CELLS), BF16), ((WIDTH, CELLS), BF16),
         ((512, CELLS), BF16), ((16, CELLS), F32)],
        [count, temper], [rows, gain1, bias1, w_fx, w_x, w_slice],
    )
    pay = space_sum(pay)
    layer, gres, gs, tok, keep2, send2, ln2, mix = call(
        middle_kernel, "middle",
        [((CELLS, WIDTH), BF16), ((WIDTH, CELLS), F32), ((WIDTH, CELLS), BF16), ((HEAD, 512), F32),
         ((LATE_HALF, 128), F32), ((LATE_HALF, 128), F32), ((8, WIDTH), F32), ((288, 512), F32)],
        [core],
        [pay, query_weight, key_weight, value_weight, xt, weights, cot, w_out, w_up, w_down, gain2,
         bias2],
        [(768, WIDTH), (512, 128)],
    )
    tok = space_sum(tok)
    late = keep2 + swap(send2, OTHER_CORE)
    out_rows, keep3, send3 = call(
        rear_kernel, "rear",
        [((CELLS, WIDTH), BF16), ((EARLY_HALF, 128), F32), ((EARLY_HALF, 128), F32)],
        [core, count, temper],
        [pay, tok, mix, query_weight, key_weight, value_weight, xt, feats, mids, stats, gs, gres,
         gain1, bias1, w_fx, w_x, w_slice, ln2],
        [(512, WIDTH), (512, 128), (HEAD, 128), (8, 128)],
    )
    early = keep3 + swap(send3, OTHER_CORE)
    both = jnp.concatenate(
        [late.reshape(16, LATE_PART, 128), early.reshape(16, EARLY_PART, 128)], axis=1
    )
    part = jnp.sum(lax.all_to_all(both, PLANE, 0, 0), axis=0)
    for pairs in (Z_ONE, Z_TWO, Z_FAR):
        part = part + swap(part, pairs)
    mine = lax.all_to_all(jnp.broadcast_to(part[None], both.shape), PLANE, 0, 0)
    theirs = swap(mine, OTHER_CORE)
    fx, gx, out, up, down, sl, q, k, v, temp, norms = call(
        last_kernel, "last",
        [((WIDTH, WIDTH), F32)] * 5
        + [((HEAD, SLICES), F32)] + [((HEAD, HEAD), F32)] * 3 + [((8, 128), F32), ((8, WIDTH), F32)],
        [core], [mine, theirs],
        [(LATE_HALF + EARLY_HALF, WIDTH)],
    )
    return (
        layer[None], out_rows[None], norms[0], norms[1], fx, gx, sl, temp[:, 0], q, k, v, out,
        norms[2], norms[3], up, down,
    )


def solution(mesh):
    fine = Mesh(mesh.devices.reshape(2, 4, 2, 8, 2), AXES)
    split = P(("yl", "x"), ("yh", "z", "c"), None)
    return jax.shard_map(
        body,
        mesh=fine,
        in_specs=(split, split, P(("yl", "x"), ("yh", "z", "c"))) + (P(),) * 14,
        out_specs=(split, split) + (P(),) * 14,
        check_vma=False,
    )
```

time: 832 us -> 142 us (0.17)
  waiting for transfers between devices: 586 us -> 33 us
  blocking collectives: 148 us -> 33 us
  starting transfers between devices: 0.3 us -> 39.6 us
  matrix products: 39.3 us -> 0 us
  Pallas kernels: 0 us -> 26.2 us
  local copies, waits for them, and re-layouts: 28.1 us -> 6.59 us
  between operations: 15.5 us -> 1.61 us
  other arithmetic: 13.5 us -> 1.91 us
    psum x3 -> x0, waiting for transfers between devices: 586 us -> none  [the longest x1 238 us: body(): tok_grad = lax.psum(token_partial, 'space')]
    psum x2 -> x0, blocking collectives: 148 us -> none  [the longest x1 79 us: body(): lax.psum((pieces[0], pieces[1], pieces[2], pieces[3], pieces[4], pieces[5...]
    ppermute x0 -> x16, starting transfers between devices: none -> 39.6 us  [swap(): return lax.ppermute(v, AXES, pairs)]
    dot_general x39 -> x0, matrix products: 39.3 us -> none  [the longest x3 3.52 us: mix_tokens(): jnp.einsum('pfq,plq->pfl', query_rows, key_rows, precision=maximum_logit)]
    all_to_all x0 -> x2, blocking collectives: none -> 33 us  [the longest x1 19.6 us: body(): part = jnp.sum(lax.all_to_all(both, PLANE, 0, 0), axis=0)]
    ppermute x0 -> x16, waiting for transfers between devices: none -> 33 us  [swap(): return lax.ppermute(v, AXES, pairs)]
    pallas_call x0 -> x4, Pallas kernels: none -> 26.2 us  [call(): pl.pallas_call(kernel, name=name, out_shape=[jax.ShapeDtypeStruct(shape,...]
    unnamed x165 -> x38, local copies, waits for them, and re-layouts: 15.3 us -> 4.09 us
  transfers between devices with their start and end apart: 3 -> 16, of which waited for: 3 -> 14; matrix products, arithmetic and copies ran while one was open for 1% -> 0% of each run, Pallas kernels for 0% -> 7%
where the time goes in v1:
time: 142 us
  starting transfers between devices  39.6 us (28%)
  waiting for transfers between devices  33 us (23%)
  blocking collectives  33 us (23%)
  Pallas kernels  26.2 us (18%)
  local copies, waits for them, and re-layouts  6.59 us (5%)
  other arithmetic  1.91 us (1%)
  between operations  1.61 us (1%)
    ppermute x16, starting transfers between devices, swap(): return lax.ppermute(v, AXES, pairs)  39.6 us
    ppermute x16, waiting for transfers between devices, swap(): return lax.ppermute(v, AXES, pairs)  33 us
    pallas_call x4, Pallas kernels, call(): pl.pallas_call(kernel, name=name, out_shape=[jax.ShapeDtypeStruct(shape,...  26.2 us
    all_to_all x1, blocking collectives, body(): part = jnp.sum(lax.all_to_all(both, PLANE, 0, 0), axis=0)  19.6 us
    all_to_all x1, blocking collectives, body(): mine = lax.all_to_all(jnp.broadcast_to(part[None], both.shape), PLANE, 0, 0)  13.4 us
    unnamed x38, local copies, waits for them, and re-layouts  4.09 us
  transfers between devices with their start and end apart: 16, of which 14 were waited for; matrix products, arithmetic and copies ran while one was open for 0% of the time, Pallas kernels for 7%

profile of v1, /device:TPU:1, one launch (start us, length us, event | category | flops | bytes accessed | tf_op | source)
XLA Modules:
  0.0 141.9 jit_solution(17288839209156772517)
XLA Ops:
  1.3 0.8 copy.33.gain_ref
  2.2 0.1 copy.34.bias_ref
  2.4 0.6 copy-done.15
  3.0 1.0 copy-done
  4.1 6.3 %front.1 = (f32[40,512]{1,0:T(8,128)S(1)}, bf16[256,1024]{1,0:T(8,128)(2,1)S(1)}, bf16[256,1024]{1,0:T(8,128)(2,1)S(1)}, bf16[256,1024]{1,0:T(8,128)(2,1)S(1)}, ...) custom-call(s32[1]{0:T(128)} %bitcast.16.count_ref, f32[8]{0:T(128)S(1)} %copy-done.15, ...), custom_call_target="tpu_custom_call" | custom-call | tf_op jit(solution)/shard_map/front/pallas_call | solution.py:424
  10.4 0.8 copy-done.2
  11.2 3.2 %collective-permute-start = (f32[40,512]{1,0:T(8,128)S(1)}, f32[40,512]{1,0:T(8,128)S(1)}, u32[]{:S(2)}, u32[]{:S(2)}) collective-permute-start(f32[40,512]{1,0:T(8,128)S(1)} %get-tuple-element.44), channel_id=1, source_target_pairs={{0,1},{1,0},{2,3},{3,2},{4,5},{5,4},{6,7},{7,6},{8,9},{9,8},{10,11... | collective-permute-start | bytes 245768 | tf_op jit(solution)/shard_map/ppermute | solution.py:409
  14.4 0.9 collective-permute-done
  15.5 3.7 %collective-permute-done.1 = f32[40,512]{1,0:T(8,128)S(1)} collective-permute-done((f32[40,512]{1,0:T(8,128)S(1)}, f32[40,512]{1,0:T(8,128)S(1)}, u32[]{:S(2)}, u32[]{:S(2)}) %collective-permute-start.1) | collective-permute-done | bytes 81952 | tf_op jit(solution)/shard_map/ppermute | solution.py:409
  19.2 1.7 %collective-permute-start.2 = (f32[40,512]{1,0:T(8,128)S(1)}, f32[40,512]{1,0:T(8,128)S(1)}, u32[]{:S(2)}, u32[]{:S(2)}) collective-permute-start(f32[40,512]{1,0:T(8,128)S(1)} %add.46), channel_id=1, source_target_pairs={{0,4},{1,5},{2,6},{3,7},{4,0},{5,1},{6,2},{7,3},{8,12},{9,13},{10,... | collective-permute-start | bytes 245768 | tf_op jit(solution)/shard_map/ppermute | solution.py:409
  20.9 4.7 %collective-permute-done.2 = f32[40,512]{1,0:T(8,128)S(1)} collective-permute-done((f32[40,512]{1,0:T(8,128)S(1)}, f32[40,512]{1,0:T(8,128)S(1)}, u32[]{:S(2)}, u32[]{:S(2)}) %collective-permute-start.2) | collective-permute-done | bytes 81952 | tf_op jit(solution)/shard_map/ppermute | solution.py:409
  25.6 3.0 %collective-permute-start.3 = (f32[40,512]{1,0:T(8,128)S(1)}, f32[40,512]{1,0:T(8,128)S(1)}, u32[]{:S(2)}, u32[]{:S(2)}) collective-permute-start(f32[40,512]{1,0:T(8,128)S(1)} %add.47), channel_id=1, source_target_pairs={{0,14},{1,15},{2,12},{3,13},{4,10},{5,11},{6,8},{7,9},{8,6},{9,7},... | collective-permute-start | bytes 245768 | tf_op jit(solution)/shard_map/ppermute | solution.py:409
  28.6 2.7 %collective-permute-done.3 = f32[40,512]{1,0:T(8,128)S(1)} collective-permute-done((f32[40,512]{1,0:T(8,128)S(1)}, f32[40,512]{1,0:T(8,128)S(1)}, u32[]{:S(2)}, u32[]{:S(2)}) %collective-permute-start.3) | collective-permute-done | bytes 81952 | tf_op jit(solution)/shard_map/ppermute | solution.py:409
  31.3 0.6 add.48
  32.0 2.9 %collective-permute-start.4 = (f32[40,512]{1,0:T(8,128)}, f32[40,512]{1,0:T(8,128)}, u32[]{:S(2)}, u32[]{:S(2)}) collective-permute-start(f32[40,512]{1,0:T(8,128)} %add.48), channel_id=1, source_target_pairs={{0,16},{1,17},{2,18},{3,19},{4,20},{5,21},{6,22},{7,23},{8,24},{9,... | collective-permute-start | bytes 245768 | tf_op jit(solution)/shard_map/ppermute | solution.py:409
  34.9 0.1 copy.35.gain_ref
  35.0 0.7 copy-done.18
  35.7 0.1 copy.36.bias_ref
  35.9 1.2 collective-permute-done.4
  37.1 1.0 add.49.pay_ref
  38.1 0.9 copy-done.8
  39.0 9.0 %middle.1 = (bf16[1024,256]{1,0:T(8,128)(2,1)}, f32[256,1024]{1,0:T(8,128)S(1)}, bf16[256,1024]{1,0:T(8,128)(2,1)S(1)}, f32[32,512]{1,0:T(8,128)S(1)}, f32[768,1...) custom-call(s32[1]{0:T(128)} %bitcast.core_ref, ...), custom_call_target="tpu_custom_call" | custom-call | tf_op jit(solution)/shard_map/middle/pallas_call | solution.py:424
  48.0 3.7 %collective-permute-start.5 = (f32[32,512]{1,0:T(8,128)S(1)}, f32[32,512]{1,0:T(8,128)S(1)}, u32[]{:S(2)}, u32[]{:S(2)}) collective-permute-start(f32[32,512]{1,0:T(8,128)S(1)} %get-tuple-element.48), channel_id=1, source_target_pairs={{0,1},{1,0},{2,3},{3,2},{4,5},{5,4},{6,7},{7,6},{8,9},{9,8},{10,11... | collective-permute-start | bytes 196616 | tf_op jit(solution)/shard_map/ppermute | solution.py:409
  51.7 0.9 collective-permute-done.5
  52.7 0.4 collective-permute-start.6
  53.1 2.8 %collective-permute-done.6 = f32[32,512]{1,0:T(8,128)S(1)} collective-permute-done((f32[32,512]{1,0:T(8,128)S(1)}, f32[32,512]{1,0:T(8,128)S(1)}, u32[]{:S(2)}, u32[]{:S(2)}) %collective-permute-start.6) | collective-permute-done | bytes 65568 | tf_op jit(solution)/shard_map/ppermute | solution.py:409
  55.9 1.2 collective-permute-start.7
  57.0 3.7 %collective-permute-done.7 = f32[32,512]{1,0:T(8,128)S(1)} collective-permute-done((f32[32,512]{1,0:T(8,128)S(1)}, f32[32,512]{1,0:T(8,128)S(1)}, u32[]{:S(2)}, u32[]{:S(2)}) %collective-permute-start.7) | collective-permute-done | bytes 65568 | tf_op jit(solution)/shard_map/ppermute | solution.py:409
  60.7 3.5 %collective-permute-start.8 = (f32[32,512]{1,0:T(8,128)S(1)}, f32[32,512]{1,0:T(8,128)S(1)}, u32[]{:S(2)}, u32[]{:S(2)}) collective-permute-start(f32[32,512]{1,0:T(8,128)S(1)} %add.52), channel_id=1, source_target_pairs={{0,14},{1,15},{2,12},{3,13},{4,10},{5,11},{6,8},{7,9},{8,6},{9,7},... | collective-permute-start | bytes 196616 | tf_op jit(solution)/shard_map/ppermute | solution.py:409
  64.2 2.3 %collective-permute-done.8 = f32[32,512]{1,0:T(8,128)S(1)} collective-permute-done((f32[32,512]{1,0:T(8,128)S(1)}, f32[32,512]{1,0:T(8,128)S(1)}, u32[]{:S(2)}, u32[]{:S(2)}) %collective-permute-start.8) | collective-permute-done | bytes 65568 | tf_op jit(solution)/shard_map/ppermute | solution.py:409
  66.5 3.0 %collective-permute-start.9 = (f32[32,512]{1,0:T(8,128)S(1)}, f32[32,512]{1,0:T(8,128)S(1)}, u32[]{:S(2)}, u32[]{:S(2)}) collective-permute-start(f32[32,512]{1,0:T(8,128)S(1)} %add.53), channel_id=1, source_target_pairs={{0,16},{1,17},{2,18},{3,19},{4,20},{5,21},{6,22},{7,23},{8,24},{9,... | collective-permute-start | bytes 196616 | tf_op jit(solution)/shard_map/ppermute | solution.py:409
  69.5 3.8 %collective-permute-start.10 = (f32[768,128]{1,0:T(8,128)S(1)}, f32[768,128]{1,0:T(8,128)S(1)}, u32[]{:S(2)}, u32[]{:S(2)}) collective-permute-start(f32[768,128]{1,0:T(8,128)S(1)} %get-tuple-element.58), channel_id=1, source_target_pairs={{0,1},{1,0},{2,3},{3,2},{4,5},{5,4},{6,7},{7,6},{8,9},{9,8},{10,11... | collective-permute-start | bytes 1179656 | tf_op jit(solution)/shard_map/ppermute | solution.py:409
  73.3 9.7 %rear.1 = (bf16[1024,256]{1,0:T(8,128)(2,1)}, f32[640,128]{1,0:T(8,128)S(1)}, f32[640,128]{1,0:T(8,128)S(1)}) custom-call(s32[1]{0:T(128)} %bitcast.core_ref, s32[1]{0:T(128)} %bitcast.17.count_ref, f32[8]{0:T(128)S(1)} %copy-done.15, f32[40,512]{1,0:T(8,128)S(1)} %add.49.pay_ref, f32[32,512]{1,0:T(8,128)S(1)} %add.54.grad_ref, ...), custom_call_target="tpu_custom_call" | custom-call | tf_op jit(solution)/shard_map/rear/pallas_call | solution.py:424
  83.1 2.6 %collective-permute-start.11 = (f32[640,128]{1,0:T(8,128)S(1)}, f32[640,128]{1,0:T(8,128)S(1)}, u32[]{:S(2)}, u32[]{:S(2)}) collective-permute-start(f32[640,128]{1,0:T(8,128)S(1)} %get-tuple-element.60), channel_id=1, source_target_pairs={{0,1},{1,0},{2,3},{3,2},{4,5},{5,4},{6,7},{7,6},{8,9},{9,8},{10,11... | collective-permute-start | bytes 983048 | tf_op jit(solution)/shard_map/ppermute | solution.py:409
  85.7 1.2 collective-permute-done.11
  87.0 19.6 %all_to_all.10 = f32[16,88,128]{2,1,0:T(8,128)S(1)} all-to-all(f32[16,88,128]{2,1,0:T(8,128)S(1)} %pad_maximum_fusion), channel_id=1, replica_groups=mesh['yl'=2,'x'=4,'yh'=2,'z'=8,'c'=2] {'yl','x','yh'}, dimensions={0} | all-to-all | bytes 1441792 | tf_op jit(solution)/shard_map/all_to_all | solution.py:474
  106.7 0.6 collective-permute-start.12
  107.3 2.4 %collective-permute-done.12 = f32[88,128]{1,0:T(8,128)S(1)} collective-permute-done((f32[88,128]{1,0:T(8,128)S(1)}, f32[88,128]{1,0:T(8,128)S(1)}, u32[]{:S(2)}, u32[]{:S(2)}) %collective-permute-start.12) | collective-permute-done | bytes 45088 | tf_op jit(solution)/shard_map/ppermute | solution.py:409
  109.6 1.3 collective-permute-start.13
  111.0 3.0 %collective-permute-done.13 = f32[88,128]{1,0:T(8,128)S(1)} collective-permute-done((f32[88,128]{1,0:T(8,128)S(1)}, f32[88,128]{1,0:T(8,128)S(1)}, u32[]{:S(2)}, u32[]{:S(2)}) %collective-permute-start.13) | collective-permute-done | bytes 45088 | tf_op jit(solution)/shard_map/ppermute | solution.py:409
  114.0 2.5 %collective-permute-start.14 = (f32[88,128]{1,0:T(8,128)S(1)}, f32[88,128]{1,0:T(8,128)S(1)}, u32[]{:S(2)}, u32[]{:S(2)}) collective-permute-start(f32[88,128]{1,0:T(8,128)S(1)} %add.58), channel_id=1, source_target_pairs={{0,14},{1,15},{2,12},{3,13},{4,10},{5,11},{6,8},{7,9},{8,6},{9,7},... | collective-permute-start | bytes 135176 | tf_op jit(solution)/shard_map/ppermute | solution.py:409
  116.5 1.7 %collective-permute-done.14 = f32[88,128]{1,0:T(8,128)S(1)} collective-permute-done((f32[88,128]{1,0:T(8,128)S(1)}, f32[88,128]{1,0:T(8,128)S(1)}, u32[]{:S(2)}, u32[]{:S(2)}) %collective-permute-start.14) | collective-permute-done | bytes 45088 | tf_op jit(solution)/shard_map/ppermute | solution.py:409
  118.3 13.4 %all_to_all.11.mine_ref = f32[16,88,128]{2,1,0:T(8,128)S(1)} all-to-all(f32[16,88,128]{2,1,0:T(8,128)S(1)} %broadcast_in_dim.14), channel_id=1, replica_groups=mesh['yl'=2,'x'=4,'yh'=2,'z'=8,'c'=2] {'yl','x','yh'}, dimensions={0} | all-to-all | bytes 1441792 | tf_op jit(solution)/shard_map/all_to_all | solution.py:477
  131.7 6.1 %collective-permute-start.15 = (f32[16,88,128]{2,1,0:T(8,128)S(1)}, f32[16,88,128]{2,1,0:T(8,128)S(1)}, u32[]{:S(2)}, u32[]{:S(2)}) collective-permute-start(f32[16,88,128]{2,1,0:T(8,128)S(1)} %all_to_all.11.mine_ref), channel_id=1, source_target_pairs={{0,1},{1,0},{2,3},{3,2},{4,5},{5,4},{6,7},{7,6},{8,9},{9,8},{10,11... | collective-permute-start | bytes 2162696 | tf_op jit(solution)/shard_map/ppermute | solution.py:409
  137.8 1.8 %collective-permute-done.15.theirs_ref = f32[16,88,128]{2,1,0:T(8,128)S(1)} collective-permute-done((f32[16,88,128]{2,1,0:T(8,128)S(1)}, f32[16,88,128]{2,1,0:T(8,128)S(1)}, u32[]{:S(2)}, u32[]{:S(2)}) %collective-permute-start.15) | collective-permute-done | bytes 720928 | tf_op jit(solution)/shard_map/ppermute | solution.py:409
  139.6 1.1 last.1
  140.7 0.6 fusion
  141.3 0.6 slice_reduce_fusion
  (52 shorter events, 0.5 us)
Async XLA Ops:
  0.6 1.7 %copy-start.14 = (bf16[32,64]{1,0:T(8,128)(2,1)S(1)}, bf16[32,64]{1,0:T(8,128)(2,1)}, u32[]{:S(2)}) copy-start(bf16[32,64]{1,0:T(8,128)(2,1)} %wsl_ref.3) | copy-start | bytes 12292
  1.3 0.9 copy-start.16
  1.3 1.1 copy-start.4
  1.3 1.1 copy-start.5
  2.4 0.7 copy-start.15
  3.0 1.0 copy-start
  10.4 0.8 copy-start.2
  11.2 4.2 %copy-start.9 = (f32[16,1024]{1,0:T(8,128)}, f32[16,1024]{1,0:T(8,128)S(1)}, u32[]{:S(2)}) copy-start(f32[16,1024]{1,0:T(8,128)S(1)} %get-tuple-element.52.stats_ref) | copy-start | bytes 196612
  11.2 4.2 %collective-permute-start = (f32[40,512]{1,0:T(8,128)S(1)}, f32[40,512]{1,0:T(8,128)S(1)}, u32[]{:S(2)}, u32[]{:S(2)}) collective-permute-start(f32[40,512]{1,0:T(8,128)S(1)} %get-tuple-element.44), channel_id=1, source_target_pairs={{0,1},{1,0},{2,3},{3,2},{4,5},{5,4},{6,7},{7,6},{8,9},{9,8},{10,11... | collective-permute-start | bytes 245768 | tf_op jit(solution)/shard_map/ppermute | solution.py:409
  15.4 3.8 %collective-permute-start.1 = (f32[40,512]{1,0:T(8,128)S(1)}, f32[40,512]{1,0:T(8,128)S(1)}, u32[]{:S(2)}, u32[]{:S(2)}) collective-permute-start(f32[40,512]{1,0:T(8,128)S(1)} %add.45), channel_id=1, source_target_pairs={{0,2},{1,3},{2,0},{3,1},{4,6},{5,7},{6,4},{7,5},{8,10},{9,11},{10,... | collective-permute-start | bytes 245768 | tf_op jit(solution)/shard_map/ppermute | solution.py:409
  19.1 15.7 %copy-start.17 = (f32[256]{0:T(256)S(1)}, f32[256]{0:T(256)}, u32[]{:S(2)}) copy-start(f32[256]{0:T(256)} %param.30) | copy-start | bytes 3076
  19.2 18.9 %copy-start.1 = (bf16[1,1024,256]{2,1,0:T(8,128)(2,1)S(1)}, bf16[1,1024,256]{2,1,0:T(8,128)(2,1)}, u32[]{:S(2)}) copy-start(bf16[1,1024,256]{2,1,0:T(8,128)(2,1)} %param.18) | copy-start | bytes 1572868
  19.2 6.4 %collective-permute-start.2 = (f32[40,512]{1,0:T(8,128)S(1)}, f32[40,512]{1,0:T(8,128)S(1)}, u32[]{:S(2)}, u32[]{:S(2)}) collective-permute-start(f32[40,512]{1,0:T(8,128)S(1)} %add.46), channel_id=1, source_target_pairs={{0,4},{1,5},{2,6},{3,7},{4,0},{5,1},{6,2},{7,3},{8,12},{9,13},{10,... | collective-permute-start | bytes 245768 | tf_op jit(solution)/shard_map/ppermute | solution.py:409
  25.6 5.7 %collective-permute-start.3 = (f32[40,512]{1,0:T(8,128)S(1)}, f32[40,512]{1,0:T(8,128)S(1)}, u32[]{:S(2)}, u32[]{:S(2)}) collective-permute-start(f32[40,512]{1,0:T(8,128)S(1)} %add.47), channel_id=1, source_target_pairs={{0,14},{1,15},{2,12},{3,13},{4,10},{5,11},{6,8},{7,9},{8,6},{9,7},... | collective-permute-start | bytes 245768 | tf_op jit(solution)/shard_map/ppermute | solution.py:409
  32.0 5.1 %collective-permute-start.4 = (f32[40,512]{1,0:T(8,128)}, f32[40,512]{1,0:T(8,128)}, u32[]{:S(2)}, u32[]{:S(2)}) collective-permute-start(f32[40,512]{1,0:T(8,128)} %add.48), channel_id=1, source_target_pairs={{0,16},{1,17},{2,18},{3,19},{4,20},{5,21},{6,22},{7,23},{8,24},{9,... | collective-permute-start | bytes 245768 | tf_op jit(solution)/shard_map/ppermute | solution.py:409
  35.0 0.7 copy-start.18
  35.7 2.4 %copy-start.7 = (bf16[256,256]{1,0:T(8,128)(2,1)S(1)}, bf16[256,256]{1,0:T(8,128)(2,1)}, u32[]{:S(2)}) copy-start(bf16[256,256]{1,0:T(8,128)(2,1)} %wup_ref.1) | copy-start | bytes 393220
  35.8 2.2 %copy-start.6 = (bf16[256,256]{1,0:T(8,128)(2,1)S(1)}, bf16[256,256]{1,0:T(8,128)(2,1)}, u32[]{:S(2)}) copy-start(bf16[256,256]{1,0:T(8,128)(2,1)} %wout_ref.1) | copy-start | bytes 393220
  37.1 1.0 copy-start.11
  37.1 1.0 copy-start.12
  37.1 1.0 copy-start.13
  38.1 0.9 copy-start.8
  48.0 25.3 %copy-start.3 = (bf16[256,1024]{1,0:T(8,128)(2,1)S(1)}, bf16[256,1024]{1,0:T(8,128)(2,1)}, u32[]{:S(2)}) copy-start(bf16[256,1024]{1,0:T(8,128)(2,1)} %copy-done.2) | copy-start | bytes 1572868
  48.0 4.6 %collective-permute-start.5 = (f32[32,512]{1,0:T(8,128)S(1)}, f32[32,512]{1,0:T(8,128)S(1)}, u32[]{:S(2)}, u32[]{:S(2)}) collective-permute-start(f32[32,512]{1,0:T(8,128)S(1)} %get-tuple-element.48), channel_id=1, source_target_pairs={{0,1},{1,0},{2,3},{3,2},{4,5},{5,4},{6,7},{7,6},{8,9},{9,8},{10,11... | collective-permute-start | bytes 196616 | tf_op jit(solution)/shard_map/ppermute | solution.py:409
  52.7 3.2 %collective-permute-start.6 = (f32[32,512]{1,0:T(8,128)S(1)}, f32[32,512]{1,0:T(8,128)S(1)}, u32[]{:S(2)}, u32[]{:S(2)}) collective-permute-start(f32[32,512]{1,0:T(8,128)S(1)} %add.50), channel_id=1, source_target_pairs={{0,2},{1,3},{2,0},{3,1},{4,6},{5,7},{6,4},{7,5},{8,10},{9,11},{10,... | collective-permute-start | bytes 196616 | tf_op jit(solution)/shard_map/ppermute | solution.py:409
  55.9 4.8 %collective-permute-start.7 = (f32[32,512]{1,0:T(8,128)S(1)}, f32[32,512]{1,0:T(8,128)S(1)}, u32[]{:S(2)}, u32[]{:S(2)}) collective-permute-start(f32[32,512]{1,0:T(8,128)S(1)} %add.51), channel_id=1, source_target_pairs={{0,4},{1,5},{2,6},{3,7},{4,0},{5,1},{6,2},{7,3},{8,12},{9,13},{10,... | collective-permute-start | bytes 196616 | tf_op jit(solution)/shard_map/ppermute | solution.py:409
  60.7 5.8 %collective-permute-start.8 = (f32[32,512]{1,0:T(8,128)S(1)}, f32[32,512]{1,0:T(8,128)S(1)}, u32[]{:S(2)}, u32[]{:S(2)}) collective-permute-start(f32[32,512]{1,0:T(8,128)S(1)} %add.52), channel_id=1, source_target_pairs={{0,14},{1,15},{2,12},{3,13},{4,10},{5,11},{6,8},{7,9},{8,6},{9,7},... | collective-permute-start | bytes 196616 | tf_op jit(solution)/shard_map/ppermute | solution.py:409
  66.5 6.8 %collective-permute-start.9 = (f32[32,512]{1,0:T(8,128)S(1)}, f32[32,512]{1,0:T(8,128)S(1)}, u32[]{:S(2)}, u32[]{:S(2)}) collective-permute-start(f32[32,512]{1,0:T(8,128)S(1)} %add.53), channel_id=1, source_target_pairs={{0,16},{1,17},{2,18},{3,19},{4,20},{5,21},{6,22},{7,23},{8,24},{9,... | collective-permute-start | bytes 196616 | tf_op jit(solution)/shard_map/ppermute | solution.py:409
  69.5 3.8 %copy-start.10 = (f32[16,1024]{1,0:T(8,128)S(1)}, f32[16,1024]{1,0:T(8,128)}, u32[]{:S(2)}) copy-start(f32[16,1024]{1,0:T(8,128)} %copy-done.9) | copy-start | bytes 196612
  69.5 16.1 %collective-permute-start.10 = (f32[768,128]{1,0:T(8,128)S(1)}, f32[768,128]{1,0:T(8,128)S(1)}, u32[]{:S(2)}, u32[]{:S(2)}) collective-permute-start(f32[768,128]{1,0:T(8,128)S(1)} %get-tuple-element.58), channel_id=1, source_target_pairs={{0,1},{1,0},{2,3},{3,2},{4,5},{5,4},{6,7},{7,6},{8,9},{9,8},{10,11... | collective-permute-start | bytes 1179656 | tf_op jit(solution)/shard_map/ppermute | solution.py:409
  83.1 3.8 %collective-permute-start.11 = (f32[640,128]{1,0:T(8,128)S(1)}, f32[640,128]{1,0:T(8,128)S(1)}, u32[]{:S(2)}, u32[]{:S(2)}) collective-permute-start(f32[640,128]{1,0:T(8,128)S(1)} %get-tuple-element.60), channel_id=1, source_target_pairs={{0,1},{1,0},{2,3},{3,2},{4,5},{5,4},{6,7},{7,6},{8,9},{9,8},{10,11... | collective-permute-start | bytes 983048 | tf_op jit(solution)/shard_map/ppermute | solution.py:409
  106.7 3.0 %collective-permute-start.12 = (f32[88,128]{1,0:T(8,128)S(1)}, f32[88,128]{1,0:T(8,128)S(1)}, u32[]{:S(2)}, u32[]{:S(2)}) collective-permute-start(f32[88,128]{1,0:T(8,128)S(1)} %reduce_sum.9), channel_id=1, source_target_pairs={{0,2},{1,3},{2,0},{3,1},{4,6},{5,7},{6,4},{7,5},{8,10},{9,11},{10,... | collective-permute-start | bytes 135176 | tf_op jit(solution)/shard_map/ppermute | solution.py:409
  109.6 4.4 %collective-permute-start.13 = (f32[88,128]{1,0:T(8,128)S(1)}, f32[88,128]{1,0:T(8,128)S(1)}, u32[]{:S(2)}, u32[]{:S(2)}) collective-permute-start(f32[88,128]{1,0:T(8,128)S(1)} %add.57), channel_id=1, source_target_pairs={{0,4},{1,5},{2,6},{3,7},{4,0},{5,1},{6,2},{7,3},{8,12},{9,13},{10,... | collective-permute-start | bytes 135176 | tf_op jit(solution)/shard_map/ppermute | solution.py:409
  114.0 4.2 %collective-permute-start.14 = (f32[88,128]{1,0:T(8,128)S(1)}, f32[88,128]{1,0:T(8,128)S(1)}, u32[]{:S(2)}, u32[]{:S(2)}) collective-permute-start(f32[88,128]{1,0:T(8,128)S(1)} %add.58), channel_id=1, source_target_pairs={{0,14},{1,15},{2,12},{3,13},{4,10},{5,11},{6,8},{7,9},{8,6},{9,7},... | collective-permute-start | bytes 135176 | tf_op jit(solution)/shard_map/ppermute | solution.py:409
  131.7 7.9 %collective-permute-start.15 = (f32[16,88,128]{2,1,0:T(8,128)S(1)}, f32[16,88,128]{2,1,0:T(8,128)S(1)}, u32[]{:S(2)}, u32[]{:S(2)}) collective-permute-start(f32[16,88,128]{2,1,0:T(8,128)S(1)} %all_to_all.11.mine_ref), channel_id=1, source_target_pairs={{0,1},{1,0},{2,3},{3,2},{4,5},{5,4},{6,7},{7,6},{8,9},{9,8},{10,11... | collective-permute-start | bytes 2162696 | tf_op jit(solution)/shard_map/ppermute | solution.py:409

commit v2 on v1

v2 whole, which is shorter than its diff:
```python
import math

import jax
import jax.numpy as jnp
from jax import lax
from jax.experimental import pallas as pl
from jax.experimental.pallas import tpu as pltpu
from jax.sharding import Mesh, PartitionSpec as P

WIDTH = 256
HEADS = 8
SLICES = 64
HEAD = 32
CELLS = 1024
PAIRS = HEADS // 2
EPS = 1e-05
F32 = jnp.float32
BF16 = jnp.bfloat16
AXES = ("yl", "x", "yh", "z", "c")
PLANE = ("yl", "x", "yh")
SPACE = 32
Z_SCALE = 1.0 / math.sqrt(8 * 32768)
LATE, EARLY = 1536, 1280
LATE_HALF, EARLY_HALF = LATE // 2, EARLY // 2
LATE_PART, EARLY_PART = LATE_HALF // 16, EARLY_HALF // 16


def nn(a, b, precision=None):
    return lax.dot_general(
        a, b, (((1,), (0,)), ((), ())), precision=precision, preferred_element_type=F32
    )


def nt(a, b, precision=None):
    return lax.dot_general(
        a, b, (((1,), (1,)), ((), ())), precision=precision, preferred_element_type=F32
    )


def exact(f, a, b):
    return f(a, b, precision=lax.Precision.HIGHEST)


def turned(w):
    return w.astype(F32).T.astype(BF16)


def lane_half(rows):
    return lax.broadcasted_iota(jnp.int32, (rows, 128), 1) < SLICES


def diagonal_128():
    row = lax.broadcasted_iota(jnp.int32, (128, 128), 0) < SLICES
    lane = lax.broadcasted_iota(jnp.int32, (128, 128), 1) < SLICES
    return row == lane


def spread_pair(t):
    first = lane_half(HEAD)
    return jnp.concatenate([jnp.where(first, t, 0.0), jnp.where(first, 0.0, t)], axis=0)


def fold_pair(d):
    return jnp.where(lane_half(HEAD), d[:HEAD], d[HEAD:])


def slice_pair(w_slice):
    w = w_slice.astype(F32)
    return spread_pair(jnp.concatenate([w, w], axis=1))


def norm_stats(xt):
    mean = jnp.sum(xt, axis=0, keepdims=True) * (1.0 / WIDTH)
    centred = xt - mean
    inv = lax.rsqrt(jnp.sum(centred * centred, axis=0, keepdims=True) * (1.0 / WIDTH) + EPS)
    return mean, inv, centred * inv


def norm_back(g, xhat, inv, gain):
    ng = g * gain
    m1 = jnp.sum(ng, axis=0, keepdims=True) * (1.0 / WIDTH)
    m2 = jnp.sum(ng * xhat, axis=0, keepdims=True) * (1.0 / WIDTH)
    return inv * (ng - m1 - xhat * m2)


def lanes128(v):
    return sum(v[:, i : i + 128] for i in range(128, CELLS, 128)) + v[:, :128]


def live_row(count):
    return (lax.broadcasted_iota(jnp.int32, (1, CELLS), 1) < count).astype(F32)


def as_row(column128):
    return jnp.sum(column128.T, axis=0, keepdims=True)


def as_column(row):
    return jnp.broadcast_to(row, (128, row.shape[1])).T[:, 0:1]


def inverse_temper(temper_ref):
    return [1.0 / jnp.full((1, CELLS), temper_ref[h], F32) for h in range(HEADS)]


def fetch(sources, targets, sems):
    copies = [
        pltpu.make_async_copy(source, target, sems.at[i])
        for i, (source, target) in enumerate(zip(sources, targets))
    ]
    for copy in copies:
        copy.start()
    return copies


def front_kernel(
    count_ref, temper_hbm, cells_hbm, gain_hbm, bias_hbm, wfx_hbm, wx_hbm, wsl_hbm, gain2_hbm,
    bias2_hbm,
    pay_ref, feats_ref, mids_ref, weights_ref, stats_ref,
    temper_ref, cells_ref, gain_ref, bias_ref, wfx_ref, wx_ref, wsl_ref, gain2_ref, bias2_ref, sems,
):
    copies = fetch(
        (cells_hbm, wx_hbm, wsl_hbm, gain_hbm, bias_hbm, wfx_hbm, temper_hbm, gain2_hbm, bias2_hbm),
        (cells_ref, wx_ref, wsl_ref, gain_ref, bias_ref, wfx_ref, temper_ref, gain2_ref, bias2_ref),
        sems,
    )
    ones = jnp.ones((16, CELLS), BF16)
    for copy in copies:
        copy.wait()
    pair_t = slice_pair(wsl_ref[...]).T.astype(BF16)
    inv_t = inverse_temper(temper_ref)
    xt = cells_ref[...].astype(F32).T
    mean, inv, xhat = norm_stats(xt)
    n1 = (xhat * as_column(gain_ref[...]) + as_column(bias_ref[...])).astype(BF16)
    mids = nn(turned(wx_ref[...]), n1).astype(BF16)
    feats = nn(turned(wfx_ref[...]), n1).astype(BF16)
    mids_ref[...] = mids
    feats_ref[...] = feats
    live = live_row(count_ref[0, 0])
    stats_ref[14:15, :] = live
    stats_ref[0:1, :] = mean
    stats_ref[1:2, :] = inv
    for i, ref in enumerate((gain_ref, bias_ref, gain2_ref, bias2_ref)):
        stats_ref[10 + i : 11 + i, 0:WIDTH] = ref[...]
    for p in range(PAIRS):
        rows = slice(64 * p, 64 * p + 64)
        logits = nn(pair_t, mids[rows])
        halves = []
        for k in range(2):
            h = 2 * p + k
            l = logits[64 * k : 64 * k + 64] * inv_t[h]
            m = jnp.max(l, axis=0, keepdims=True)
            e = jnp.exp(l - m)
            s = jnp.sum(e, axis=0, keepdims=True)
            halves.append((e * (live / s)).astype(BF16))
            stats_ref[2 + h : 3 + h, :] = m + jnp.log(s)
        w = jnp.concatenate(halves, axis=0)
        weights_ref[128 * p : 128 * p + 128, :] = w
        d = nt(jnp.concatenate([feats[rows], ones], axis=0), w)
        pay_ref[0:32, 128 * p : 128 * p + 128] = fold_pair(d[:64])
        pay_ref[32:40, 128 * p : 128 * p + 128] = d[64:72]


def middle_kernel(
    core_ref, pay_ref, wq_ref, wk_ref, wv_ref, weights_ref, stats_ref, cells_ref, cot_ref, wout_ref,
    wup_ref, wdown_ref,
    tok_ref, gres_ref, gs_ref, keep_ref, send_ref, ln2_ref, mix_ref, xt_ref, layer_hbm,
    layer_ref, sems,
):
    core = core_ref[0]
    lifted = pay_ref[HEAD : HEAD + 1, :] + EPS
    tok = pay_ref[:HEAD, :] / lifted
    qt = exact(nn, wq_ref[...].T, tok)
    kt = exact(nn, wk_ref[...].T, tok)
    vt = exact(nn, wv_ref[...].T, tok)
    mix_ref[0:32, :] = tok
    mix_ref[32:64, :] = qt
    mix_ref[64:96, :] = kt
    mix_ref[96:128, :] = vt
    mix_ref[288:296, :] = jnp.broadcast_to(lifted, (8, 512))
    diagonal = diagonal_128()

    def give(at, grad):
        left = grad[:, :128] * Z_SCALE
        right = grad[:, 128:] * Z_SCALE
        keep_ref[at : at + 256, :] = jnp.where(core == 0, left, right)
        send_ref[at : at + 256, :] = jnp.where(core == 0, right, left)

    spread = []
    for p in range(PAIRS):
        lanes = slice(128 * p, 128 * p + 128)
        scores = exact(nn, kt[:, lanes].T, qt[:, lanes]) * (HEAD**-0.5)
        scores = jnp.where(diagonal, scores, -1e30)
        e = jnp.exp(scores - jnp.max(scores, axis=0, keepdims=True))
        e = jnp.where(diagonal, e, 0.0)
        attn = e / jnp.sum(e, axis=0, keepdims=True)
        mixed = exact(nn, vt[:, lanes], attn)
        mix_ref[128:256, lanes] = attn
        mixed = mixed.astype(BF16).astype(F32)
        mix_ref[256:288, lanes] = mixed
        spread.append(
            nn(spread_pair(mixed).astype(BF16), weights_ref[128 * p : 128 * p + 128, :])
        )
    xt = cells_ref[...].astype(F32).T
    xt_ref[...] = xt.astype(BF16)
    gain = as_column(stats_ref[12:13, 0:WIDTH])
    bias = as_column(stats_ref[13:14, 0:WIDTH])
    c0 = math.sqrt(2.0 / math.pi)
    gt = cot_ref[...].astype(F32).T.astype(BF16)
    g_act = nn(wdown_ref[...], gt)
    spread = jnp.concatenate(spread, axis=0).astype(BF16)
    resid = (xt + nn(turned(wout_ref[...]), spread)).astype(BF16)
    _, inv, xhat = norm_stats(resid.astype(F32))
    n2 = (xhat * gain + bias).astype(BF16)
    up = nn(turned(wup_ref[...]), n2)
    sq = up * up
    t = jnp.tanh(c0 * up * (1.0 + 0.044715 * sq))
    half = 0.5 * (1.0 + t)
    act = (up * half).astype(BF16)
    layer = resid.astype(F32) + nn(turned(wdown_ref[...]), act)
    layer_ref[...] = layer.T.astype(BF16)
    (leave,) = fetch((layer_ref,), (layer_hbm,), sems)
    give(512, nt(act, gt))
    slope = half + 0.5 * up * (1.0 - t * t) * (c0 * (1.0 + 3.0 * 0.044715 * sq))
    g_up = (slope * g_act).astype(BF16)
    give(256, nt(n2, g_up))
    g_n2 = nn(wup_ref[...], g_up)
    ln2_ref[0:1, :] = as_row(lanes128(g_n2 * xhat))
    ln2_ref[1:2, :] = as_row(lanes128(g_n2))
    gres = gt.astype(F32) + norm_back(g_n2, xhat, inv, gain)
    gres_ref[...] = gres
    gres_b = gres.astype(BF16)
    give(0, nt(spread, gres_b))
    gs = nn(wout_ref[...], gres_b).astype(BF16)
    gs_ref[...] = gs
    for p in range(PAIRS):
        d = nt(gs[64 * p : 64 * p + 64], weights_ref[128 * p : 128 * p + 128, :])
        tok_ref[:, 128 * p : 128 * p + 128] = fold_pair(d)
    leave.wait()


def rear_kernel(
    core_ref, temper_ref, grad_ref, mix_ref, wq_ref, wk_ref, wv_ref, feats_ref, mids_ref,
    gs_ref, weights_ref, xt_ref, stats_ref, gres_ref, ln2_ref, wfx_ref, wx_ref, wsl_ref,
    keep_ref, send_ref, out_ref,
):
    core = core_ref[0]
    lifted = mix_ref[288:289, :]
    tok = mix_ref[0:32, :]
    qt = mix_ref[32:64, :]
    kt = mix_ref[64:96, :]
    vt = mix_ref[96:128, :]
    dqs, dks, dvs = [], [], []
    for p in range(PAIRS):
        lanes = slice(128 * p, 128 * p + 128)
        gm = grad_ref[:, lanes]
        attn = mix_ref[128:256, lanes]
        da = exact(nn, vt[:, lanes].T, gm)
        dvs.append(exact(nt, gm, attn))
        pulled = attn * da
        ds = (pulled - attn * jnp.sum(pulled, axis=0, keepdims=True)) * (HEAD**-0.5)
        dqs.append(exact(nn, kt[:, lanes], ds))
        dks.append(exact(nt, qt[:, lanes], ds))
    dq = jnp.concatenate(dqs, axis=1)
    dk = jnp.concatenate(dks, axis=1)
    dv = jnp.concatenate(dvs, axis=1)
    dtok = exact(nn, wq_ref[...], dq) + exact(nn, wk_ref[...], dk) + exact(nn, wv_ref[...], dv)
    qkv = exact(nt, tok, jnp.concatenate([dq, dk, dv, jnp.zeros_like(dq)], axis=0))
    gnum = (dtok / lifted).astype(BF16).astype(F32)
    gden = -jnp.sum(dtok * tok, axis=0, keepdims=True) / lifted

    live = stats_ref[14:15, :]
    pair_t = slice_pair(wsl_ref[...]).T.astype(BF16)
    pair_b = slice_pair(wsl_ref[...]).astype(BF16)
    inv_t = inverse_temper(temper_ref)
    g_mids, g_feats, temps, slices = [], [], [], 0.0
    for p in range(PAIRS):
        lanes = slice(128 * p, 128 * p + 128)
        rows = slice(64 * p, 64 * p + 64)
        num = spread_pair(gnum[:, lanes])
        g_feats.append(nn(num.astype(BF16), weights_ref[lanes, :]))
        both = jnp.concatenate([spread_pair(mix_ref[256:288, lanes]), num], axis=0)
        gw = nn(
            both.T.astype(BF16), jnp.concatenate([gs_ref[rows, :], feats_ref[rows, :]], axis=0)
        )
        den = as_column(gden[:, lanes])
        logits = nn(pair_t, mids_ref[rows, :])
        scaled = []
        for k in range(2):
            h = 2 * p + k
            part = slice(64 * k, 64 * k + 64)
            l = logits[part] * inv_t[h]
            pr = jnp.exp(l - stats_ref[2 + h : 3 + h, :]) * live
            pulled = (gw[part] + den[part]) * pr
            gl = pulled - pr * jnp.sum(pulled, axis=0, keepdims=True)
            temps.append(jnp.sum(gl * l, axis=0, keepdims=True))
            scaled.append((gl * inv_t[h]).astype(BF16))
        scaled = jnp.concatenate(scaled, axis=0)
        g_mids.append(nn(pair_b, scaled))
        slices = slices + fold_pair(nt(mids_ref[rows, :], scaled))
    g_mids = jnp.concatenate(g_mids, axis=0).astype(BF16)
    g_feats = jnp.concatenate(g_feats, axis=0).astype(BF16)
    gain = as_column(stats_ref[10:11, 0:WIDTH])
    inv = stats_ref[1:2, :]
    xhat = (xt_ref[...].astype(F32) - stats_ref[0:1, :]) * inv
    n1 = (xhat * gain + as_column(stats_ref[11:12, 0:WIDTH])).astype(BF16)
    grad_fx = nt(n1, g_feats)
    grad_x = nt(n1, g_mids)
    g_n1 = nn(wfx_ref[...], g_feats) + nn(wx_ref[...], g_mids)
    slices = slices + pltpu.roll(slices, 64, 1)
    inv_col = jnp.concatenate([t[:, :128] for t in inv_t], axis=0)
    temps = jnp.sum(lanes128(jnp.concatenate(temps, axis=0)), axis=1, keepdims=True)
    temper = -jnp.broadcast_to(temps, (8, 128)) * inv_col
    rows = jnp.concatenate(
        [as_row(lanes128(g_n1 * xhat)), as_row(lanes128(g_n1)), ln2_ref[0:2, :],
         jnp.zeros((4, WIDTH), F32)],
        axis=0,
    )

    def give(at, left, right):
        left = left * Z_SCALE
        right = right * Z_SCALE
        keep_ref[at : at + left.shape[0], :] = jnp.where(core == 0, left, right)
        send_ref[at : at + left.shape[0], :] = jnp.where(core == 0, right, left)

    give(0, grad_fx[:, :128], grad_fx[:, 128:])
    give(256, grad_x[:, :128], grad_x[:, 128:])
    give(512, slices, qkv * (1.0 / SPACE))
    give(544, temper, jnp.zeros((8, 128), F32))
    give(552, rows[:, :128], rows[:, 128:])
    nothing = jnp.zeros((EARLY_HALF - 560, 128), F32)
    give(560, nothing, nothing)
    out_ref[...] = (gres_ref[...] + norm_back(g_n1, xhat, inv, gain)).T.astype(BF16)


def last_kernel(
    core_ref, mine_ref, theirs_ref,
    fx_ref, x_ref, out_ref, up_ref, down_ref, slice_ref, q_ref, k_ref, v_ref, temper_ref, gain1_ref, bias1_ref,
    gain2_ref, bias2_ref,
    whole_ref,
):
    core = core_ref[0]
    for part in range(16):
        mine = mine_ref[part]
        theirs = theirs_ref[part]
        left = jnp.where(core == 0, mine, theirs)
        right = jnp.where(core == 0, theirs, mine)
        both = jnp.concatenate([left, right], axis=1)
        whole_ref[part * LATE_PART : (part + 1) * LATE_PART, :] = both[:LATE_PART]
        at = LATE_HALF + part * EARLY_PART
        whole_ref[at : at + EARLY_PART, :] = both[LATE_PART:]
    out_ref[...] = whole_ref[0:256, :]
    up_ref[...] = whole_ref[256:512, :]
    down_ref[...] = whole_ref[512:768, :]
    fx_ref[...] = whole_ref[768:1024, :]
    x_ref[...] = whole_ref[1024:1280, :]
    slice_ref[...] = whole_ref[1280:1312, 0:64]
    qkv = whole_ref[1280:1312, 128:256]
    q_ref[...] = qkv[:, 0:32]
    k_ref[...] = qkv[:, 32:64]
    v_ref[...] = qkv[:, 64:96]
    temper_ref[...] = whole_ref[1312:1320, 0:128].T[0:1, :]
    gain1_ref[...] = whole_ref[1320:1321, :]
    bias1_ref[...] = whole_ref[1321:1322, :]
    gain2_ref[...] = whole_ref[1322:1323, :]
    bias2_ref[...] = whole_ref[1323:1324, :]


def permutation(move):
    pairs = []
    for yl in range(2):
        for x in range(4):
            for yh in range(2):
                for z in range(8):
                    for c in range(2):
                        place = lambda a, b, e, f, g: (((a * 4 + b) * 2 + e) * 8 + f) * 2 + g
                        pairs.append((place(yl, x, yh, z, c), place(*move(yl, x, yh, z, c))))
    return pairs


OTHER_CORE = permutation(lambda yl, x, yh, z, c: (yl, x, yh, z, 1 - c))
Z_ONE = permutation(lambda yl, x, yh, z, c: (yl, x, yh, z ^ 1, c))
Z_TWO = permutation(lambda yl, x, yh, z, c: (yl, x, yh, z ^ 2, c))
Z_FAR = permutation(lambda yl, x, yh, z, c: (yl, x, yh, 7 - z, c))
Y_FAR = permutation(lambda yl, x, yh, z, c: (yl, x, 1 - yh, z, c))


def swap(v, pairs):
    return lax.ppermute(v, AXES, pairs)


def space_sum(v):
    for pairs in (OTHER_CORE, Z_ONE, Z_TWO, Z_FAR, Y_FAR):
        v = v + swap(v, pairs)
    return v


VMEM = pl.BlockSpec(memory_space=pltpu.VMEM)
SMEM = pl.BlockSpec(memory_space=pltpu.SMEM)
HBM = pl.BlockSpec(memory_space=pltpu.HBM)
PARAMS = pltpu.CompilerParams(vmem_limit_bytes=16 * 1024 * 1024)


def call(kernel, name, outs, scalars, held, fetched=(), scratch=(), left=0, copies=0):
    near = len(outs) - left
    fetched = [pltpu.with_memory_space_constraint(a, pltpu.HBM) for a in fetched]
    return pl.pallas_call(
        kernel,
        name=name,
        out_shape=[jax.ShapeDtypeStruct(shape, dtype) for shape, dtype in outs],
        in_specs=[SMEM] * len(scalars) + [VMEM] * len(held) + [HBM] * len(fetched),
        out_specs=[VMEM] * near + [HBM] * left,
        scratch_shapes=list(scratch) + [pltpu.SemaphoreType.DMA((copies,))] * (copies > 0),
        compiler_params=PARAMS,
    )(*scalars, *held, *fetched)


def room(*arrays):
    return [pltpu.VMEM(a.shape, a.dtype) for a in arrays]


def body(
    cells, cotangent, cell_count, first_norm_gain, first_norm_bias, w_fx, w_x, w_slice, temper,
    query_weight, key_weight, value_weight, w_out, second_norm_gain, second_norm_bias, w_up, w_down,
):
    rows, cot = cells[0], cotangent[0]
    core = lax.axis_index("c").astype(jnp.int32).reshape(1)
    gain1, bias1 = first_norm_gain.reshape(1, WIDTH), first_norm_bias.reshape(1, WIDTH)
    gain2, bias2 = second_norm_gain.reshape(1, WIDTH), second_norm_bias.reshape(1, WIDTH)
    tall, tall_b = ((WIDTH, CELLS), F32), ((WIDTH, CELLS), BF16)
    square = ((WIDTH, WIDTH), F32)
    pay, feats, mids, weights, stats = call(
        front_kernel, "front",
        [((40, 512), F32), tall_b, tall_b, ((512, CELLS), BF16), ((16, CELLS), F32)],
        [cell_count], [], [temper, rows, gain1, bias1, w_fx, w_x, w_slice, gain2, bias2],
        [pltpu.SMEM((HEADS,), F32)]
        + room(rows, gain1, bias1, w_fx, w_x, w_slice, gain2, bias2), copies=9,
    )
    pay = space_sum(pay)
    tok, gres, gs, keep2, send2, ln2, mix, xt, layer = call(
        middle_kernel, "middle",
        [((HEAD, 512), F32), tall, tall_b, ((LATE_HALF, 128), F32), ((LATE_HALF, 128), F32),
         ((8, WIDTH), F32), ((296, 512), F32), tall_b, ((CELLS, WIDTH), BF16)],
        [core],
        [pay, query_weight, key_weight, value_weight, weights, stats, rows, cot, w_out, w_up, w_down],
        (), room(rows), left=1, copies=1,
    )
    tok = space_sum(tok)
    late = keep2 + swap(send2, OTHER_CORE)
    keep3, send3, out_rows = call(
        rear_kernel, "rear",
        [((EARLY_HALF, 128), F32), ((EARLY_HALF, 128), F32), ((CELLS, WIDTH), BF16)],
        [core, temper],
        [tok, mix, query_weight, key_weight, value_weight, feats, mids, gs, weights, xt, stats, gres,
         ln2, w_fx, w_x, w_slice],
    )
    early = keep3 + swap(send3, OTHER_CORE)
    both = jnp.concatenate(
        [late.reshape(16, LATE_PART, 128), early.reshape(16, EARLY_PART, 128)], axis=1
    )
    part = jnp.sum(lax.all_to_all(both, PLANE, 0, 0), axis=0)
    for pairs in (Z_ONE, Z_TWO, Z_FAR):
        part = part + swap(part, pairs)
    mine = lax.all_to_all(jnp.broadcast_to(part[None], both.shape), PLANE, 0, 0)
    theirs = swap(mine, OTHER_CORE)
    fx, gx, out, up, down, sl, q, k, v, temp, dg1, db1, dg2, db2 = call(
        last_kernel, "last",
        [square] * 5 + [((HEAD, SLICES), F32)] + [((HEAD, HEAD), F32)] * 3 + [((1, HEADS), F32)]
        + [((1, WIDTH), F32)] * 4,
        [core], [mine, theirs], (),
        [pltpu.VMEM((LATE_HALF + EARLY_HALF, WIDTH), F32)],
    )
    flat = lambda a: a.reshape(WIDTH)
    return (
        layer[None], out_rows[None], flat(dg1), flat(db1), fx, gx, sl, temp.reshape(HEADS), q, k, v, out,
        flat(dg2), flat(db2), up, down,
    )


def solution(mesh):
    fine = Mesh(mesh.devices.reshape(2, 4, 2, 8, 2), AXES)
    split = P(("yl", "x"), ("yh", "z", "c"), None)
    return jax.shard_map(
        body,
        mesh=fine,
        in_specs=(split, split, P(("yl", "x"), ("yh", "z", "c"))) + (P(),) * 14,
        out_specs=(split, split) + (P(),) * 14,
        check_vma=False,
    )
```

time: 142 us -> 129 us (0.908)
  Pallas kernels: 26.2 us -> 17.4 us
  local copies, waits for them, and re-layouts: 6.59 us -> 1.66 us
    pallas_call x4, Pallas kernels: 26.2 us -> 17.4 us  [call(): pl.pallas_call(kernel, name=name, out_shape=[jax.ShapeDtypeStruct(shape,...]
    unnamed x38 -> x24, local copies, waits for them, and re-layouts: 4.09 us -> 1.61 us
  transfers between devices with their start and end apart: 16 -> 16, of which waited for: 14 -> 14; matrix products, arithmetic and copies ran while one was open for 0% -> 0% of each run, Pallas kernels for 7% -> 5%
where the time goes in v2:
time: 129 us
  starting transfers between devices  39.9 us (31%)
  waiting for transfers between devices  33.8 us (26%)
  blocking collectives  33 us (26%)
  Pallas kernels  17.4 us (13%)
  between operations  1.67 us (1%)
  local copies, waits for them, and re-layouts  1.66 us (1%)
    ppermute x16, starting transfers between devices, swap(): return lax.ppermute(v, AXES, pairs)  39.9 us
    ppermute x16, waiting for transfers between devices, swap(): return lax.ppermute(v, AXES, pairs)  33.8 us
    all_to_all x1, blocking collectives, body(): part = jnp.sum(lax.all_to_all(both, PLANE, 0, 0), axis=0)  19.6 us
    pallas_call x4, Pallas kernels, call(): pl.pallas_call(kernel, name=name, out_shape=[jax.ShapeDtypeStruct(shape,...  17.4 us
    all_to_all x1, blocking collectives, body(): mine = lax.all_to_all(jnp.broadcast_to(part[None], both.shape), PLANE, 0, 0)  13.4 us
  transfers between devices with their start and end apart: 16, of which 14 were waited for; matrix products, arithmetic and copies ran while one was open for 0% of the time, Pallas kernels for 5%

profile of v2, /device:TPU:1, one launch (start us, length us, event | category | flops | bytes accessed | tf_op | source)
XLA Modules:
  0.0 128.7 jit_solution(18405361433324712656)
XLA Ops:
  1.3 0.0 copy-start.5
  1.3 3.2 %front.1 = (f32[40,512]{1,0:T(8,128)S(1)}, bf16[256,1024]{1,0:T(8,128)(2,1)S(1)}, bf16[256,1024]{1,0:T(8,128)(2,1)S(1)}, bf16[512,1024]{1,0:T(8,128)(2,1)S(1)}, f32[16,1024]{1,0:T(8,128)S(1)}) custom-call(s32[1,1]{1,0:T(1,128)S(6)} %copy.33.count_ref, f32[8]{0:T(128)} %temper_ref.1, bf16[1024,256]{1,0:T(8,128)(2,1)} %bitcast.16, f32[1,256]{1,0:T(1,128)} %bitcast.21, ...), custom_call_target="tpu_custom_call" | custom-call | tf_op jit(solution)/shard_map/front/pallas_call | solution.py:407
  4.5 3.3 %collective-permute-start = (f32[40,512]{1,0:T(8,128)S(1)}, f32[40,512]{1,0:T(8,128)S(1)}, u32[]{:S(2)}, u32[]{:S(2)}) collective-permute-start(f32[40,512]{1,0:T(8,128)S(1)} %get-tuple-element.47), channel_id=1, source_target_pairs={{0,1},{1,0},{2,3},{3,2},{4,5},{5,4},{6,7},{7,6},{8,9},{9,8},{10,11... | collective-permute-start | bytes 245768 | tf_op jit(solution)/shard_map/ppermute | solution.py:389
  7.8 0.9 collective-permute-done
  8.8 0.0 copy-start
  8.8 0.1 collective-permute-start.1
  8.9 3.7 %collective-permute-done.1 = f32[40,512]{1,0:T(8,128)S(1)} collective-permute-done((f32[40,512]{1,0:T(8,128)S(1)}, f32[40,512]{1,0:T(8,128)S(1)}, u32[]{:S(2)}, u32[]{:S(2)}) %collective-permute-start.1) | collective-permute-done | bytes 81952 | tf_op jit(solution)/shard_map/ppermute | solution.py:389
  12.6 1.7 %collective-permute-start.2 = (f32[40,512]{1,0:T(8,128)S(1)}, f32[40,512]{1,0:T(8,128)S(1)}, u32[]{:S(2)}, u32[]{:S(2)}) collective-permute-start(f32[40,512]{1,0:T(8,128)S(1)} %add.46), channel_id=1, source_target_pairs={{0,4},{1,5},{2,6},{3,7},{4,0},{5,1},{6,2},{7,3},{8,12},{9,13},{10,... | collective-permute-start | bytes 245768 | tf_op jit(solution)/shard_map/ppermute | solution.py:389
  14.3 4.7 %collective-permute-done.2 = f32[40,512]{1,0:T(8,128)S(1)} collective-permute-done((f32[40,512]{1,0:T(8,128)S(1)}, f32[40,512]{1,0:T(8,128)S(1)}, u32[]{:S(2)}, u32[]{:S(2)}) %collective-permute-start.2) | collective-permute-done | bytes 81952 | tf_op jit(solution)/shard_map/ppermute | solution.py:389
  19.0 3.0 %collective-permute-start.3 = (f32[40,512]{1,0:T(8,128)S(1)}, f32[40,512]{1,0:T(8,128)S(1)}, u32[]{:S(2)}, u32[]{:S(2)}) collective-permute-start(f32[40,512]{1,0:T(8,128)S(1)} %add.47), channel_id=1, source_target_pairs={{0,14},{1,15},{2,12},{3,13},{4,10},{5,11},{6,8},{7,9},{8,6},{9,7},... | collective-permute-start | bytes 245768 | tf_op jit(solution)/shard_map/ppermute | solution.py:389
  22.0 2.7 %collective-permute-done.3 = f32[40,512]{1,0:T(8,128)S(1)} collective-permute-done((f32[40,512]{1,0:T(8,128)S(1)}, f32[40,512]{1,0:T(8,128)S(1)}, u32[]{:S(2)}, u32[]{:S(2)}) %collective-permute-start.3) | collective-permute-done | bytes 81952 | tf_op jit(solution)/shard_map/ppermute | solution.py:389
  24.7 0.0 copy-start.4
  24.8 3.0 %collective-permute-start.4 = (f32[40,512]{1,0:T(8,128)S(1)}, f32[40,512]{1,0:T(8,128)}, u32[]{:S(2)}, u32[]{:S(2)}) collective-permute-start(f32[40,512]{1,0:T(8,128)S(1)} %add.48), channel_id=1, source_target_pairs={{0,16},{1,17},{2,18},{3,19},{4,20},{5,21},{6,22},{7,23},{8,24},{9,... | collective-permute-start | bytes 245768 | tf_op jit(solution)/shard_map/ppermute | solution.py:389
  27.8 2.0 %collective-permute-done.4 = f32[40,512]{1,0:T(8,128)} collective-permute-done((f32[40,512]{1,0:T(8,128)S(1)}, f32[40,512]{1,0:T(8,128)}, u32[]{:S(2)}, u32[]{:S(2)}) %collective-permute-start.4) | collective-permute-done | bytes 81952 | tf_op jit(solution)/shard_map/ppermute | solution.py:389
  29.7 0.9 add.49.pay_ref
  30.7 0.0 copy-start.6
  30.8 0.9 copy-done.6
  31.6 6.3 %middle.1 = (f32[32,512]{1,0:T(8,128)S(1)}, f32[256,1024]{1,0:T(8,128)S(1)}, bf16[256,1024]{1,0:T(8,128)(2,1)S(1)}, f32[768,128]{1,0:T(8,128)S(1)}, f32[768,128]...) custom-call(s32[1]{0:T(128)} %bitcast.core_ref, ...), custom_call_target="tpu_custom_call" | custom-call | tf_op jit(solution)/shard_map/middle/pallas_call | solution.py:407
  37.9 3.8 %collective-permute-start.5 = (f32[32,512]{1,0:T(8,128)S(1)}, f32[32,512]{1,0:T(8,128)S(1)}, u32[]{:S(2)}, u32[]{:S(2)}) collective-permute-start(f32[32,512]{1,0:T(8,128)S(1)} %get-tuple-element.51), channel_id=1, source_target_pairs={{0,1},{1,0},{2,3},{3,2},{4,5},{5,4},{6,7},{7,6},{8,9},{9,8},{10,11... | collective-permute-start | bytes 196616 | tf_op jit(solution)/shard_map/ppermute | solution.py:389
  41.7 0.9 collective-permute-done.5
  42.6 0.4 collective-permute-start.6
  43.1 2.8 %collective-permute-done.6 = f32[32,512]{1,0:T(8,128)S(1)} collective-permute-done((f32[32,512]{1,0:T(8,128)S(1)}, f32[32,512]{1,0:T(8,128)S(1)}, u32[]{:S(2)}, u32[]{:S(2)}) %collective-permute-start.6) | collective-permute-done | bytes 65568 | tf_op jit(solution)/shard_map/ppermute | solution.py:389
  45.9 1.2 collective-permute-start.7
  47.0 3.7 %collective-permute-done.7 = f32[32,512]{1,0:T(8,128)S(1)} collective-permute-done((f32[32,512]{1,0:T(8,128)S(1)}, f32[32,512]{1,0:T(8,128)S(1)}, u32[]{:S(2)}, u32[]{:S(2)}) %collective-permute-start.7) | collective-permute-done | bytes 65568 | tf_op jit(solution)/shard_map/ppermute | solution.py:389
  50.7 3.5 %collective-permute-start.8 = (f32[32,512]{1,0:T(8,128)S(1)}, f32[32,512]{1,0:T(8,128)S(1)}, u32[]{:S(2)}, u32[]{:S(2)}) collective-permute-start(f32[32,512]{1,0:T(8,128)S(1)} %add.52), channel_id=1, source_target_pairs={{0,14},{1,15},{2,12},{3,13},{4,10},{5,11},{6,8},{7,9},{8,6},{9,7},... | collective-permute-start | bytes 196616 | tf_op jit(solution)/shard_map/ppermute | solution.py:389
  54.1 2.3 %collective-permute-done.8 = f32[32,512]{1,0:T(8,128)S(1)} collective-permute-done((f32[32,512]{1,0:T(8,128)S(1)}, f32[32,512]{1,0:T(8,128)S(1)}, u32[]{:S(2)}, u32[]{:S(2)}) %collective-permute-start.8) | collective-permute-done | bytes 65568 | tf_op jit(solution)/shard_map/ppermute | solution.py:389
  56.5 0.0 copy-start.1
  56.5 3.0 %collective-permute-start.9 = (f32[32,512]{1,0:T(8,128)S(1)}, f32[32,512]{1,0:T(8,128)S(1)}, u32[]{:S(2)}, u32[]{:S(2)}) collective-permute-start(f32[32,512]{1,0:T(8,128)S(1)} %add.53), channel_id=1, source_target_pairs={{0,16},{1,17},{2,18},{3,19},{4,20},{5,21},{6,22},{7,23},{8,24},{9,... | collective-permute-start | bytes 196616 | tf_op jit(solution)/shard_map/ppermute | solution.py:389
  59.5 3.8 %collective-permute-start.10 = (f32[768,128]{1,0:T(8,128)S(1)}, f32[768,128]{1,0:T(8,128)S(1)}, u32[]{:S(2)}, u32[]{:S(2)}) collective-permute-start(f32[768,128]{1,0:T(8,128)S(1)} %get-tuple-element.61), channel_id=1, source_target_pairs={{0,1},{1,0},{2,3},{3,2},{4,5},{5,4},{6,7},{7,6},{8,9},{9,8},{10,11... | collective-permute-start | bytes 1179656 | tf_op jit(solution)/shard_map/ppermute | solution.py:389
  63.3 0.0 collective-permute-done.9
  63.3 0.0 copy-start.10
  63.3 0.0 copy-start.11
  63.4 0.7 copy-done.10
  64.0 6.8 %rear.1 = (f32[640,128]{1,0:T(8,128)S(1)}, f32[640,128]{1,0:T(8,128)S(1)}, bf16[1024,256]{1,0:T(8,128)(2,1)}) custom-call(s32[1]{0:T(128)} %bitcast.core_ref, f32[8]{0:T(128)S(1)} %copy-done.11, f32[32,512]{1,0:T(8,128)S(1)} %add.54.grad_ref, f32[296,512]{1,0:T(8,128)S(1)} %get-tuple-element.52.mix_ref, f32[32,32]{1,0:T(8,128)S(1)} %copy-done.7, ...), custom_call_target="tpu_custom_call" | custom-call | tf_op jit(solution)/shard_map/rear/pallas_call | solution.py:407
  70.9 2.6 %collective-permute-start.11 = (f32[640,128]{1,0:T(8,128)S(1)}, f32[640,128]{1,0:T(8,128)S(1)}, u32[]{:S(2)}, u32[]{:S(2)}) collective-permute-start(f32[640,128]{1,0:T(8,128)S(1)} %get-tuple-element.63), channel_id=1, source_target_pairs={{0,1},{1,0},{2,3},{3,2},{4,5},{5,4},{6,7},{7,6},{8,9},{9,8},{10,11... | collective-permute-start | bytes 983048 | tf_op jit(solution)/shard_map/ppermute | solution.py:389
  73.5 0.0 collective-permute-done.10
  73.5 1.2 collective-permute-done.11
  74.8 19.6 %all_to_all.10 = f32[16,88,128]{2,1,0:T(8,128)S(1)} all-to-all(f32[16,88,128]{2,1,0:T(8,128)S(1)} %pad_maximum_fusion), channel_id=1, replica_groups=mesh['yl'=2,'x'=4,'yh'=2,'z'=8,'c'=2] {'yl','x','yh'}, dimensions={0} | all-to-all | bytes 1441792 | tf_op jit(solution)/shard_map/all_to_all | solution.py:461
  94.5 0.6 collective-permute-start.12
  95.1 2.3 %collective-permute-done.12 = f32[88,128]{1,0:T(8,128)S(1)} collective-permute-done((f32[88,128]{1,0:T(8,128)S(1)}, f32[88,128]{1,0:T(8,128)S(1)}, u32[]{:S(2)}, u32[]{:S(2)}) %collective-permute-start.12) | collective-permute-done | bytes 45088 | tf_op jit(solution)/shard_map/ppermute | solution.py:389
  97.5 1.3 %collective-permute-start.13 = (f32[88,128]{1,0:T(8,128)S(1)}, f32[88,128]{1,0:T(8,128)S(1)}, u32[]{:S(2)}, u32[]{:S(2)}) collective-permute-start(f32[88,128]{1,0:T(8,128)S(1)} %add.57), channel_id=1, source_target_pairs={{0,4},{1,5},{2,6},{3,7},{4,0},{5,1},{6,2},{7,3},{8,12},{9,13},{10,... | collective-permute-start | bytes 135176 | tf_op jit(solution)/shard_map/ppermute | solution.py:389
  98.8 3.0 %collective-permute-done.13 = f32[88,128]{1,0:T(8,128)S(1)} collective-permute-done((f32[88,128]{1,0:T(8,128)S(1)}, f32[88,128]{1,0:T(8,128)S(1)}, u32[]{:S(2)}, u32[]{:S(2)}) %collective-permute-start.13) | collective-permute-done | bytes 45088 | tf_op jit(solution)/shard_map/ppermute | solution.py:389
  101.8 2.5 %collective-permute-start.14 = (f32[88,128]{1,0:T(8,128)S(1)}, f32[88,128]{1,0:T(8,128)S(1)}, u32[]{:S(2)}, u32[]{:S(2)}) collective-permute-start(f32[88,128]{1,0:T(8,128)S(1)} %add.58), channel_id=1, source_target_pairs={{0,14},{1,15},{2,12},{3,13},{4,10},{5,11},{6,8},{7,9},{8,6},{9,7},... | collective-permute-start | bytes 135176 | tf_op jit(solution)/shard_map/ppermute | solution.py:389
  104.3 1.7 %collective-permute-done.14 = f32[88,128]{1,0:T(8,128)S(1)} collective-permute-done((f32[88,128]{1,0:T(8,128)S(1)}, f32[88,128]{1,0:T(8,128)S(1)}, u32[]{:S(2)}, u32[]{:S(2)}) %collective-permute-start.14) | collective-permute-done | bytes 45088 | tf_op jit(solution)/shard_map/ppermute | solution.py:389
  106.1 13.4 %all_to_all.11.mine_ref = f32[16,88,128]{2,1,0:T(8,128)S(1)} all-to-all(f32[16,88,128]{2,1,0:T(8,128)S(1)} %broadcast_in_dim.14), channel_id=1, replica_groups=mesh['yl'=2,'x'=4,'yh'=2,'z'=8,'c'=2] {'yl','x','yh'}, dimensions={0} | all-to-all | bytes 1441792 | tf_op jit(solution)/shard_map/all_to_all | solution.py:464
  119.5 6.1 %collective-permute-start.15 = (f32[16,88,128]{2,1,0:T(8,128)S(1)}, f32[16,88,128]{2,1,0:T(8,128)S(1)}, u32[]{:S(2)}, u32[]{:S(2)}) collective-permute-start(f32[16,88,128]{2,1,0:T(8,128)S(1)} %all_to_all.11.mine_ref), channel_id=1, source_target_pairs={{0,1},{1,0},{2,3},{3,2},{4,5},{5,4},{6,7},{7,6},{8,9},{9,8},{10,11... | collective-permute-start | bytes 2162696 | tf_op jit(solution)/shard_map/ppermute | solution.py:389
  125.6 1.8 %collective-permute-done.15.theirs_ref = f32[16,88,128]{2,1,0:T(8,128)S(1)} collective-permute-done((f32[16,88,128]{2,1,0:T(8,128)S(1)}, f32[16,88,128]{2,1,0:T(8,128)S(1)}, u32[]{:S(2)}, u32[]{:S(2)}) %collective-permute-start.15) | collective-permute-done | bytes 720928 | tf_op jit(solution)/shard_map/ppermute | solution.py:389
  127.4 1.1 last.1
  (32 shorter events, 0.4 us)
Async XLA Ops:
  1.3 29.4 %copy-start.5 = (bf16[256,256]{1,0:T(8,128)(2,1)S(1)}, bf16[256,256]{1,0:T(8,128)(2,1)}, u32[]{:S(2)}) copy-start(bf16[256,256]{1,0:T(8,128)(2,1)} %wup_ref.1) | copy-start | bytes 393220
  4.5 4.3 %collective-permute-start = (f32[40,512]{1,0:T(8,128)S(1)}, f32[40,512]{1,0:T(8,128)S(1)}, u32[]{:S(2)}, u32[]{:S(2)}) collective-permute-start(f32[40,512]{1,0:T(8,128)S(1)} %get-tuple-element.47), channel_id=1, source_target_pairs={{0,1},{1,0},{2,3},{3,2},{4,5},{5,4},{6,7},{7,6},{8,9},{9,8},{10,11... | collective-permute-start | bytes 245768 | tf_op jit(solution)/shard_map/ppermute | solution.py:389
  8.8 21.9 %copy-start.3 = (bf16[1,1024,256]{2,1,0:T(8,128)(2,1)S(1)}, bf16[1,1024,256]{2,1,0:T(8,128)(2,1)}, u32[]{:S(2)}) copy-start(bf16[1,1024,256]{2,1,0:T(8,128)(2,1)} %param.18) | copy-start | bytes 1572868
  8.8 21.9 %copy-start = (bf16[1,1024,256]{2,1,0:T(8,128)(2,1)S(1)}, bf16[1,1024,256]{2,1,0:T(8,128)(2,1)}, u32[]{:S(2)}) copy-start(bf16[1,1024,256]{2,1,0:T(8,128)(2,1)} %param.17) | copy-start | bytes 1572868
  8.8 3.8 %collective-permute-start.1 = (f32[40,512]{1,0:T(8,128)S(1)}, f32[40,512]{1,0:T(8,128)S(1)}, u32[]{:S(2)}, u32[]{:S(2)}) collective-permute-start(f32[40,512]{1,0:T(8,128)S(1)} %add.45), channel_id=1, source_target_pairs={{0,2},{1,3},{2,0},{3,1},{4,6},{5,7},{6,4},{7,5},{8,10},{9,11},{10,... | collective-permute-start | bytes 245768 | tf_op jit(solution)/shard_map/ppermute | solution.py:389
  12.6 6.4 %collective-permute-start.2 = (f32[40,512]{1,0:T(8,128)S(1)}, f32[40,512]{1,0:T(8,128)S(1)}, u32[]{:S(2)}, u32[]{:S(2)}) collective-permute-start(f32[40,512]{1,0:T(8,128)S(1)} %add.46), channel_id=1, source_target_pairs={{0,4},{1,5},{2,6},{3,7},{4,0},{5,1},{6,2},{7,3},{8,12},{9,13},{10,... | collective-permute-start | bytes 245768 | tf_op jit(solution)/shard_map/ppermute | solution.py:389
  19.0 5.7 %collective-permute-start.3 = (f32[40,512]{1,0:T(8,128)S(1)}, f32[40,512]{1,0:T(8,128)S(1)}, u32[]{:S(2)}, u32[]{:S(2)}) collective-permute-start(f32[40,512]{1,0:T(8,128)S(1)} %add.47), channel_id=1, source_target_pairs={{0,14},{1,15},{2,12},{3,13},{4,10},{5,11},{6,8},{7,9},{8,6},{9,7},... | collective-permute-start | bytes 245768 | tf_op jit(solution)/shard_map/ppermute | solution.py:389
  24.7 6.0 %copy-start.4 = (bf16[256,256]{1,0:T(8,128)(2,1)S(1)}, bf16[256,256]{1,0:T(8,128)(2,1)}, u32[]{:S(2)}) copy-start(bf16[256,256]{1,0:T(8,128)(2,1)} %wout_ref.1) | copy-start | bytes 393220
  24.8 5.0 %collective-permute-start.4 = (f32[40,512]{1,0:T(8,128)S(1)}, f32[40,512]{1,0:T(8,128)}, u32[]{:S(2)}, u32[]{:S(2)}) collective-permute-start(f32[40,512]{1,0:T(8,128)S(1)} %add.48), channel_id=1, source_target_pairs={{0,16},{1,17},{2,18},{3,19},{4,20},{5,21},{6,22},{7,23},{8,24},{9,... | collective-permute-start | bytes 245768 | tf_op jit(solution)/shard_map/ppermute | solution.py:389
  29.7 1.0 copy-start.7
  29.7 1.0 copy-start.8
  29.7 1.0 copy-start.9
  30.7 0.9 copy-start.6
  37.9 4.7 %collective-permute-start.5 = (f32[32,512]{1,0:T(8,128)S(1)}, f32[32,512]{1,0:T(8,128)S(1)}, u32[]{:S(2)}, u32[]{:S(2)}) collective-permute-start(f32[32,512]{1,0:T(8,128)S(1)} %get-tuple-element.51), channel_id=1, source_target_pairs={{0,1},{1,0},{2,3},{3,2},{4,5},{5,4},{6,7},{7,6},{8,9},{9,8},{10,11... | collective-permute-start | bytes 196616 | tf_op jit(solution)/shard_map/ppermute | solution.py:389
  42.6 3.2 %collective-permute-start.6 = (f32[32,512]{1,0:T(8,128)S(1)}, f32[32,512]{1,0:T(8,128)S(1)}, u32[]{:S(2)}, u32[]{:S(2)}) collective-permute-start(f32[32,512]{1,0:T(8,128)S(1)} %add.50), channel_id=1, source_target_pairs={{0,2},{1,3},{2,0},{3,1},{4,6},{5,7},{6,4},{7,5},{8,10},{9,11},{10,... | collective-permute-start | bytes 196616 | tf_op jit(solution)/shard_map/ppermute | solution.py:389
  45.9 4.8 %collective-permute-start.7 = (f32[32,512]{1,0:T(8,128)S(1)}, f32[32,512]{1,0:T(8,128)S(1)}, u32[]{:S(2)}, u32[]{:S(2)}) collective-permute-start(f32[32,512]{1,0:T(8,128)S(1)} %add.51), channel_id=1, source_target_pairs={{0,4},{1,5},{2,6},{3,7},{4,0},{5,1},{6,2},{7,3},{8,12},{9,13},{10,... | collective-permute-start | bytes 196616 | tf_op jit(solution)/shard_map/ppermute | solution.py:389
  50.7 5.8 %collective-permute-start.8 = (f32[32,512]{1,0:T(8,128)S(1)}, f32[32,512]{1,0:T(8,128)S(1)}, u32[]{:S(2)}, u32[]{:S(2)}) collective-permute-start(f32[32,512]{1,0:T(8,128)S(1)} %add.52), channel_id=1, source_target_pairs={{0,14},{1,15},{2,12},{3,13},{4,10},{5,11},{6,8},{7,9},{8,6},{9,7},... | collective-permute-start | bytes 196616 | tf_op jit(solution)/shard_map/ppermute | solution.py:389
  56.5 6.9 %copy-start.2 = (bf16[256,256]{1,0:T(8,128)(2,1)S(1)}, bf16[256,256]{1,0:T(8,128)(2,1)}, u32[]{:S(2)}) copy-start(bf16[256,256]{1,0:T(8,128)(2,1)} %wx_ref.1) | copy-start | bytes 393220
  56.5 6.9 %copy-start.1 = (bf16[256,256]{1,0:T(8,128)(2,1)S(1)}, bf16[256,256]{1,0:T(8,128)(2,1)}, u32[]{:S(2)}) copy-start(bf16[256,256]{1,0:T(8,128)(2,1)} %wfx_ref.1) | copy-start | bytes 393220
  56.5 6.8 %collective-permute-start.9 = (f32[32,512]{1,0:T(8,128)S(1)}, f32[32,512]{1,0:T(8,128)S(1)}, u32[]{:S(2)}, u32[]{:S(2)}) collective-permute-start(f32[32,512]{1,0:T(8,128)S(1)} %add.53), channel_id=1, source_target_pairs={{0,16},{1,17},{2,18},{3,19},{4,20},{5,21},{6,22},{7,23},{8,24},{9,... | collective-permute-start | bytes 196616 | tf_op jit(solution)/shard_map/ppermute | solution.py:389
  59.5 14.0 %collective-permute-start.10 = (f32[768,128]{1,0:T(8,128)S(1)}, f32[768,128]{1,0:T(8,128)S(1)}, u32[]{:S(2)}, u32[]{:S(2)}) collective-permute-start(f32[768,128]{1,0:T(8,128)S(1)} %get-tuple-element.61), channel_id=1, source_target_pairs={{0,1},{1,0},{2,3},{3,2},{4,5},{5,4},{6,7},{7,6},{8,9},{9,8},{10,11... | collective-permute-start | bytes 1179656 | tf_op jit(solution)/shard_map/ppermute | solution.py:389
  63.3 0.7 copy-start.10
  63.3 0.7 copy-start.11
  70.9 3.8 %collective-permute-start.11 = (f32[640,128]{1,0:T(8,128)S(1)}, f32[640,128]{1,0:T(8,128)S(1)}, u32[]{:S(2)}, u32[]{:S(2)}) collective-permute-start(f32[640,128]{1,0:T(8,128)S(1)} %get-tuple-element.63), channel_id=1, source_target_pairs={{0,1},{1,0},{2,3},{3,2},{4,5},{5,4},{6,7},{7,6},{8,9},{9,8},{10,11... | collective-permute-start | bytes 983048 | tf_op jit(solution)/shard_map/ppermute | solution.py:389
  94.5 3.0 %collective-permute-start.12 = (f32[88,128]{1,0:T(8,128)S(1)}, f32[88,128]{1,0:T(8,128)S(1)}, u32[]{:S(2)}, u32[]{:S(2)}) collective-permute-start(f32[88,128]{1,0:T(8,128)S(1)} %reduce_sum.9), channel_id=1, source_target_pairs={{0,2},{1,3},{2,0},{3,1},{4,6},{5,7},{6,4},{7,5},{8,10},{9,11},{10,... | collective-permute-start | bytes 135176 | tf_op jit(solution)/shard_map/ppermute | solution.py:389
  97.5 4.4 %collective-permute-start.13 = (f32[88,128]{1,0:T(8,128)S(1)}, f32[88,128]{1,0:T(8,128)S(1)}, u32[]{:S(2)}, u32[]{:S(2)}) collective-permute-start(f32[88,128]{1,0:T(8,128)S(1)} %add.57), channel_id=1, source_target_pairs={{0,4},{1,5},{2,6},{3,7},{4,0},{5,1},{6,2},{7,3},{8,12},{9,13},{10,... | collective-permute-start | bytes 135176 | tf_op jit(solution)/shard_map/ppermute | solution.py:389
  101.8 4.2 %collective-permute-start.14 = (f32[88,128]{1,0:T(8,128)S(1)}, f32[88,128]{1,0:T(8,128)S(1)}, u32[]{:S(2)}, u32[]{:S(2)}) collective-permute-start(f32[88,128]{1,0:T(8,128)S(1)} %add.58), channel_id=1, source_target_pairs={{0,14},{1,15},{2,12},{3,13},{4,10},{5,11},{6,8},{7,9},{8,6},{9,7},... | collective-permute-start | bytes 135176 | tf_op jit(solution)/shard_map/ppermute | solution.py:389
  119.5 7.9 %collective-permute-start.15 = (f32[16,88,128]{2,1,0:T(8,128)S(1)}, f32[16,88,128]{2,1,0:T(8,128)S(1)}, u32[]{:S(2)}, u32[]{:S(2)}) collective-permute-start(f32[16,88,128]{2,1,0:T(8,128)S(1)} %all_to_all.11.mine_ref), channel_id=1, source_target_pairs={{0,1},{1,0},{2,3},{3,2},{4,5},{5,4},{6,7},{7,6},{8,9},{9,8},{10,11... | collective-permute-start | bytes 2162696 | tf_op jit(solution)/shard_map/ppermute | solution.py:389

commit v3 on v2

--- a/solution.py
+++ b/solution.py
@@ -38,7 +38,7 @@
 
 
 def exact(f, a, b):
-    return f(a, b, precision=lax.Precision.HIGHEST)
+    return f(a, b, precision=lax.Precision.HIGH)
 
 
 def turned(w):
@@ -115,20 +115,28 @@
 
 def front_kernel(
     count_ref, temper_hbm, cells_hbm, gain_hbm, bias_hbm, wfx_hbm, wx_hbm, wsl_hbm, gain2_hbm,
-    bias2_hbm,
+    bias2_hbm, wq_hbm, wk_hbm, wv_hbm,
     pay_ref, feats_ref, mids_ref, weights_ref, stats_ref,
-    temper_ref, cells_ref, gain_ref, bias_ref, wfx_ref, wx_ref, wsl_ref, gain2_ref, bias2_ref, sems,
+    temper_ref, cells_ref, gain_ref, bias_ref, wfx_ref, wx_ref, wsl_ref, gain2_ref, bias2_ref,
+    wq_ref, wk_ref, wv_ref, sems,
 ):
     copies = fetch(
-        (cells_hbm, wx_hbm, wsl_hbm, gain_hbm, bias_hbm, wfx_hbm, temper_hbm, gain2_hbm, bias2_hbm),
-        (cells_ref, wx_ref, wsl_ref, gain_ref, bias_ref, wfx_ref, temper_ref, gain2_ref, bias2_ref),
+        (cells_hbm, wx_hbm, wsl_hbm, gain_hbm, bias_hbm, wfx_hbm, temper_hbm, gain2_hbm, bias2_hbm,
+         wq_hbm, wk_hbm, wv_hbm),
+        (cells_ref, wx_ref, wsl_ref, gain_ref, bias_ref, wfx_ref, temper_ref, gain2_ref, bias2_ref,
+         wq_ref, wk_ref, wv_ref),
         sems,
     )
     ones = jnp.ones((16, CELLS), BF16)
     for copy in copies:
         copy.wait()
-    pair_t = slice_pair(wsl_ref[...]).T.astype(BF16)
+    pair = slice_pair(wsl_ref[...])
+    for i in range(8):
+        stats_ref[24:32, 128 * i : 128 * i + 128] = pair[8 * i : 8 * i + 8]
+    pair_t = pair.T.astype(BF16)
     inv_t = inverse_temper(temper_ref)
+    for h in range(HEADS):
+        stats_ref[16 + h : 17 + h, :] = inv_t[h]
     xt = cells_ref[...].astype(F32).T
     mean, inv, xhat = norm_stats(xt)
     n1 = (xhat * as_column(gain_ref[...]) + as_column(bias_ref[...])).astype(BF16)
@@ -142,6 +150,9 @@
     stats_ref[1:2, :] = inv
     for i, ref in enumerate((gain_ref, bias_ref, gain2_ref, bias2_ref)):
         stats_ref[10 + i : 11 + i, 0:WIDTH] = ref[...]
+    stats_ref[32:64, 0:128] = jnp.concatenate(
+        [wq_ref[...], wk_ref[...], wv_ref[...], jnp.zeros((HEAD, HEAD), F32)], axis=1
+    )
     for p in range(PAIRS):
         rows = slice(64 * p, 64 * p + 64)
         logits = nn(pair_t, mids[rows])
@@ -157,22 +168,40 @@
         w = jnp.concatenate(halves, axis=0)
         weights_ref[128 * p : 128 * p + 128, :] = w
         d = nt(jnp.concatenate([feats[rows], ones], axis=0), w)
-        pay_ref[0:32, 128 * p : 128 * p + 128] = fold_pair(d[:64])
-        pay_ref[32:40, 128 * p : 128 * p + 128] = d[64:72]
+        pay_ref[32 * p : 32 * p + 32, :] = fold_pair(d[:64])
+        pay_ref[128 + p : 129 + p, :] = d[64:65]
+    pay_ref[132:136, :] = jnp.zeros((4, 128), F32)
+
+
+def keep_kernel(wout_hbm, wup_hbm, wdown_hbm, cells_hbm, cot_hbm, near_ref, sems):
+    sources = (wout_hbm, wup_hbm, wdown_hbm, cells_hbm, cot_hbm)
+    places = ((0, 256), (256, 256), (512, 256), (768, CELLS), (1792, CELLS))
+    targets = [near_ref.at[pl.ds(start, size), :] for start, size in places]
+    for copy in fetch(sources, targets, sems):
+        copy.wait()
 
 
 def middle_kernel(
-    core_ref, pay_ref, wq_ref, wk_ref, wv_ref, weights_ref, stats_ref, cells_ref, cot_ref, wout_ref,
-    wup_ref, wdown_ref,
+    core_ref, mine_ref, theirs_ref, weights_ref, stats_ref, near_ref,
     tok_ref, gres_ref, gs_ref, keep_ref, send_ref, ln2_ref, mix_ref, xt_ref, layer_hbm,
-    layer_ref, sems,
+    layer_ref, pay_ref, sems,
 ):
+    wout_ref = near_ref.at[0:256, :]
+    wup_ref = near_ref.at[256:512, :]
+    wdown_ref = near_ref.at[512:768, :]
+    cells_ref = near_ref.at[768:1792, :]
+    cot_ref = near_ref.at[1792:2816, :]
+    maps = stats_ref[32:64, 0:128]
+    wq, wk, wv = maps[:, 0:32], maps[:, 32:64], maps[:, 64:96]
+    pay_ref[...] = mine_ref[...] + theirs_ref[...]
+    gt = cot_ref[...].astype(F32).T.astype(BF16)
+    g_act = nn(wdown_ref[...], gt)
     core = core_ref[0]
-    lifted = pay_ref[HEAD : HEAD + 1, :] + EPS
-    tok = pay_ref[:HEAD, :] / lifted
-    qt = exact(nn, wq_ref[...].T, tok)
-    kt = exact(nn, wk_ref[...].T, tok)
-    vt = exact(nn, wv_ref[...].T, tok)
+    lifted = jnp.concatenate([pay_ref[128 + p : 129 + p, :] for p in range(PAIRS)], axis=1) + EPS
+    tok = jnp.concatenate([pay_ref[32 * p : 32 * p + 32, :] for p in range(PAIRS)], axis=1) / lifted
+    qt = exact(nn, wq.T, tok)
+    kt = exact(nn, wk.T, tok)
+    vt = exact(nn, wv.T, tok)
     mix_ref[0:32, :] = tok
     mix_ref[32:64, :] = qt
     mix_ref[64:96, :] = kt
@@ -206,8 +235,6 @@
     gain = as_column(stats_ref[12:13, 0:WIDTH])
     bias = as_column(stats_ref[13:14, 0:WIDTH])
     c0 = math.sqrt(2.0 / math.pi)
-    gt = cot_ref[...].astype(F32).T.astype(BF16)
-    g_act = nn(wdown_ref[...], gt)
     spread = jnp.concatenate(spread, axis=0).astype(BF16)
     resid = (xt + nn(turned(wout_ref[...]), spread)).astype(BF16)
     _, inv, xhat = norm_stats(resid.astype(F32))
@@ -240,9 +267,10 @@
 
 
 def rear_kernel(
-    core_ref, temper_ref, grad_ref, mix_ref, wq_ref, wk_ref, wv_ref, feats_ref, mids_ref,
-    gs_ref, weights_ref, xt_ref, stats_ref, gres_ref, ln2_ref, wfx_ref, wx_ref, wsl_ref,
-    keep_ref, send_ref, out_ref,
+    core_ref, mine_ref, theirs_ref, mix_ref, feats_ref, mids_ref,
+    gs_ref, weights_ref, xt_ref, stats_ref, ln2_ref,
+    wfx_ref, wx_ref,
+    keep_ref, send_ref, g_n1_ref,
 ):
     core = core_ref[0]
     lifted = mix_ref[288:289, :]
@@ -253,7 +281,7 @@
     dqs, dks, dvs = [], [], []
     for p in range(PAIRS):
         lanes = slice(128 * p, 128 * p + 128)
-        gm = grad_ref[:, lanes]
+        gm = mine_ref[:, lanes] + theirs_ref[:, lanes]
         attn = mix_ref[128:256, lanes]
         da = exact(nn, vt[:, lanes].T, gm)
         dvs.append(exact(nt, gm, attn))
@@ -264,15 +292,21 @@
     dq = jnp.concatenate(dqs, axis=1)
     dk = jnp.concatenate(dks, axis=1)
     dv = jnp.concatenate(dvs, axis=1)
-    dtok = exact(nn, wq_ref[...], dq) + exact(nn, wk_ref[...], dk) + exact(nn, wv_ref[...], dv)
+    maps = stats_ref[32:64, 0:128]
+    dtok = (
+        exact(nn, maps[:, 0:32], dq) + exact(nn, maps[:, 32:64], dk) + exact(nn, maps[:, 64:96], dv)
+    )
     qkv = exact(nt, tok, jnp.concatenate([dq, dk, dv, jnp.zeros_like(dq)], axis=0))
     gnum = (dtok / lifted).astype(BF16).astype(F32)
     gden = -jnp.sum(dtok * tok, axis=0, keepdims=True) / lifted
 
     live = stats_ref[14:15, :]
-    pair_t = slice_pair(wsl_ref[...]).T.astype(BF16)
-    pair_b = slice_pair(wsl_ref[...]).astype(BF16)
-    inv_t = inverse_temper(temper_ref)
+    pair = jnp.concatenate(
+        [stats_ref[24:32, 128 * i : 128 * i + 128] for i in range(8)], axis=0
+    )
+    pair_b = pair.astype(BF16)
+    pair_t = pair.T.astype(BF16)
+    inv_t = [stats_ref[16 + h : 17 + h, :] for h in range(HEADS)]
     g_mids, g_feats, temps, slices = [], [], [], 0.0
     for p in range(PAIRS):
         lanes = slice(128 * p, 128 * p + 128)
@@ -307,6 +341,7 @@
     grad_fx = nt(n1, g_feats)
     grad_x = nt(n1, g_mids)
     g_n1 = nn(wfx_ref[...], g_feats) + nn(wx_ref[...], g_mids)
+    g_n1_ref[...] = g_n1
     slices = slices + pltpu.roll(slices, 64, 1)
     inv_col = jnp.concatenate([t[:, :128] for t in inv_t], axis=0)
     temps = jnp.sum(lanes128(jnp.concatenate(temps, axis=0)), axis=1, keepdims=True)
@@ -330,7 +365,13 @@
     give(552, rows[:, :128], rows[:, 128:])
     nothing = jnp.zeros((EARLY_HALF - 560, 128), F32)
     give(560, nothing, nothing)
-    out_ref[...] = (gres_ref[...] + norm_back(g_n1, xhat, inv, gain)).T.astype(BF16)
+
+
+def cells_kernel(g_n1_ref, xt_ref, gres_ref, stats_ref, out_ref):
+    inv = stats_ref[1:2, :]
+    xhat = (xt_ref[...].astype(F32) - stats_ref[0:1, :]) * inv
+    gain = as_column(stats_ref[10:11, 0:WIDTH])
+    out_ref[...] = (gres_ref[...] + norm_back(g_n1_ref[...], xhat, inv, gain)).T.astype(BF16)
 
 
 def last_kernel(
@@ -389,8 +430,8 @@
     return lax.ppermute(v, AXES, pairs)
 
 
-def space_sum(v):
-    for pairs in (OTHER_CORE, Z_ONE, Z_TWO, Z_FAR, Y_FAR):
+def near_sum(v):
+    for pairs in (OTHER_CORE, Z_ONE, Z_TWO, Z_FAR):
         v = v + swap(v, pairs)
     return v
 
@@ -431,30 +472,44 @@
     square = ((WIDTH, WIDTH), F32)
     pay, feats, mids, weights, stats = call(
         front_kernel, "front",
-        [((40, 512), F32), tall_b, tall_b, ((512, CELLS), BF16), ((16, CELLS), F32)],
-        [cell_count], [], [temper, rows, gain1, bias1, w_fx, w_x, w_slice, gain2, bias2],
+        [((136, 128), F32), tall_b, tall_b, ((512, CELLS), BF16), ((64, CELLS), F32)],
+        [cell_count], [], [temper, rows, gain1, bias1, w_fx, w_x, w_slice, gain2, bias2,
+         query_weight, key_weight, value_weight],
         [pltpu.SMEM((HEADS,), F32)]
-        + room(rows, gain1, bias1, w_fx, w_x, w_slice, gain2, bias2), copies=9,
-    )
-    pay = space_sum(pay)
+        + room(rows, gain1, bias1, w_fx, w_x, w_slice, gain2, bias2, query_weight, key_weight,
+               value_weight),
+        copies=12,
+    )
+    for pairs in (OTHER_CORE, Z_ONE):
+        pay = pay + swap(pay, pairs)
+    (near,) = call(
+        keep_kernel, "keep", [((2816, WIDTH), BF16)], [], [], [w_out, w_up, w_down, rows, cot], copies=5
+    )
+    got, near = lax.optimization_barrier((swap(pay, Z_TWO), near))
+    pay = pay + got
+    pay = pay + swap(pay, Z_FAR)
     tok, gres, gs, keep2, send2, ln2, mix, xt, layer = call(
         middle_kernel, "middle",
         [((HEAD, 512), F32), tall, tall_b, ((LATE_HALF, 128), F32), ((LATE_HALF, 128), F32),
          ((8, WIDTH), F32), ((296, 512), F32), tall_b, ((CELLS, WIDTH), BF16)],
         [core],
-        [pay, query_weight, key_weight, value_weight, weights, stats, rows, cot, w_out, w_up, w_down],
-        (), room(rows), left=1, copies=1,
-    )
-    tok = space_sum(tok)
+        [pay, swap(pay, Y_FAR), weights, stats, near],
+        (), room(rows) + [pltpu.VMEM((136, 128), F32)], left=1, copies=1,
+    )
+    tok = near_sum(tok)
     late = keep2 + swap(send2, OTHER_CORE)
-    keep3, send3, out_rows = call(
+    keep3, send3, g_n1 = call(
         rear_kernel, "rear",
-        [((EARLY_HALF, 128), F32), ((EARLY_HALF, 128), F32), ((CELLS, WIDTH), BF16)],
-        [core, temper],
-        [tok, mix, query_weight, key_weight, value_weight, feats, mids, gs, weights, xt, stats, gres,
-         ln2, w_fx, w_x, w_slice],
-    )
-    early = keep3 + swap(send3, OTHER_CORE)
+        [((EARLY_HALF, 128), F32), ((EARLY_HALF, 128), F32), tall],
+        [core],
+        [tok, swap(tok, Y_FAR), mix, feats, mids, gs, weights,
+         xt, stats, ln2, w_fx, w_x],
+    )
+    (out_rows,) = call(
+        cells_kernel, "cells", [((CELLS, WIDTH), BF16)], [], [g_n1, xt, gres, stats]
+    )
+    swapped, out_rows = lax.optimization_barrier((swap(send3, OTHER_CORE), out_rows))
+    early = keep3 + swapped
     both = jnp.concatenate(
         [late.reshape(16, LATE_PART, 128), early.reshape(16, EARLY_PART, 128)], axis=1
     )

time: 129 us -> 122 us (0.946)
  waiting for transfers between devices: 33.8 us -> 25.7 us
  starting transfers between devices: 39.9 us -> 43.5 us
  local copies, waits for them, and re-layouts: 1.66 us -> 0.07 us
    ppermute x16, waiting for transfers between devices: 33.8 us -> 25.7 us  [swap(): return lax.ppermute(v, AXES, pairs)]
    ppermute x16, starting transfers between devices: 39.9 us -> 43.5 us  [swap(): return lax.ppermute(v, AXES, pairs)]
    unnamed x24 -> x8, local copies, waits for them, and re-layouts: 1.61 us -> 0.02 us
    pallas_call x4 -> x6, Pallas kernels: 17.4 us -> 17.5 us  [call(): pl.pallas_call(kernel, name=name, out_shape=[jax.ShapeDtypeStruct(shape,...]
  transfers between devices with their start and end apart: 16 -> 16, of which waited for: 14 -> 13; matrix products, arithmetic and copies ran while one was open for 0% -> 0% of each run, Pallas kernels for 5% -> 6%
where the time goes in v3:
time: 122 us
  starting transfers between devices  43.5 us (36%)
  blocking collectives  33.4 us (27%)
  waiting for transfers between devices  25.7 us (21%)
  Pallas kernels  17.5 us (14%)
  between operations  1.58 us (1%)
    ppermute x16, starting transfers between devices, swap(): return lax.ppermute(v, AXES, pairs)  43.5 us
    ppermute x16, waiting for transfers between devices, swap(): return lax.ppermute(v, AXES, pairs)  25.7 us
    all_to_all x1, blocking collectives, body(): part = jnp.sum(lax.all_to_all(both, PLANE, 0, 0), axis=0)  19.7 us
    pallas_call x6, Pallas kernels, call(): pl.pallas_call(kernel, name=name, out_shape=[jax.ShapeDtypeStruct(shape,...  17.5 us
    all_to_all x1, blocking collectives, body(): mine = lax.all_to_all(jnp.broadcast_to(part[None], both.shape), PLANE, 0, 0)  13.7 us
  transfers between devices with their start and end apart: 16, of which 13 were waited for; matrix products, arithmetic and copies ran while one was open for 0% of the time, Pallas kernels for 6%

profile of v3, /device:TPU:1, one launch (start us, length us, event | category | flops | bytes accessed | tf_op | source)
XLA Modules:
  0.0 122.0 jit_solution(6491587021526098997)
XLA Ops:
  1.3 3.2 %front.1 = (f32[136,128]{1,0:T(8,128)S(1)}, bf16[256,1024]{1,0:T(8,128)(2,1)S(1)}, bf16[256,1024]{1,0:T(8,128)(2,1)S(1)}, bf16[512,1024]{1,0:T(8,128)(2,1)S(1)}, f32[64,1024]{1,0:T(8,128)S(1)}) custom-call(s32[1,1]{1,0:T(1,128)S(6)} %copy.33.count_ref, f32[8]{0:T(128)} %temper_hbm.1, bf16[1024,256]{1,0:T(8,128)(2,1)} %bitcast.16, f32[1,256]{1,0:T(1,128)} %bitcast.22, ...), custom_call_target="tpu_custom_call" | custom-call | tf_op jit(solution)/shard_map/front/pallas_call | solution.py:448
  4.5 0.0 copy-start
  4.5 3.3 %collective-permute-start = (f32[136,128]{1,0:T(8,128)S(1)}, f32[136,128]{1,0:T(8,128)S(1)}, u32[]{:S(2)}, u32[]{:S(2)}) collective-permute-start(f32[136,128]{1,0:T(8,128)S(1)} %get-tuple-element.51), channel_id=1, source_target_pairs={{0,1},{1,0},{2,3},{3,2},{4,5},{5,4},{6,7},{7,6},{8,9},{9,8},{10,11... | collective-permute-start | bytes 208904 | tf_op jit(solution)/shard_map/ppermute | solution.py:430
  7.9 0.9 collective-permute-done
  8.8 0.1 collective-permute-start.1
  8.9 3.1 %collective-permute-done.1 = f32[136,128]{1,0:T(8,128)S(1)} collective-permute-done((f32[136,128]{1,0:T(8,128)S(1)}, f32[136,128]{1,0:T(8,128)S(1)}, u32[]{:S(2)}, u32[]{:S(2)}) %collective-permute-start.1) | collective-permute-done | bytes 69664 | tf_op jit(solution)/shard_map/ppermute | solution.py:430
  12.0 2.0 %collective-permute-start.2 = (f32[136,128]{1,0:T(8,128)S(1)}, f32[136,128]{1,0:T(8,128)S(1)}, u32[]{:S(2)}, u32[]{:S(2)}) collective-permute-start(f32[136,128]{1,0:T(8,128)S(1)} %add.40), channel_id=1, source_target_pairs={{0,4},{1,5},{2,6},{3,7},{4,0},{5,1},{6,2},{7,3},{8,12},{9,13},{10,... | collective-permute-start | bytes 208904 | tf_op jit(solution)/shard_map/ppermute | solution.py:430
  14.0 1.4 %keep.1.near_ref = bf16[2816,256]{1,0:T(8,128)(2,1)S(1)} custom-call(bf16[256,256]{1,0:T(8,128)(2,1)} %wout_hbm.1, bf16[256,256]{1,0:T(8,128)(2,1)} %wup_hbm.1, bf16[256,256]{1,0:T(8,128)(2,1)} %wdown_hbm.1, bf16[1024,256]{1,0:T(8,128)(2,1)} %bitcast.17, bf16[1024,256]{1,0:T(8,128)(2,1)} %bitcast.20), custom_call_target="tpu_custom_call" | custom-call | tf_op jit(solution)/shard_map/keep/pallas_call | solution.py:448
  15.5 0.0 copy-done
  15.5 1.5 %collective-permute-done.2 = f32[136,128]{1,0:T(8,128)S(1)} collective-permute-done((f32[136,128]{1,0:T(8,128)S(1)}, f32[136,128]{1,0:T(8,128)S(1)}, u32[]{:S(2)}, u32[]{:S(2)}) %collective-permute-start.2) | collective-permute-done | bytes 69664 | tf_op jit(solution)/shard_map/ppermute | solution.py:430
  16.9 3.9 %collective-permute-start.3 = (f32[136,128]{1,0:T(8,128)S(1)}, f32[136,128]{1,0:T(8,128)S(1)}, u32[]{:S(2)}, u32[]{:S(2)}) collective-permute-start(f32[136,128]{1,0:T(8,128)S(1)} %add.41), channel_id=1, source_target_pairs={{0,14},{1,15},{2,12},{3,13},{4,10},{5,11},{6,8},{7,9},{8,6},{9,7},... | collective-permute-start | bytes 208904 | tf_op jit(solution)/shard_map/ppermute | solution.py:430
  20.9 2.2 %collective-permute-done.3 = f32[136,128]{1,0:T(8,128)S(1)} collective-permute-done((f32[136,128]{1,0:T(8,128)S(1)}, f32[136,128]{1,0:T(8,128)S(1)}, u32[]{:S(2)}, u32[]{:S(2)}) %collective-permute-start.3) | collective-permute-done | bytes 69664 | tf_op jit(solution)/shard_map/ppermute | solution.py:430
  23.1 3.0 %collective-permute-start.4 = (f32[136,128]{1,0:T(8,128)S(1)}, f32[136,128]{1,0:T(8,128)S(1)}, u32[]{:S(2)}, u32[]{:S(2)}) collective-permute-start(f32[136,128]{1,0:T(8,128)S(1)} %add.42.mine_ref), channel_id=1, source_target_pairs={{0,16},{1,17},{2,18},{3,19},{4,20},{5,21},{6,22},{7,23},{8,24},{9,... | collective-permute-start | bytes 208904 | tf_op jit(solution)/shard_map/ppermute | solution.py:430
  26.1 1.7 %collective-permute-done.4.theirs_ref = f32[136,128]{1,0:T(8,128)S(1)} collective-permute-done((f32[136,128]{1,0:T(8,128)S(1)}, f32[136,128]{1,0:T(8,128)S(1)}, u32[]{:S(2)}, u32[]{:S(2)}) %collective-permute-start.4) | collective-permute-done | bytes 69664 | tf_op jit(solution)/shard_map/ppermute | solution.py:430
  27.9 0.0 copy-start.1
  27.9 0.0 copy-start.2
  27.9 0.0 copy-start.3
  27.9 5.9 %middle.1 = (f32[32,512]{1,0:T(8,128)S(1)}, f32[256,1024]{1,0:T(8,128)S(1)}, bf16[256,1024]{1,0:T(8,128)(2,1)S(1)}, f32[768,128]{1,0:T(8,128)S(1)}, f32[768,128]...) custom-call(s32[1]{0:T(128)} %bitcast.core_ref, ...), custom_call_target="tpu_custom_call" | custom-call | tf_op jit(solution)/shard_map/middle/pallas_call | solution.py:448
  33.8 4.8 %collective-permute-start.5 = (f32[32,512]{1,0:T(8,128)S(1)}, f32[32,512]{1,0:T(8,128)S(1)}, u32[]{:S(2)}, u32[]{:S(2)}) collective-permute-start(f32[32,512]{1,0:T(8,128)S(1)} %get-tuple-element.57), channel_id=1, source_target_pairs={{0,1},{1,0},{2,3},{3,2},{4,5},{5,4},{6,7},{7,6},{8,9},{9,8},{10,11... | collective-permute-start | bytes 196616 | tf_op jit(solution)/shard_map/ppermute | solution.py:430
  38.6 0.9 collective-permute-done.5
  39.5 0.6 collective-permute-start.6
  40.1 2.6 %collective-permute-done.6 = f32[32,512]{1,0:T(8,128)S(1)} collective-permute-done((f32[32,512]{1,0:T(8,128)S(1)}, f32[32,512]{1,0:T(8,128)S(1)}, u32[]{:S(2)}, u32[]{:S(2)}) %collective-permute-start.6) | collective-permute-done | bytes 65568 | tf_op jit(solution)/shard_map/ppermute | solution.py:430
  42.7 1.2 collective-permute-start.7
  43.9 3.6 %collective-permute-done.7 = f32[32,512]{1,0:T(8,128)S(1)} collective-permute-done((f32[32,512]{1,0:T(8,128)S(1)}, f32[32,512]{1,0:T(8,128)S(1)}, u32[]{:S(2)}, u32[]{:S(2)}) %collective-permute-start.7) | collective-permute-done | bytes 65568 | tf_op jit(solution)/shard_map/ppermute | solution.py:430
  47.5 2.6 %collective-permute-start.8 = (f32[32,512]{1,0:T(8,128)S(1)}, f32[32,512]{1,0:T(8,128)S(1)}, u32[]{:S(2)}, u32[]{:S(2)}) collective-permute-start(f32[32,512]{1,0:T(8,128)S(1)} %add.45), channel_id=1, source_target_pairs={{0,14},{1,15},{2,12},{3,13},{4,10},{5,11},{6,8},{7,9},{8,6},{9,7},... | collective-permute-start | bytes 196616 | tf_op jit(solution)/shard_map/ppermute | solution.py:430
  50.2 1.8 %collective-permute-done.8 = f32[32,512]{1,0:T(8,128)S(1)} collective-permute-done((f32[32,512]{1,0:T(8,128)S(1)}, f32[32,512]{1,0:T(8,128)S(1)}, u32[]{:S(2)}, u32[]{:S(2)}) %collective-permute-start.8) | collective-permute-done | bytes 65568 | tf_op jit(solution)/shard_map/ppermute | solution.py:430
  52.0 3.0 %collective-permute-start.9 = (f32[32,512]{1,0:T(8,128)S(1)}, f32[32,512]{1,0:T(8,128)S(1)}, u32[]{:S(2)}, u32[]{:S(2)}) collective-permute-start(f32[32,512]{1,0:T(8,128)S(1)} %add.46.mine_ref), channel_id=1, source_target_pairs={{0,16},{1,17},{2,18},{3,19},{4,20},{5,21},{6,22},{7,23},{8,24},{9,... | collective-permute-start | bytes 196616 | tf_op jit(solution)/shard_map/ppermute | solution.py:430
  55.0 4.8 %collective-permute-start.11 = (f32[768,128]{1,0:T(8,128)S(1)}, f32[768,128]{1,0:T(8,128)S(1)}, u32[]{:S(2)}, u32[]{:S(2)}) collective-permute-start(f32[768,128]{1,0:T(8,128)S(1)} %get-tuple-element.69), channel_id=1, source_target_pairs={{0,1},{1,0},{2,3},{3,2},{4,5},{5,4},{6,7},{7,6},{8,9},{9,8},{10,11... | collective-permute-start | bytes 1179656 | tf_op jit(solution)/shard_map/ppermute | solution.py:430
  59.7 0.0 collective-permute-done.9.theirs_ref
  59.8 0.0 copy-done.1
  59.8 0.0 copy-done.2
  59.8 0.0 copy-done.3
  59.8 4.3 %rear.1 = (f32[640,128]{1,0:T(8,128)S(1)}, f32[640,128]{1,0:T(8,128)S(1)}, f32[256,1024]{1,0:T(8,128)S(1)}) custom-call(s32[1]{0:T(128)} %bitcast.core_ref, f32[32,512]{1,0:T(8,128)S(1)} %add.46.mine_ref, f32[32,512]{1,0:T(8,128)S(1)} %collective-permute-done.9.theirs_ref, f32[296,512]{1,0:T(8,128)S(1)} %get-tuple-element.58.mix_ref, ...), custom_call_target="tpu_custom_call" | custom-call | tf_op jit(solution)/shard_map/rear/pallas_call | solution.py:448
  64.0 2.6 %collective-permute-start.10 = (f32[640,128]{1,0:T(8,128)S(1)}, f32[640,128]{1,0:T(8,128)S(1)}, u32[]{:S(2)}, u32[]{:S(2)}) collective-permute-start(f32[640,128]{1,0:T(8,128)S(1)} %get-tuple-element.64), channel_id=1, source_target_pairs={{0,1},{1,0},{2,3},{3,2},{4,5},{5,4},{6,7},{7,6},{8,9},{9,8},{10,11... | collective-permute-start | bytes 983048 | tf_op jit(solution)/shard_map/ppermute | solution.py:430
  66.7 1.5 %cells.1 = bf16[1024,256]{1,0:T(8,128)(2,1)} custom-call(f32[256,1024]{1,0:T(8,128)S(1)} %get-tuple-element.65.g_n1_ref, bf16[256,1024]{1,0:T(8,128)(2,1)S(1)} %get-tuple-element.62.xt_ref, f32[256,1024]{1,0:T(8,128)S(1)} %get-tuple-element.66.gres_ref, f32[64,1024]{1,0:T(8,128)S(1)} %get-tuple-element.54.stats_ref), custom_call_target="tpu_custom_call" | custom-call | tf_op jit(solution)/shard_map/cells/pallas_call | solution.py:448
  68.2 0.0 collective-permute-done.11
  68.3 0.0 collective-permute-done.10
  68.4 19.7 %all_to_all.10 = f32[16,88,128]{2,1,0:T(8,128)S(1)} all-to-all(f32[16,88,128]{2,1,0:T(8,128)S(1)} %pad_maximum_fusion), channel_id=1, replica_groups=mesh['yl'=2,'x'=4,'yh'=2,'z'=8,'c'=2] {'yl','x','yh'}, dimensions={0} | all-to-all | bytes 1441792 | tf_op jit(solution)/shard_map/all_to_all | solution.py:516
  88.1 1.2 collective-permute-start.12
  89.3 1.8 %collective-permute-done.12 = f32[88,128]{1,0:T(8,128)S(1)} collective-permute-done((f32[88,128]{1,0:T(8,128)S(1)}, f32[88,128]{1,0:T(8,128)S(1)}, u32[]{:S(2)}, u32[]{:S(2)}) %collective-permute-start.12) | collective-permute-done | bytes 45088 | tf_op jit(solution)/shard_map/ppermute | solution.py:430
  91.1 1.8 %collective-permute-start.13 = (f32[88,128]{1,0:T(8,128)S(1)}, f32[88,128]{1,0:T(8,128)S(1)}, u32[]{:S(2)}, u32[]{:S(2)}) collective-permute-start(f32[88,128]{1,0:T(8,128)S(1)} %add.49), channel_id=1, source_target_pairs={{0,4},{1,5},{2,6},{3,7},{4,0},{5,1},{6,2},{7,3},{8,12},{9,13},{10,... | collective-permute-start | bytes 135176 | tf_op jit(solution)/shard_map/ppermute | solution.py:430
  92.9 2.1 %collective-permute-done.13 = f32[88,128]{1,0:T(8,128)S(1)} collective-permute-done((f32[88,128]{1,0:T(8,128)S(1)}, f32[88,128]{1,0:T(8,128)S(1)}, u32[]{:S(2)}, u32[]{:S(2)}) %collective-permute-start.13) | collective-permute-done | bytes 45088 | tf_op jit(solution)/shard_map/ppermute | solution.py:430
  95.0 3.4 %collective-permute-start.14 = (f32[88,128]{1,0:T(8,128)S(1)}, f32[88,128]{1,0:T(8,128)S(1)}, u32[]{:S(2)}, u32[]{:S(2)}) collective-permute-start(f32[88,128]{1,0:T(8,128)S(1)} %add.50), channel_id=1, source_target_pairs={{0,14},{1,15},{2,12},{3,13},{4,10},{5,11},{6,8},{7,9},{8,6},{9,7},... | collective-permute-start | bytes 135176 | tf_op jit(solution)/shard_map/ppermute | solution.py:430
  98.4 1.4 %collective-permute-done.14 = f32[88,128]{1,0:T(8,128)S(1)} collective-permute-done((f32[88,128]{1,0:T(8,128)S(1)}, f32[88,128]{1,0:T(8,128)S(1)}, u32[]{:S(2)}, u32[]{:S(2)}) %collective-permute-start.14) | collective-permute-done | bytes 45088 | tf_op jit(solution)/shard_map/ppermute | solution.py:430
  99.9 13.7 %all_to_all.11.mine_ref = f32[16,88,128]{2,1,0:T(8,128)S(1)} all-to-all(f32[16,88,128]{2,1,0:T(8,128)S(1)} %broadcast_in_dim.14), channel_id=1, replica_groups=mesh['yl'=2,'x'=4,'yh'=2,'z'=8,'c'=2] {'yl','x','yh'}, dimensions={0} | all-to-all | bytes 1441792 | tf_op jit(solution)/shard_map/all_to_all | solution.py:519
  113.6 5.3 %collective-permute-start.15 = (f32[16,88,128]{2,1,0:T(8,128)S(1)}, f32[16,88,128]{2,1,0:T(8,128)S(1)}, u32[]{:S(2)}, u32[]{:S(2)}) collective-permute-start(f32[16,88,128]{2,1,0:T(8,128)S(1)} %all_to_all.11.mine_ref), channel_id=1, source_target_pairs={{0,1},{1,0},{2,3},{3,2},{4,5},{5,4},{6,7},{7,6},{8,9},{9,8},{10,11... | collective-permute-start | bytes 2162696 | tf_op jit(solution)/shard_map/ppermute | solution.py:430
  118.9 1.8 %collective-permute-done.15.theirs_ref = f32[16,88,128]{2,1,0:T(8,128)S(1)} collective-permute-done((f32[16,88,128]{2,1,0:T(8,128)S(1)}, f32[16,88,128]{2,1,0:T(8,128)S(1)}, u32[]{:S(2)}, u32[]{:S(2)}) %collective-permute-start.15) | collective-permute-done | bytes 720928 | tf_op jit(solution)/shard_map/ppermute | solution.py:430
  120.7 1.1 last.1
  (16 shorter events, 0.3 us)
Async XLA Ops:
  4.5 10.9 %copy-start = (bf16[256,1024]{1,0:T(8,128)(2,1)}, bf16[256,1024]{1,0:T(8,128)(2,1)S(1)}, u32[]{:S(2)}) copy-start(bf16[256,1024]{1,0:T(8,128)(2,1)S(1)} %get-tuple-element.60.mids_ref) | copy-start | bytes 1572868
  4.5 4.2 %collective-permute-start = (f32[136,128]{1,0:T(8,128)S(1)}, f32[136,128]{1,0:T(8,128)S(1)}, u32[]{:S(2)}, u32[]{:S(2)}) collective-permute-start(f32[136,128]{1,0:T(8,128)S(1)} %get-tuple-element.51), channel_id=1, source_target_pairs={{0,1},{1,0},{2,3},{3,2},{4,5},{5,4},{6,7},{7,6},{8,9},{9,8},{10,11... | collective-permute-start | bytes 208904 | tf_op jit(solution)/shard_map/ppermute | solution.py:430
  8.8 3.2 %collective-permute-start.1 = (f32[136,128]{1,0:T(8,128)S(1)}, f32[136,128]{1,0:T(8,128)S(1)}, u32[]{:S(2)}, u32[]{:S(2)}) collective-permute-start(f32[136,128]{1,0:T(8,128)S(1)} %add.39), channel_id=1, source_target_pairs={{0,2},{1,3},{2,0},{3,1},{4,6},{5,7},{6,4},{7,5},{8,10},{9,11},{10,... | collective-permute-start | bytes 208904 | tf_op jit(solution)/shard_map/ppermute | solution.py:430
  12.0 4.9 %collective-permute-start.2 = (f32[136,128]{1,0:T(8,128)S(1)}, f32[136,128]{1,0:T(8,128)S(1)}, u32[]{:S(2)}, u32[]{:S(2)}) collective-permute-start(f32[136,128]{1,0:T(8,128)S(1)} %add.40), channel_id=1, source_target_pairs={{0,4},{1,5},{2,6},{3,7},{4,0},{5,1},{6,2},{7,3},{8,12},{9,13},{10,... | collective-permute-start | bytes 208904 | tf_op jit(solution)/shard_map/ppermute | solution.py:430
  16.9 6.2 %collective-permute-start.3 = (f32[136,128]{1,0:T(8,128)S(1)}, f32[136,128]{1,0:T(8,128)S(1)}, u32[]{:S(2)}, u32[]{:S(2)}) collective-permute-start(f32[136,128]{1,0:T(8,128)S(1)} %add.41), channel_id=1, source_target_pairs={{0,14},{1,15},{2,12},{3,13},{4,10},{5,11},{6,8},{7,9},{8,6},{9,7},... | collective-permute-start | bytes 208904 | tf_op jit(solution)/shard_map/ppermute | solution.py:430
  23.1 4.8 %collective-permute-start.4 = (f32[136,128]{1,0:T(8,128)S(1)}, f32[136,128]{1,0:T(8,128)S(1)}, u32[]{:S(2)}, u32[]{:S(2)}) collective-permute-start(f32[136,128]{1,0:T(8,128)S(1)} %add.42.mine_ref), channel_id=1, source_target_pairs={{0,16},{1,17},{2,18},{3,19},{4,20},{5,21},{6,22},{7,23},{8,24},{9,... | collective-permute-start | bytes 208904 | tf_op jit(solution)/shard_map/ppermute | solution.py:430
  27.9 31.9 %copy-start.1 = (bf16[256,1024]{1,0:T(8,128)(2,1)S(1)}, bf16[256,1024]{1,0:T(8,128)(2,1)}, u32[]{:S(2)}) copy-start(bf16[256,1024]{1,0:T(8,128)(2,1)} %copy-done) | copy-start | bytes 1572868
  27.9 31.9 %copy-start.2 = (bf16[256,256]{1,0:T(8,128)(2,1)S(1)}, bf16[256,256]{1,0:T(8,128)(2,1)}, u32[]{:S(2)}) copy-start(bf16[256,256]{1,0:T(8,128)(2,1)} %wfx_ref.1) | copy-start | bytes 393220
  27.9 31.9 %copy-start.3 = (bf16[256,256]{1,0:T(8,128)(2,1)S(1)}, bf16[256,256]{1,0:T(8,128)(2,1)}, u32[]{:S(2)}) copy-start(bf16[256,256]{1,0:T(8,128)(2,1)} %wx_ref.1) | copy-start | bytes 393220
  33.8 5.7 %collective-permute-start.5 = (f32[32,512]{1,0:T(8,128)S(1)}, f32[32,512]{1,0:T(8,128)S(1)}, u32[]{:S(2)}, u32[]{:S(2)}) collective-permute-start(f32[32,512]{1,0:T(8,128)S(1)} %get-tuple-element.57), channel_id=1, source_target_pairs={{0,1},{1,0},{2,3},{3,2},{4,5},{5,4},{6,7},{7,6},{8,9},{9,8},{10,11... | collective-permute-start | bytes 196616 | tf_op jit(solution)/shard_map/ppermute | solution.py:430
  39.5 3.2 %collective-permute-start.6 = (f32[32,512]{1,0:T(8,128)S(1)}, f32[32,512]{1,0:T(8,128)S(1)}, u32[]{:S(2)}, u32[]{:S(2)}) collective-permute-start(f32[32,512]{1,0:T(8,128)S(1)} %add.43), channel_id=1, source_target_pairs={{0,2},{1,3},{2,0},{3,1},{4,6},{5,7},{6,4},{7,5},{8,10},{9,11},{10,... | collective-permute-start | bytes 196616 | tf_op jit(solution)/shard_map/ppermute | solution.py:430
  42.7 4.8 %collective-permute-start.7 = (f32[32,512]{1,0:T(8,128)S(1)}, f32[32,512]{1,0:T(8,128)S(1)}, u32[]{:S(2)}, u32[]{:S(2)}) collective-permute-start(f32[32,512]{1,0:T(8,128)S(1)} %add.44), channel_id=1, source_target_pairs={{0,4},{1,5},{2,6},{3,7},{4,0},{5,1},{6,2},{7,3},{8,12},{9,13},{10,... | collective-permute-start | bytes 196616 | tf_op jit(solution)/shard_map/ppermute | solution.py:430
  47.5 4.4 %collective-permute-start.8 = (f32[32,512]{1,0:T(8,128)S(1)}, f32[32,512]{1,0:T(8,128)S(1)}, u32[]{:S(2)}, u32[]{:S(2)}) collective-permute-start(f32[32,512]{1,0:T(8,128)S(1)} %add.45), channel_id=1, source_target_pairs={{0,14},{1,15},{2,12},{3,13},{4,10},{5,11},{6,8},{7,9},{8,6},{9,7},... | collective-permute-start | bytes 196616 | tf_op jit(solution)/shard_map/ppermute | solution.py:430
  52.0 7.8 %collective-permute-start.9 = (f32[32,512]{1,0:T(8,128)S(1)}, f32[32,512]{1,0:T(8,128)S(1)}, u32[]{:S(2)}, u32[]{:S(2)}) collective-permute-start(f32[32,512]{1,0:T(8,128)S(1)} %add.46.mine_ref), channel_id=1, source_target_pairs={{0,16},{1,17},{2,18},{3,19},{4,20},{5,21},{6,22},{7,23},{8,24},{9,... | collective-permute-start | bytes 196616 | tf_op jit(solution)/shard_map/ppermute | solution.py:430
  55.0 13.2 %collective-permute-start.11 = (f32[768,128]{1,0:T(8,128)S(1)}, f32[768,128]{1,0:T(8,128)S(1)}, u32[]{:S(2)}, u32[]{:S(2)}) collective-permute-start(f32[768,128]{1,0:T(8,128)S(1)} %get-tuple-element.69), channel_id=1, source_target_pairs={{0,1},{1,0},{2,3},{3,2},{4,5},{5,4},{6,7},{7,6},{8,9},{9,8},{10,11... | collective-permute-start | bytes 1179656 | tf_op jit(solution)/shard_map/ppermute | solution.py:430
  64.0 4.2 %collective-permute-start.10 = (f32[640,128]{1,0:T(8,128)S(1)}, f32[640,128]{1,0:T(8,128)S(1)}, u32[]{:S(2)}, u32[]{:S(2)}) collective-permute-start(f32[640,128]{1,0:T(8,128)S(1)} %get-tuple-element.64), channel_id=1, source_target_pairs={{0,1},{1,0},{2,3},{3,2},{4,5},{5,4},{6,7},{7,6},{8,9},{9,8},{10,11... | collective-permute-start | bytes 983048 | tf_op jit(solution)/shard_map/ppermute | solution.py:430
  88.1 3.0 %collective-permute-start.12 = (f32[88,128]{1,0:T(8,128)S(1)}, f32[88,128]{1,0:T(8,128)S(1)}, u32[]{:S(2)}, u32[]{:S(2)}) collective-permute-start(f32[88,128]{1,0:T(8,128)S(1)} %reduce_sum.9), channel_id=1, source_target_pairs={{0,2},{1,3},{2,0},{3,1},{4,6},{5,7},{6,4},{7,5},{8,10},{9,11},{10,... | collective-permute-start | bytes 135176 | tf_op jit(solution)/shard_map/ppermute | solution.py:430
  91.1 3.9 %collective-permute-start.13 = (f32[88,128]{1,0:T(8,128)S(1)}, f32[88,128]{1,0:T(8,128)S(1)}, u32[]{:S(2)}, u32[]{:S(2)}) collective-permute-start(f32[88,128]{1,0:T(8,128)S(1)} %add.49), channel_id=1, source_target_pairs={{0,4},{1,5},{2,6},{3,7},{4,0},{5,1},{6,2},{7,3},{8,12},{9,13},{10,... | collective-permute-start | bytes 135176 | tf_op jit(solution)/shard_map/ppermute | solution.py:430
  95.0 4.8 %collective-permute-start.14 = (f32[88,128]{1,0:T(8,128)S(1)}, f32[88,128]{1,0:T(8,128)S(1)}, u32[]{:S(2)}, u32[]{:S(2)}) collective-permute-start(f32[88,128]{1,0:T(8,128)S(1)} %add.50), channel_id=1, source_target_pairs={{0,14},{1,15},{2,12},{3,13},{4,10},{5,11},{6,8},{7,9},{8,6},{9,7},... | collective-permute-start | bytes 135176 | tf_op jit(solution)/shard_map/ppermute | solution.py:430
  113.6 7.1 %collective-permute-start.15 = (f32[16,88,128]{2,1,0:T(8,128)S(1)}, f32[16,88,128]{2,1,0:T(8,128)S(1)}, u32[]{:S(2)}, u32[]{:S(2)}) collective-permute-start(f32[16,88,128]{2,1,0:T(8,128)S(1)} %all_to_all.11.mine_ref), channel_id=1, source_target_pairs={{0,1},{1,0},{2,3},{3,2},{4,5},{5,4},{6,7},{7,6},{8,9},{9,8},{10,11... | collective-permute-start | bytes 2162696 | tf_op jit(solution)/shard_map/ppermute | solution.py:430

commit v4 on v3

--- a/solution.py
+++ b/solution.py
@@ -425,15 +425,17 @@
 Z_FAR = permutation(lambda yl, x, yh, z, c: (yl, x, yh, 7 - z, c))
 Y_FAR = permutation(lambda yl, x, yh, z, c: (yl, x, 1 - yh, z, c))
 
+BOTH_FAR = permutation(lambda yl, x, yh, z, c: (yl, x, 1 - yh, z ^ 2, c))
+
 
 def swap(v, pairs):
     return lax.ppermute(v, AXES, pairs)
 
 
 def near_sum(v):
-    for pairs in (OTHER_CORE, Z_ONE, Z_TWO, Z_FAR):
+    for pairs in (OTHER_CORE, Z_ONE):
         v = v + swap(v, pairs)
-    return v
+    return (v + swap(v, Z_TWO)) + (swap(v, Y_FAR) + swap(v, BOTH_FAR))
 
 
 VMEM = pl.BlockSpec(memory_space=pltpu.VMEM)
@@ -485,15 +487,16 @@
     (near,) = call(
         keep_kernel, "keep", [((2816, WIDTH), BF16)], [], [], [w_out, w_up, w_down, rows, cot], copies=5
     )
-    got, near = lax.optimization_barrier((swap(pay, Z_TWO), near))
-    pay = pay + got
-    pay = pay + swap(pay, Z_FAR)
+    two, far, both_far, near = lax.optimization_barrier(
+        (swap(pay, Z_TWO), swap(pay, Y_FAR), swap(pay, BOTH_FAR), near)
+    )
+    pay = (pay + two) + (far + both_far)
     tok, gres, gs, keep2, send2, ln2, mix, xt, layer = call(
         middle_kernel, "middle",
         [((HEAD, 512), F32), tall, tall_b, ((LATE_HALF, 128), F32), ((LATE_HALF, 128), F32),
          ((8, WIDTH), F32), ((296, 512), F32), tall_b, ((CELLS, WIDTH), BF16)],
         [core],
-        [pay, swap(pay, Y_FAR), weights, stats, near],
+        [pay, swap(pay, Z_FAR), weights, stats, near],
         (), room(rows) + [pltpu.VMEM((136, 128), F32)], left=1, copies=1,
     )
     tok = near_sum(tok)
@@ -502,7 +505,7 @@
         rear_kernel, "rear",
         [((EARLY_HALF, 128), F32), ((EARLY_HALF, 128), F32), tall],
         [core],
-        [tok, swap(tok, Y_FAR), mix, feats, mids, gs, weights,
+        [tok, swap(tok, Z_FAR), mix, feats, mids, gs, weights,
          xt, stats, ln2, w_fx, w_x],
     )
     (out_rows,) = call(

time: 122 us -> 122 us (level); the launches traced: 122 us -> 121 us
  blocking collectives: 33.4 us -> 30.9 us
  starting transfers between devices: 43.5 us -> 45.5 us
    all_to_all x1, blocking collectives: 19.7 us -> 17.2 us  [body(): part = jnp.sum(lax.all_to_all(both, PLANE, 0, 0), axis=0)]
    ppermute x16 -> x18, starting transfers between devices: 43.5 us -> 45.5 us  [swap(): return lax.ppermute(v, AXES, pairs)]
    ppermute x16 -> x18, waiting for transfers between devices: 25.7 us -> 24.6 us  [swap(): return lax.ppermute(v, AXES, pairs)]
  transfers between devices with their start and end apart: 16 -> 18, of which waited for: 13 -> 12; matrix products, arithmetic and copies ran while one was open for 0% -> 0% of each run, Pallas kernels for 6% -> 6%
where the time goes in v4:
time: 122 us; the launch traced here: 121 us
  starting transfers between devices  45.5 us (37%)
  blocking collectives  30.9 us (25%)
  waiting for transfers between devices  24.6 us (20%)
  Pallas kernels  17.5 us (14%)
  between operations  1.58 us (1%)
    ppermute x18, starting transfers between devices, swap(): return lax.ppermute(v, AXES, pairs)  45.5 us
    ppermute x18, waiting for transfers between devices, swap(): return lax.ppermute(v, AXES, pairs)  24.6 us
    pallas_call x6, Pallas kernels, call(): pl.pallas_call(kernel, name=name, out_shape=[jax.ShapeDtypeStruct(shape,...  17.5 us
    all_to_all x1, blocking collectives, body(): part = jnp.sum(lax.all_to_all(both, PLANE, 0, 0), axis=0)  17.2 us
    all_to_all x1, blocking collectives, body(): mine = lax.all_to_all(jnp.broadcast_to(part[None], both.shape), PLANE, 0, 0)  13.7 us
  transfers between devices with their start and end apart: 18, of which 12 were waited for; matrix products, arithmetic and copies ran while one was open for 0% of the time, Pallas kernels for 6%

profile of v4, /device:TPU:1, one launch (start us, length us, event | category | flops | bytes accessed | tf_op | source)
XLA Modules:
  0.0 120.5 jit_solution(7718848017058679465)
XLA Ops:
  1.3 3.2 %front.1 = (f32[136,128]{1,0:T(8,128)S(1)}, bf16[256,1024]{1,0:T(8,128)(2,1)S(1)}, bf16[256,1024]{1,0:T(8,128)(2,1)S(1)}, bf16[512,1024]{1,0:T(8,128)(2,1)S(1)}, f32[64,1024]{1,0:T(8,128)S(1)}) custom-call(s32[1,1]{1,0:T(1,128)S(6)} %copy.33.count_ref, f32[8]{0:T(128)} %temper_hbm.1, bf16[1024,256]{1,0:T(8,128)(2,1)} %bitcast.16, f32[1,256]{1,0:T(1,128)} %bitcast.22, ...), custom_call_target="tpu_custom_call" | custom-call | tf_op jit(solution)/shard_map/front/pallas_call | solution.py:450
  4.5 0.0 copy-start
  4.5 3.3 %collective-permute-start = (f32[136,128]{1,0:T(8,128)S(1)}, f32[136,128]{1,0:T(8,128)S(1)}, u32[]{:S(2)}, u32[]{:S(2)}) collective-permute-start(f32[136,128]{1,0:T(8,128)S(1)} %get-tuple-element.53), channel_id=1, source_target_pairs={{0,1},{1,0},{2,3},{3,2},{4,5},{5,4},{6,7},{7,6},{8,9},{9,8},{10,11... | collective-permute-start | bytes 208904 | tf_op jit(solution)/shard_map/ppermute | solution.py:432
  7.9 0.9 collective-permute-done
  8.8 0.1 collective-permute-start.1
  8.9 3.1 %collective-permute-done.1 = f32[136,128]{1,0:T(8,128)S(1)} collective-permute-done((f32[136,128]{1,0:T(8,128)S(1)}, f32[136,128]{1,0:T(8,128)S(1)}, u32[]{:S(2)}, u32[]{:S(2)}) %collective-permute-start.1) | collective-permute-done | bytes 69664 | tf_op jit(solution)/shard_map/ppermute | solution.py:432
  12.0 2.0 %collective-permute-start.2 = (f32[136,128]{1,0:T(8,128)S(1)}, f32[136,128]{1,0:T(8,128)S(1)}, u32[]{:S(2)}, u32[]{:S(2)}) collective-permute-start(f32[136,128]{1,0:T(8,128)S(1)} %add.46), channel_id=1, source_target_pairs={{0,4},{1,5},{2,6},{3,7},{4,0},{5,1},{6,2},{7,3},{8,12},{9,13},{10,... | collective-permute-start | bytes 208904 | tf_op jit(solution)/shard_map/ppermute | solution.py:432
  14.0 2.9 %collective-permute-start.3 = (f32[136,128]{1,0:T(8,128)S(1)}, f32[136,128]{1,0:T(8,128)S(1)}, u32[]{:S(2)}, u32[]{:S(2)}) collective-permute-start(f32[136,128]{1,0:T(8,128)S(1)} %add.46), channel_id=1, source_target_pairs={{0,16},{1,17},{2,18},{3,19},{4,20},{5,21},{6,22},{7,23},{8,24},{9,... | collective-permute-start | bytes 208904 | tf_op jit(solution)/shard_map/ppermute | solution.py:432
  16.9 0.3 collective-permute-start.4
  17.2 1.4 %keep.1.near_ref = bf16[2816,256]{1,0:T(8,128)(2,1)S(1)} custom-call(bf16[256,256]{1,0:T(8,128)(2,1)} %wout_hbm.1, bf16[256,256]{1,0:T(8,128)(2,1)} %wup_hbm.1, bf16[256,256]{1,0:T(8,128)(2,1)} %wdown_hbm.1, bf16[1024,256]{1,0:T(8,128)(2,1)} %bitcast.17, bf16[1024,256]{1,0:T(8,128)(2,1)} %bitcast.20), custom_call_target="tpu_custom_call" | custom-call | tf_op jit(solution)/shard_map/keep/pallas_call | solution.py:450
  18.6 0.0 copy-done
  18.6 0.0 collective-permute-done.2
  18.6 0.0 collective-permute-done.3
  18.7 4.7 %collective-permute-done.4 = f32[136,128]{1,0:T(8,128)S(1)} collective-permute-done((f32[136,128]{1,0:T(8,128)S(1)}, f32[136,128]{1,0:T(8,128)S(1)}, u32[]{:S(2)}, u32[]{:S(2)}) %collective-permute-start.4) | collective-permute-done | bytes 69664 | tf_op jit(solution)/shard_map/ppermute | solution.py:432
  23.4 4.0 %collective-permute-start.5 = (f32[136,128]{1,0:T(8,128)S(1)}, f32[136,128]{1,0:T(8,128)S(1)}, u32[]{:S(2)}, u32[]{:S(2)}) collective-permute-start(f32[136,128]{1,0:T(8,128)S(1)} %add_add_fusion.mine_ref), channel_id=1, source_target_pairs={{0,14},{1,15},{2,12},{3,13},{4,10},{5,11},{6,8},{7,9},{8,6},{9,7},... | collective-permute-start | bytes 208904 | tf_op jit(solution)/shard_map/ppermute | solution.py:432
  27.4 2.4 %collective-permute-done.5.theirs_ref = f32[136,128]{1,0:T(8,128)S(1)} collective-permute-done((f32[136,128]{1,0:T(8,128)S(1)}, f32[136,128]{1,0:T(8,128)S(1)}, u32[]{:S(2)}, u32[]{:S(2)}) %collective-permute-start.5) | collective-permute-done | bytes 69664 | tf_op jit(solution)/shard_map/ppermute | solution.py:432
  29.8 5.9 %middle.1 = (f32[32,512]{1,0:T(8,128)S(1)}, f32[256,1024]{1,0:T(8,128)S(1)}, bf16[256,1024]{1,0:T(8,128)(2,1)S(1)}, f32[768,128]{1,0:T(8,128)S(1)}, f32[768,128]...) custom-call(s32[1]{0:T(128)} %bitcast.core_ref, ...), custom_call_target="tpu_custom_call" | custom-call | tf_op jit(solution)/shard_map/middle/pallas_call | solution.py:450
  35.7 3.5 %collective-permute-start.6 = (f32[32,512]{1,0:T(8,128)S(1)}, f32[32,512]{1,0:T(8,128)S(1)}, u32[]{:S(2)}, u32[]{:S(2)}) collective-permute-start(f32[32,512]{1,0:T(8,128)S(1)} %get-tuple-element.61), channel_id=1, source_target_pairs={{0,1},{1,0},{2,3},{3,2},{4,5},{5,4},{6,7},{7,6},{8,9},{9,8},{10,11... | collective-permute-start | bytes 196616 | tf_op jit(solution)/shard_map/ppermute | solution.py:432
  39.2 0.9 collective-permute-done.6
  40.1 2.0 %collective-permute-start.7 = (f32[32,512]{1,0:T(8,128)S(1)}, f32[32,512]{1,0:T(8,128)S(1)}, u32[]{:S(2)}, u32[]{:S(2)}) collective-permute-start(f32[32,512]{1,0:T(8,128)S(1)} %add.50), channel_id=1, source_target_pairs={{0,2},{1,3},{2,0},{3,1},{4,6},{5,7},{6,4},{7,5},{8,10},{9,11},{10,... | collective-permute-start | bytes 196616 | tf_op jit(solution)/shard_map/ppermute | solution.py:432
  42.1 2.2 %collective-permute-done.7 = f32[32,512]{1,0:T(8,128)S(1)} collective-permute-done((f32[32,512]{1,0:T(8,128)S(1)}, f32[32,512]{1,0:T(8,128)S(1)}, u32[]{:S(2)}, u32[]{:S(2)}) %collective-permute-start.7) | collective-permute-done | bytes 65568 | tf_op jit(solution)/shard_map/ppermute | solution.py:432
  44.3 0.3 collective-permute-start.10
  44.7 1.9 %collective-permute-start.8 = (f32[32,512]{1,0:T(8,128)S(1)}, f32[32,512]{1,0:T(8,128)S(1)}, u32[]{:S(2)}, u32[]{:S(2)}) collective-permute-start(f32[32,512]{1,0:T(8,128)S(1)} %add.51), channel_id=1, source_target_pairs={{0,4},{1,5},{2,6},{3,7},{4,0},{5,1},{6,2},{7,3},{8,12},{9,13},{10,... | collective-permute-start | bytes 196616 | tf_op jit(solution)/shard_map/ppermute | solution.py:432
  46.5 2.9 %collective-permute-start.9 = (f32[32,512]{1,0:T(8,128)S(1)}, f32[32,512]{1,0:T(8,128)S(1)}, u32[]{:S(2)}, u32[]{:S(2)}) collective-permute-start(f32[32,512]{1,0:T(8,128)S(1)} %add.51), channel_id=1, source_target_pairs={{0,16},{1,17},{2,18},{3,19},{4,20},{5,21},{6,22},{7,23},{8,24},{9,... | collective-permute-start | bytes 196616 | tf_op jit(solution)/shard_map/ppermute | solution.py:432
  49.5 1.4 %collective-permute-done.10 = f32[32,512]{1,0:T(8,128)S(1)} collective-permute-done((f32[32,512]{1,0:T(8,128)S(1)}, f32[32,512]{1,0:T(8,128)S(1)}, u32[]{:S(2)}, u32[]{:S(2)}) %collective-permute-start.10) | collective-permute-done | bytes 65568 | tf_op jit(solution)/shard_map/ppermute | solution.py:432
  50.9 1.4 %collective-permute-done.8 = f32[32,512]{1,0:T(8,128)S(1)} collective-permute-done((f32[32,512]{1,0:T(8,128)S(1)}, f32[32,512]{1,0:T(8,128)S(1)}, u32[]{:S(2)}, u32[]{:S(2)}) %collective-permute-start.8) | collective-permute-done | bytes 65568 | tf_op jit(solution)/shard_map/ppermute | solution.py:432
  52.3 0.0 collective-permute-done.9
  52.3 3.4 %collective-permute-start.11 = (f32[32,512]{1,0:T(8,128)S(1)}, f32[32,512]{1,0:T(8,128)S(1)}, u32[]{:S(2)}, u32[]{:S(2)}) collective-permute-start(f32[32,512]{1,0:T(8,128)S(1)} %add_add_fusion.1.mine_ref), channel_id=1, source_target_pairs={{0,14},{1,15},{2,12},{3,13},{4,10},{5,11},{6,8},{7,9},{8,6},{9,7},... | collective-permute-start | bytes 196616 | tf_op jit(solution)/shard_map/ppermute | solution.py:432
  55.8 3.3 %collective-permute-start.13 = (f32[768,128]{1,0:T(8,128)S(1)}, f32[768,128]{1,0:T(8,128)S(1)}, u32[]{:S(2)}, u32[]{:S(2)}) collective-permute-start(f32[768,128]{1,0:T(8,128)S(1)} %get-tuple-element.73), channel_id=1, source_target_pairs={{0,1},{1,0},{2,3},{3,2},{4,5},{5,4},{6,7},{7,6},{8,9},{9,8},{10,11... | collective-permute-start | bytes 1179656 | tf_op jit(solution)/shard_map/ppermute | solution.py:432
  59.1 0.0 collective-permute-done.11.theirs_ref
  59.1 0.0 copy-done.2
  59.1 0.0 copy-done.3
  59.1 4.3 %rear.1 = (f32[640,128]{1,0:T(8,128)S(1)}, f32[640,128]{1,0:T(8,128)S(1)}, f32[256,1024]{1,0:T(8,128)S(1)}) custom-call(s32[1]{0:T(128)} %bitcast.core_ref, f32[32,512]{1,0:T(8,128)S(1)} %add_add_fusion.1.mine_ref, f32[32,512]{1,0:T(8,128)S(1)} %collective-permute-done.11.theirs_ref, f32[296,512]{1,0:T(8,128)S(1)} %get-tuple-element.62.mix_ref, ...), custom_call_target="tpu_custom_call" | custom-call | tf_op jit(solution)/shard_map/rear/pallas_call | solution.py:450
  63.3 3.0 %collective-permute-start.12 = (f32[640,128]{1,0:T(8,128)S(1)}, f32[640,128]{1,0:T(8,128)S(1)}, u32[]{:S(2)}, u32[]{:S(2)}) collective-permute-start(f32[640,128]{1,0:T(8,128)S(1)} %get-tuple-element.68), channel_id=1, source_target_pairs={{0,1},{1,0},{2,3},{3,2},{4,5},{5,4},{6,7},{7,6},{8,9},{9,8},{10,11... | collective-permute-start | bytes 983048 | tf_op jit(solution)/shard_map/ppermute | solution.py:432
  66.4 1.5 %cells.1 = bf16[1024,256]{1,0:T(8,128)(2,1)} custom-call(f32[256,1024]{1,0:T(8,128)S(1)} %get-tuple-element.69.g_n1_ref, bf16[256,1024]{1,0:T(8,128)(2,1)S(1)} %get-tuple-element.66.xt_ref, f32[256,1024]{1,0:T(8,128)S(1)} %get-tuple-element.70.gres_ref, f32[64,1024]{1,0:T(8,128)S(1)} %get-tuple-element.58.stats_ref), custom_call_target="tpu_custom_call" | custom-call | tf_op jit(solution)/shard_map/cells/pallas_call | solution.py:450
  67.9 0.0 collective-permute-done.13
  68.0 0.0 collective-permute-done.12
  68.1 17.2 %all_to_all.10 = f32[16,88,128]{2,1,0:T(8,128)S(1)} all-to-all(f32[16,88,128]{2,1,0:T(8,128)S(1)} %pad_maximum_fusion), channel_id=1, replica_groups=mesh['yl'=2,'x'=4,'yh'=2,'z'=8,'c'=2] {'yl','x','yh'}, dimensions={0} | all-to-all | bytes 1441792 | tf_op jit(solution)/shard_map/all_to_all | solution.py:519
  85.3 3.2 %collective-permute-start.14 = (f32[88,128]{1,0:T(8,128)S(1)}, f32[88,128]{1,0:T(8,128)S(1)}, u32[]{:S(2)}, u32[]{:S(2)}) collective-permute-start(f32[88,128]{1,0:T(8,128)S(1)} %reduce_sum.9), channel_id=1, source_target_pairs={{0,2},{1,3},{2,0},{3,1},{4,6},{5,7},{6,4},{7,5},{8,10},{9,11},{10,... | collective-permute-start | bytes 135176 | tf_op jit(solution)/shard_map/ppermute | solution.py:432
  88.6 1.4 %collective-permute-done.14 = f32[88,128]{1,0:T(8,128)S(1)} collective-permute-done((f32[88,128]{1,0:T(8,128)S(1)}, f32[88,128]{1,0:T(8,128)S(1)}, u32[]{:S(2)}, u32[]{:S(2)}) %collective-permute-start.14) | collective-permute-done | bytes 45088 | tf_op jit(solution)/shard_map/ppermute | solution.py:432
  90.0 1.1 collective-permute-start.15
  91.1 2.8 %collective-permute-done.15 = f32[88,128]{1,0:T(8,128)S(1)} collective-permute-done((f32[88,128]{1,0:T(8,128)S(1)}, f32[88,128]{1,0:T(8,128)S(1)}, u32[]{:S(2)}, u32[]{:S(2)}) %collective-permute-start.15) | collective-permute-done | bytes 45088 | tf_op jit(solution)/shard_map/ppermute | solution.py:432
  93.9 3.0 %collective-permute-start.16 = (f32[88,128]{1,0:T(8,128)S(1)}, f32[88,128]{1,0:T(8,128)S(1)}, u32[]{:S(2)}, u32[]{:S(2)}) collective-permute-start(f32[88,128]{1,0:T(8,128)S(1)} %add.58), channel_id=1, source_target_pairs={{0,14},{1,15},{2,12},{3,13},{4,10},{5,11},{6,8},{7,9},{8,6},{9,7},... | collective-permute-start | bytes 135176 | tf_op jit(solution)/shard_map/ppermute | solution.py:432
  97.0 1.4 %collective-permute-done.16 = f32[88,128]{1,0:T(8,128)S(1)} collective-permute-done((f32[88,128]{1,0:T(8,128)S(1)}, f32[88,128]{1,0:T(8,128)S(1)}, u32[]{:S(2)}, u32[]{:S(2)}) %collective-permute-start.16) | collective-permute-done | bytes 45088 | tf_op jit(solution)/shard_map/ppermute | solution.py:432
  98.5 13.7 %all_to_all.11.mine_ref = f32[16,88,128]{2,1,0:T(8,128)S(1)} all-to-all(f32[16,88,128]{2,1,0:T(8,128)S(1)} %broadcast_in_dim.14), channel_id=1, replica_groups=mesh['yl'=2,'x'=4,'yh'=2,'z'=8,'c'=2] {'yl','x','yh'}, dimensions={0} | all-to-all | bytes 1441792 | tf_op jit(solution)/shard_map/all_to_all | solution.py:522
  112.2 5.3 %collective-permute-start.17 = (f32[16,88,128]{2,1,0:T(8,128)S(1)}, f32[16,88,128]{2,1,0:T(8,128)S(1)}, u32[]{:S(2)}, u32[]{:S(2)}) collective-permute-start(f32[16,88,128]{2,1,0:T(8,128)S(1)} %all_to_all.11.mine_ref), channel_id=1, source_target_pairs={{0,1},{1,0},{2,3},{3,2},{4,5},{5,4},{6,7},{7,6},{8,9},{9,8},{10,11... | collective-permute-start | bytes 2162696 | tf_op jit(solution)/shard_map/ppermute | solution.py:432
  117.4 1.8 %collective-permute-done.17.theirs_ref = f32[16,88,128]{2,1,0:T(8,128)S(1)} collective-permute-done((f32[16,88,128]{2,1,0:T(8,128)S(1)}, f32[16,88,128]{2,1,0:T(8,128)S(1)}, u32[]{:S(2)}, u32[]{:S(2)}) %collective-permute-start.17) | collective-permute-done | bytes 720928 | tf_op jit(solution)/shard_map/ppermute | solution.py:432
  119.2 1.1 last.1
  (18 shorter events, 0.3 us)
Async XLA Ops:
  4.5 14.1 %copy-start = (bf16[256,1024]{1,0:T(8,128)(2,1)}, bf16[256,1024]{1,0:T(8,128)(2,1)S(1)}, u32[]{:S(2)}) copy-start(bf16[256,1024]{1,0:T(8,128)(2,1)S(1)} %get-tuple-element.64.mids_ref) | copy-start | bytes 1572868
  4.5 4.2 %collective-permute-start = (f32[136,128]{1,0:T(8,128)S(1)}, f32[136,128]{1,0:T(8,128)S(1)}, u32[]{:S(2)}, u32[]{:S(2)}) collective-permute-start(f32[136,128]{1,0:T(8,128)S(1)} %get-tuple-element.53), channel_id=1, source_target_pairs={{0,1},{1,0},{2,3},{3,2},{4,5},{5,4},{6,7},{7,6},{8,9},{9,8},{10,11... | collective-permute-start | bytes 208904 | tf_op jit(solution)/shard_map/ppermute | solution.py:432
  8.8 3.2 %collective-permute-start.1 = (f32[136,128]{1,0:T(8,128)S(1)}, f32[136,128]{1,0:T(8,128)S(1)}, u32[]{:S(2)}, u32[]{:S(2)}) collective-permute-start(f32[136,128]{1,0:T(8,128)S(1)} %add.45), channel_id=1, source_target_pairs={{0,2},{1,3},{2,0},{3,1},{4,6},{5,7},{6,4},{7,5},{8,10},{9,11},{10,... | collective-permute-start | bytes 208904 | tf_op jit(solution)/shard_map/ppermute | solution.py:432
  12.0 6.6 %collective-permute-start.2 = (f32[136,128]{1,0:T(8,128)S(1)}, f32[136,128]{1,0:T(8,128)S(1)}, u32[]{:S(2)}, u32[]{:S(2)}) collective-permute-start(f32[136,128]{1,0:T(8,128)S(1)} %add.46), channel_id=1, source_target_pairs={{0,4},{1,5},{2,6},{3,7},{4,0},{5,1},{6,2},{7,3},{8,12},{9,13},{10,... | collective-permute-start | bytes 208904 | tf_op jit(solution)/shard_map/ppermute | solution.py:432
  14.0 4.7 %collective-permute-start.3 = (f32[136,128]{1,0:T(8,128)S(1)}, f32[136,128]{1,0:T(8,128)S(1)}, u32[]{:S(2)}, u32[]{:S(2)}) collective-permute-start(f32[136,128]{1,0:T(8,128)S(1)} %add.46), channel_id=1, source_target_pairs={{0,16},{1,17},{2,18},{3,19},{4,20},{5,21},{6,22},{7,23},{8,24},{9,... | collective-permute-start | bytes 208904 | tf_op jit(solution)/shard_map/ppermute | solution.py:432
  16.9 6.5 %collective-permute-start.4 = (f32[136,128]{1,0:T(8,128)S(1)}, f32[136,128]{1,0:T(8,128)S(1)}, u32[]{:S(2)}, u32[]{:S(2)}) collective-permute-start(f32[136,128]{1,0:T(8,128)S(1)} %add.46), channel_id=1, source_target_pairs={{0,20},{1,21},{2,22},{3,23},{4,16},{5,17},{6,18},{7,19},{8,28},{9,... | collective-permute-start | bytes 208904 | tf_op jit(solution)/shard_map/ppermute | solution.py:432
  23.4 6.4 %collective-permute-start.5 = (f32[136,128]{1,0:T(8,128)S(1)}, f32[136,128]{1,0:T(8,128)S(1)}, u32[]{:S(2)}, u32[]{:S(2)}) collective-permute-start(f32[136,128]{1,0:T(8,128)S(1)} %add_add_fusion.mine_ref), channel_id=1, source_target_pairs={{0,14},{1,15},{2,12},{3,13},{4,10},{5,11},{6,8},{7,9},{8,6},{9,7},... | collective-permute-start | bytes 208904 | tf_op jit(solution)/shard_map/ppermute | solution.py:432
  29.8 29.3 %copy-start.1 = (bf16[256,1024]{1,0:T(8,128)(2,1)S(1)}, bf16[256,1024]{1,0:T(8,128)(2,1)}, u32[]{:S(2)}) copy-start(bf16[256,1024]{1,0:T(8,128)(2,1)} %copy-done) | copy-start | bytes 1572868
  29.8 29.3 %copy-start.2 = (bf16[256,256]{1,0:T(8,128)(2,1)S(1)}, bf16[256,256]{1,0:T(8,128)(2,1)}, u32[]{:S(2)}) copy-start(bf16[256,256]{1,0:T(8,128)(2,1)} %wfx_ref.1) | copy-start | bytes 393220
  29.8 29.3 %copy-start.3 = (bf16[256,256]{1,0:T(8,128)(2,1)S(1)}, bf16[256,256]{1,0:T(8,128)(2,1)}, u32[]{:S(2)}) copy-start(bf16[256,256]{1,0:T(8,128)(2,1)} %wx_ref.1) | copy-start | bytes 393220
  35.7 4.4 %collective-permute-start.6 = (f32[32,512]{1,0:T(8,128)S(1)}, f32[32,512]{1,0:T(8,128)S(1)}, u32[]{:S(2)}, u32[]{:S(2)}) collective-permute-start(f32[32,512]{1,0:T(8,128)S(1)} %get-tuple-element.61), channel_id=1, source_target_pairs={{0,1},{1,0},{2,3},{3,2},{4,5},{5,4},{6,7},{7,6},{8,9},{9,8},{10,11... | collective-permute-start | bytes 196616 | tf_op jit(solution)/shard_map/ppermute | solution.py:432
  40.1 4.2 %collective-permute-start.7 = (f32[32,512]{1,0:T(8,128)S(1)}, f32[32,512]{1,0:T(8,128)S(1)}, u32[]{:S(2)}, u32[]{:S(2)}) collective-permute-start(f32[32,512]{1,0:T(8,128)S(1)} %add.50), channel_id=1, source_target_pairs={{0,2},{1,3},{2,0},{3,1},{4,6},{5,7},{6,4},{7,5},{8,10},{9,11},{10,... | collective-permute-start | bytes 196616 | tf_op jit(solution)/shard_map/ppermute | solution.py:432
  44.3 6.5 %collective-permute-start.10 = (f32[32,512]{1,0:T(8,128)S(1)}, f32[32,512]{1,0:T(8,128)S(1)}, u32[]{:S(2)}, u32[]{:S(2)}) collective-permute-start(f32[32,512]{1,0:T(8,128)S(1)} %add.51), channel_id=1, source_target_pairs={{0,20},{1,21},{2,22},{3,23},{4,16},{5,17},{6,18},{7,19},{8,28},{9,... | collective-permute-start | bytes 196616 | tf_op jit(solution)/shard_map/ppermute | solution.py:432
  44.7 7.6 %collective-permute-start.8 = (f32[32,512]{1,0:T(8,128)S(1)}, f32[32,512]{1,0:T(8,128)S(1)}, u32[]{:S(2)}, u32[]{:S(2)}) collective-permute-start(f32[32,512]{1,0:T(8,128)S(1)} %add.51), channel_id=1, source_target_pairs={{0,4},{1,5},{2,6},{3,7},{4,0},{5,1},{6,2},{7,3},{8,12},{9,13},{10,... | collective-permute-start | bytes 196616 | tf_op jit(solution)/shard_map/ppermute | solution.py:432
  46.5 5.8 %collective-permute-start.9 = (f32[32,512]{1,0:T(8,128)S(1)}, f32[32,512]{1,0:T(8,128)S(1)}, u32[]{:S(2)}, u32[]{:S(2)}) collective-permute-start(f32[32,512]{1,0:T(8,128)S(1)} %add.51), channel_id=1, source_target_pairs={{0,16},{1,17},{2,18},{3,19},{4,20},{5,21},{6,22},{7,23},{8,24},{9,... | collective-permute-start | bytes 196616 | tf_op jit(solution)/shard_map/ppermute | solution.py:432
  52.3 6.8 %collective-permute-start.11 = (f32[32,512]{1,0:T(8,128)S(1)}, f32[32,512]{1,0:T(8,128)S(1)}, u32[]{:S(2)}, u32[]{:S(2)}) collective-permute-start(f32[32,512]{1,0:T(8,128)S(1)} %add_add_fusion.1.mine_ref), channel_id=1, source_target_pairs={{0,14},{1,15},{2,12},{3,13},{4,10},{5,11},{6,8},{7,9},{8,6},{9,7},... | collective-permute-start | bytes 196616 | tf_op jit(solution)/shard_map/ppermute | solution.py:432
  55.8 12.2 %collective-permute-start.13 = (f32[768,128]{1,0:T(8,128)S(1)}, f32[768,128]{1,0:T(8,128)S(1)}, u32[]{:S(2)}, u32[]{:S(2)}) collective-permute-start(f32[768,128]{1,0:T(8,128)S(1)} %get-tuple-element.73), channel_id=1, source_target_pairs={{0,1},{1,0},{2,3},{3,2},{4,5},{5,4},{6,7},{7,6},{8,9},{9,8},{10,11... | collective-permute-start | bytes 1179656 | tf_op jit(solution)/shard_map/ppermute | solution.py:432
  63.3 4.6 %collective-permute-start.12 = (f32[640,128]{1,0:T(8,128)S(1)}, f32[640,128]{1,0:T(8,128)S(1)}, u32[]{:S(2)}, u32[]{:S(2)}) collective-permute-start(f32[640,128]{1,0:T(8,128)S(1)} %get-tuple-element.68), channel_id=1, source_target_pairs={{0,1},{1,0},{2,3},{3,2},{4,5},{5,4},{6,7},{7,6},{8,9},{9,8},{10,11... | collective-permute-start | bytes 983048 | tf_op jit(solution)/shard_map/ppermute | solution.py:432
  85.3 4.7 %collective-permute-start.14 = (f32[88,128]{1,0:T(8,128)S(1)}, f32[88,128]{1,0:T(8,128)S(1)}, u32[]{:S(2)}, u32[]{:S(2)}) collective-permute-start(f32[88,128]{1,0:T(8,128)S(1)} %reduce_sum.9), channel_id=1, source_target_pairs={{0,2},{1,3},{2,0},{3,1},{4,6},{5,7},{6,4},{7,5},{8,10},{9,11},{10,... | collective-permute-start | bytes 135176 | tf_op jit(solution)/shard_map/ppermute | solution.py:432
  90.0 3.9 %collective-permute-start.15 = (f32[88,128]{1,0:T(8,128)S(1)}, f32[88,128]{1,0:T(8,128)S(1)}, u32[]{:S(2)}, u32[]{:S(2)}) collective-permute-start(f32[88,128]{1,0:T(8,128)S(1)} %add.57), channel_id=1, source_target_pairs={{0,4},{1,5},{2,6},{3,7},{4,0},{5,1},{6,2},{7,3},{8,12},{9,13},{10,... | collective-permute-start | bytes 135176 | tf_op jit(solution)/shard_map/ppermute | solution.py:432
  93.9 4.5 %collective-permute-start.16 = (f32[88,128]{1,0:T(8,128)S(1)}, f32[88,128]{1,0:T(8,128)S(1)}, u32[]{:S(2)}, u32[]{:S(2)}) collective-permute-start(f32[88,128]{1,0:T(8,128)S(1)} %add.58), channel_id=1, source_target_pairs={{0,14},{1,15},{2,12},{3,13},{4,10},{5,11},{6,8},{7,9},{8,6},{9,7},... | collective-permute-start | bytes 135176 | tf_op jit(solution)/shard_map/ppermute | solution.py:432
  112.2 7.1 %collective-permute-start.17 = (f32[16,88,128]{2,1,0:T(8,128)S(1)}, f32[16,88,128]{2,1,0:T(8,128)S(1)}, u32[]{:S(2)}, u32[]{:S(2)}) collective-permute-start(f32[16,88,128]{2,1,0:T(8,128)S(1)} %all_to_all.11.mine_ref), channel_id=1, source_target_pairs={{0,1},{1,0},{2,3},{3,2},{4,5},{5,4},{6,7},{7,6},{8,9},{9,8},{10,11... | collective-permute-start | bytes 2162696 | tf_op jit(solution)/shard_map/ppermute | solution.py:432
